TPU v7x, 32 devices: a whole 2x2x4 slice. The times are simulated.
32 devices in a mesh: batch: 8 (over z, x), expert: 4 (over y, core).
Axes of the slice: x: 2, y: 2, z: 4, core: 2. Of those that a mesh axis runs over, the one named last changes fastest.
Arguments:
- emb_table: bfloat16 [524288, 16], P('batch'), may hold values from -6 to 6
- dense_feats: bfloat16 [13, 20480], P(None, ('batch', 'expert')), may hold values from -5 to 5
- dense_w: bfloat16 [13, 96], replicated, may hold values from -1.75 to 1.75
- gate_w: bfloat16 [512, 8], replicated, may hold values from -0.1796875 to 0.1796875
- hidden_w: bfloat16 [4, 512, 256], P('expert'), may hold values from -0.25 to 0.25
- hidden_b: float32 [4, 256], P('expert'), may hold values from -0.6 to 0.6
- output_w: bfloat16 [4, 256, 128], P('expert'), may hold values from -0.375 to 0.375
- output_b: float32 [4, 128], P('expert'), may hold values from -0.6 to 0.6
- tower_w: bfloat16 [128, 128], replicated, may hold values from -0.5 to 0.5
- tower_b: float32 [128], replicated, may hold values from -0.6 to 0.6
- head_w: float32 [128], replicated, may hold values from -0.75 to 0.75
- head_b: float32 [2], replicated, may hold values from -1 to 1
- row_owner: int32 [532480, 1], P(('batch', 'expert')), may hold values from 0 to 7; in each aligned block of 4160 rows (0 to 4159, 4160 to 8319, ...) at most 1040 rows name the same one
- local_row: int32 [532480], P(('batch', 'expert')), may hold values from 0 to 65535
- labels: int32 [2, 20480], P(None, ('batch', 'expert')), may hold values 0 or 1
Outputs:
- grad_table: float32 [524288, 16], P('batch')
- grad_dense: float32 [13, 20480], P(None, ('batch', 'expert'))
- grad_dense_w: float32 [13, 96], replicated
- grad_gate: float32 [512, 8], replicated
- grad_hidden_w: float32 [4, 512, 256], P('expert')
- grad_hidden_b: float32 [4, 256], P('expert')
- grad_output_w: float32 [4, 256, 128], P('expert')
- grad_output_b: float32 [4, 128], P('expert')
- grad_tower_w: float32 [128, 128], replicated
- grad_tower_b: float32 [128], replicated
- grad_head_w: float32 [128], replicated
- grad_head_b: float32 [2], replicated
Inputs may be any that keep to these rules, and one draw needn't show every extreme that they name: `row_owner`: within each device's lookups of one micro-batch (aligned blocks of 4160 entries) no owner is named more than 1040 times, a bound that some block reaches.
All inputs are finite; a program needn't handle non-finite values. No bound on the sum of `labels` on one device may be relied on, other than what follows from the above.
Results may differ from a plain program's by a relative error of at most 0.017.
Values may be sent and summed in bfloat16 or wider, within the bound.
No kernel may reach another device: no remote copies, remote signals or barrier semaphores. Data moves between devices by JAX's collectives and lax.ppermute only.
A program may use at most 384 MiB of HBM per device.

v0:
```python
import math

import jax
import jax.numpy as jnp
from jax import lax
from jax.sharding import PartitionSpec as P

FIELDS = 26
EMB = 16
DENSE = 13
BOTTOM = 96
D_IN = 512
H1 = 256
H2 = 128
TOWER = 64
TASKS = 2
MICRO = 4


def silu_slope(values):
    sig = jax.nn.sigmoid(values)
    return sig * (1.0 + values * (1.0 - sig))


def shards(
    emb_table,
    dense_feats,
    dense_w,
    gate_w,
    hidden_w,
    hidden_b,
    output_w,
    output_b,
    tower_w,
    tower_b,
    head_w,
    head_b,
    row_owner,
    local_row,
    labels,
):
    fp32 = jnp.float32
    owners = lax.axis_size("batch")
    experts = lax.axis_size("expert")
    expert_index = lax.axis_index("expert")
    row_total = dense_feats.shape[1]
    row_count = row_total // MICRO
    lookups = row_count * FIELDS
    capacity = 2 * lookups // owners
    table_rows = emb_table.shape[0]
    scale = 1.0 / math.sqrt(row_total * owners * experts)
    emb_width = FIELDS * EMB
    owner_ids = jnp.arange(owners, dtype=jnp.int32)
    gate_cube = gate_w.reshape(D_IN, TASKS, experts)
    held_experts = 1
    acc_hidden_w = jnp.zeros((held_experts, D_IN, H1), fp32)
    acc_hidden_b = jnp.zeros((held_experts, H1), fp32)
    acc_output_w = jnp.zeros((held_experts, H1, H2), fp32)
    acc_output_b = jnp.zeros((held_experts, H2), fp32)
    acc_gate = jnp.zeros((D_IN, TASKS, experts), fp32)
    acc_tower_w = jnp.zeros((H2, TASKS * TOWER), fp32)
    acc_tower_b = jnp.zeros((TASKS * TOWER,), fp32)
    acc_head_w = jnp.zeros((TASKS * TOWER,), fp32)
    acc_head_b = jnp.zeros((TASKS,), fp32)
    acc_dense_w = jnp.zeros((DENSE, BOTTOM), fp32)
    acc_table = jnp.zeros((table_rows, EMB), fp32)
    dense_parts = []
    for micro in range(MICRO):
        owner_part = row_owner[micro * lookups : (micro + 1) * lookups, 0]
        local_part = local_row[micro * lookups : (micro + 1) * lookups]
        onehot = (owner_part[:, None] == owner_ids[None, :]).astype(jnp.int32)
        rank = jnp.sum(jnp.cumsum(onehot, axis=0) * onehot, axis=1) - 1
        slot_index = owner_part * capacity + rank
        requests = jnp.full((owners * capacity,), -1, jnp.int32).at[slot_index].set(local_part)
        requests = requests.reshape(owners, capacity)
        asked = lax.all_to_all(requests, "batch", split_axis=0, concat_axis=0, tiled=True)
        valid = asked >= 0
        found = jnp.take(emb_table, jnp.clip(asked, 0, table_rows - 1).reshape(-1), axis=0)
        found = found.reshape(asked.shape + (EMB,))
        found = jnp.where(valid[..., None], found, jnp.zeros_like(found))
        returned = lax.all_to_all(found, "batch", split_axis=0, concat_axis=0, tiled=True)
        embedded = returned.reshape(owners * capacity, EMB)[slot_index].reshape(
            row_count, emb_width
        )
        dense_part = dense_feats[:, micro * row_count : (micro + 1) * row_count]
        bottom = jnp.dot(dense_part.T, dense_w, preferred_element_type=fp32)
        features = jnp.concatenate([embedded.astype(fp32), bottom], axis=1).astype(jnp.bfloat16)
        gathered = lax.all_gather(features, "expert", axis=0, tiled=True)
        logits = jnp.dot(gathered, gate_w, preferred_element_type=fp32).reshape(-1, TASKS, experts)
        gates = jax.nn.softmax(logits, axis=-1)
        own_gate = lax.dynamic_index_in_dim(gates, expert_index, 2, keepdims=False)
        pre_hidden = jnp.dot(gathered, hidden_w[0], preferred_element_type=fp32) + hidden_b[0][None]
        hidden = jax.nn.silu(pre_hidden).astype(jnp.bfloat16)
        pre_output = jnp.dot(hidden, output_w[0], preferred_element_type=fp32) + output_b[0][None]
        outputs = jax.nn.silu(pre_output)
        weighted = (own_gate[:, :, None] * outputs[:, None, :]).reshape(-1, TASKS * H2)
        mixed = lax.psum_scatter(
            weighted.astype(jnp.bfloat16), "expert", scatter_dimension=0, tiled=True
        ).astype(jnp.float32)
        mixed_low = mixed.astype(jnp.bfloat16)
        tower_pieces = []
        for task in range(TASKS):
            tower_pieces.append(
                jnp.dot(
                    mixed_low[:, task * H2 : (task + 1) * H2],
                    tower_w[:, task * TOWER : (task + 1) * TOWER],
                    preferred_element_type=fp32,
                )
            )
        pre_tower = jnp.concatenate(tower_pieces, axis=1) + tower_b[None]
        tower_act = jax.nn.silu(pre_tower)
        scores = (
            jnp.sum((tower_act * head_w[None]).reshape(row_count, TASKS, TOWER), axis=-1)
            + head_b[None]
        )
        targets = labels[:, micro * row_count : (micro + 1) * row_count].T.astype(fp32)
        score_grad = (jax.nn.sigmoid(scores) - targets) * scale
        acc_head_b = acc_head_b + jnp.sum(score_grad, axis=0)
        wide_grad = jnp.repeat(score_grad, TOWER, axis=1)
        acc_head_w = acc_head_w + jnp.sum(wide_grad * tower_act, axis=0)
        tower_grad = (wide_grad * head_w[None] * silu_slope(pre_tower)).astype(jnp.bfloat16)
        acc_tower_b = acc_tower_b + jnp.sum(tower_grad.astype(fp32), axis=0)
        weight_pieces = []
        mixed_pieces = []
        for task in range(TASKS):
            mixed_slice = mixed_low[:, task * H2 : (task + 1) * H2]
            grad_slice = tower_grad[:, task * TOWER : (task + 1) * TOWER]
            weight_pieces.append(jnp.dot(mixed_slice.T, grad_slice, preferred_element_type=fp32))
            mixed_pieces.append(
                jnp.dot(
                    grad_slice,
                    tower_w[:, task * TOWER : (task + 1) * TOWER].T,
                    preferred_element_type=fp32,
                )
            )
        acc_tower_w = acc_tower_w + jnp.concatenate(weight_pieces, axis=1)
        mixed_grad = lax.optimization_barrier(
            jnp.concatenate(mixed_pieces, axis=1).astype(jnp.bfloat16)
        ).astype(fp32)
        mixed_dot = jnp.sum((mixed_grad * mixed).reshape(row_count, TASKS, H2), axis=-1)
        sent_grad, sent_dot = (
            lax.all_gather(mixed_grad.astype(jnp.bfloat16), "expert", axis=0, tiled=True).astype(
                mixed_grad.dtype
            ),
            lax.all_gather(mixed_dot.astype(jnp.bfloat16), "expert", axis=0, tiled=True).astype(
                mixed_dot.dtype
            ),
        )
        grad_cube = sent_grad.reshape(-1, TASKS, H2)
        out_grad = jnp.sum(own_gate[:, :, None] * grad_cube, axis=1)
        pre_output_grad = (out_grad * silu_slope(pre_output)).astype(jnp.bfloat16)
        acc_output_b = acc_output_b + jnp.sum(pre_output_grad.astype(fp32), axis=0)[None]
        acc_output_w = (
            acc_output_w + jnp.dot(hidden.T, pre_output_grad, preferred_element_type=fp32)[None]
        )
        hidden_grad = jnp.dot(pre_output_grad, output_w[0].T, preferred_element_type=fp32)
        pre_hidden_grad = (hidden_grad * silu_slope(pre_hidden)).astype(jnp.bfloat16)
        acc_hidden_b = acc_hidden_b + jnp.sum(pre_hidden_grad.astype(fp32), axis=0)[None]
        acc_hidden_w = (
            acc_hidden_w + jnp.dot(gathered.T, pre_hidden_grad, preferred_element_type=fp32)[None]
        )
        along = jnp.sum(grad_cube * outputs[:, None, :], axis=-1)
        logit_grad = (own_gate * (along - sent_dot)).astype(jnp.bfloat16)
        column_mask = (jnp.arange(experts) == expert_index).astype(fp32)
        acc_gate = (
            acc_gate
            + jnp.dot(gathered.T, logit_grad, preferred_element_type=fp32)[:, :, None]
            * column_mask[None, None, :]
        )
        own_gate_w = lax.dynamic_index_in_dim(gate_cube, expert_index, 2, keepdims=False)
        input_grad = lax.psum_scatter(
            (
                jnp.dot(pre_hidden_grad, hidden_w[0].T, preferred_element_type=fp32)
                + jnp.dot(logit_grad, own_gate_w.T, preferred_element_type=fp32)
            ).astype(jnp.bfloat16),
            "expert",
            scatter_dimension=0,
            tiled=True,
        )
        emb_grad = input_grad[:, :emb_width].reshape(lookups, EMB)
        bottom_grad = input_grad[:, emb_width:]
        acc_dense_w = acc_dense_w + jnp.dot(dense_part, bottom_grad, preferred_element_type=fp32)
        dense_parts.append(jnp.dot(dense_w, bottom_grad.T, preferred_element_type=fp32))
        outgoing = jnp.zeros((owners * capacity, EMB), jnp.bfloat16).at[slot_index].set(emb_grad)
        incoming = lax.all_to_all(
            outgoing.reshape(owners, capacity, EMB),
            "batch",
            split_axis=0,
            concat_axis=0,
            tiled=True,
        )
        target_rows = jnp.where(asked >= 0, asked, table_rows).reshape(-1)
        table_terms = jax.ops.segment_sum(
            incoming.reshape(-1, EMB).astype(fp32), target_rows, num_segments=table_rows + 1
        )
        acc_table = acc_table + table_terms[:table_rows]
    expert_totals = (
        lax.psum(acc_hidden_w.astype(jnp.bfloat16), "batch").astype(jnp.float32),
        lax.psum(acc_hidden_b.astype(jnp.bfloat16), "batch").astype(jnp.float32),
        lax.psum(acc_output_w.astype(jnp.bfloat16), "batch").astype(jnp.float32),
        lax.psum(acc_output_b.astype(jnp.bfloat16), "batch").astype(jnp.float32),
    )
    shared = lax.psum(
        (
            acc_gate.reshape(D_IN, TASKS * experts),
            acc_dense_w,
            acc_tower_w,
            acc_tower_b,
            acc_head_w,
            acc_head_b,
        ),
        ("batch", "expert"),
    )
    table_total = lax.psum(acc_table.astype(jnp.bfloat16), "expert").astype(jnp.float32)
    return (
        table_total,
        jnp.concatenate(dense_parts, axis=1),
        shared[1],
        shared[0],
        expert_totals[0],
        expert_totals[1],
        expert_totals[2],
        expert_totals[3],
        shared[2],
        shared[3],
        shared[4],
        shared[5],
    )


def solution(mesh):
    in_specs = (
        P("batch", None),
        P(None, ("batch", "expert")),
        P(),
        P(),
        P("expert", None, None),
        P("expert", None),
        P("expert", None, None),
        P("expert", None),
        P(),
        P(),
        P(),
        P(),
        P(("batch", "expert"), None),
        P(("batch", "expert")),
        P(None, ("batch", "expert")),
    )
    out_specs = (
        P("batch", None),
        P(None, ("batch", "expert")),
        P(),
        P(),
        P("expert", None, None),
        P("expert", None),
        P("expert", None, None),
        P("expert", None),
        P(),
        P(),
        P(),
        P(),
    )
    return jax.shard_map(shards, mesh=mesh, in_specs=in_specs, out_specs=out_specs, check_vma=False)
```

profile of v0, /device:TPU:0, one launch (start us, length us, event | category | flops | bytes accessed | tf_op | source)
XLA Modules:
  0.0 1563.5 jit_solution(5726086611410635334)
XLA Ops:
  13.2 20.6 %scatter_custom_fusion = s32[8320]{0:T(1024)S(1)} fusion(s32[4160]{0:T(1024)S(1)} %get-tuple-element.81, s32[4160]{0:T(1024)S(1)} %get-tuple-element.137, s32[]{:T(128)} %constant.84.clone.1), kind=kCustom, calls=%fused_computation.376 | custom fusion | bytes 33284 | tf_op jit(solution)/shard_map/scatter | solution.py:74
  56.4 20.6 %scatter_custom_fusion.3 = s32[8320]{0:T(1024)S(1)} fusion(s32[4160]{0:T(1024)S(1)} %get-tuple-element.85, s32[4160]{0:T(1024)S(1)} %get-tuple-element.138, s32[]{:T(128)} %constant.84.clone.1), kind=kCustom, calls=%fused_computation.374 | custom fusion | bytes 33284 | tf_op jit(solution)/shard_map/scatter | solution.py:74
  78.2 20.6 %scatter_custom_fusion.9 = s32[8320]{0:T(1024)S(1)} fusion(s32[4160]{0:T(1024)S(1)} %get-tuple-element.86, s32[4160]{0:T(1024)S(1)} %get-tuple-element.139, s32[]{:T(128)} %constant.84.clone.1), kind=kCustom, calls=%fused_computation.370 | custom fusion | bytes 33284 | tf_op jit(solution)/shard_map/scatter | solution.py:74
  100.1 20.6 %scatter_custom_fusion.6 = s32[8320]{0:T(1024)S(1)} fusion(s32[4160]{0:T(1024)S(1)} %get-tuple-element.87, s32[4160]{0:T(1024)S(1)} %get-tuple-element.140, s32[]{:T(128)} %constant.84.clone.1), kind=kCustom, calls=%fused_computation.372 | custom fusion | bytes 33284 | tf_op jit(solution)/shard_map/scatter | solution.py:74
  169.5 24.3 %gather_fusion.7 = bf16[8320,16]{1,0:T(8,128)(2,1)} fusion(bf16[65536,16]{1,0:T(8,128)(2,1)} %copy.164, s32[9216]{0:T(1024)S(1)} %pad_clamp_fusion), kind=kCustom, calls=%fused_computation.3.clone | custom fusion | bytes 565760 | tf_op jit(solution)/shard_map/jit(_take)/gather | solution.py:78
  204.8 24.3 %gather_fusion.6 = bf16[8320,16]{1,0:T(8,128)(2,1)} fusion(bf16[65536,16]{1,0:T(8,128)(2,1)} %copy.164, s32[9216]{0:T(1024)S(1)} %pad_clamp_fusion.1), kind=kCustom, calls=%fused_computation.2.clone | custom fusion | bytes 565760 | tf_op jit(solution)/shard_map/jit(_take)/gather | solution.py:78
  235.8 24.2 %gather_fusion.5 = bf16[8320,16]{1,0:T(8,128)(2,1)} fusion(bf16[65536,16]{1,0:T(8,128)(2,1)} %copy.164, s32[9216]{0:T(1024)S(1)} %pad_clamp_fusion.2), kind=kCustom, calls=%fused_computation.1.clone | custom fusion | bytes 565760 | tf_op jit(solution)/shard_map/jit(_take)/gather | solution.py:78
  260.0 24.3 %gather_fusion.4 = bf16[8320,16]{1,0:T(8,128)(2,1)} fusion(bf16[65536,16]{1,0:T(8,128)(2,1)} %copy.164, s32[9216]{0:T(1024)S(1)} %pad_clamp_fusion.3), kind=kCustom, calls=%fused_computation.clone | custom fusion | bytes 565760 | tf_op jit(solution)/shard_map/jit(_take)/gather | solution.py:78
  452.9 20.9 %reduce-scatter.13.cloned.1.call-done = bf16[160,256]{1,0:T(8,128)(2,1)} async-done(((bf16[640,256]{1,0:T(8,128)(2,1)}), bf16[160,256]{1,0:T(8,128)(2,1)}) %reduce-scatter.13.cloned.1.call-update) | async-done | bytes 81936 | tf_op jit(solution)/shard_map/reduce_scatter | solution.py:97
  475.9 20.9 %reduce-scatter.9.cloned.1.call-done = bf16[160,256]{1,0:T(8,128)(2,1)} async-done(((bf16[640,256]{1,0:T(8,128)(2,1)}), bf16[160,256]{1,0:T(8,128)(2,1)}) %reduce-scatter.9.cloned.1.call-update) | async-done | bytes 81936 | tf_op jit(solution)/shard_map/reduce_scatter | solution.py:97
  635.4 18.9 %scatter_custom_fusion.10 = bf16[8320,16]{1,0:T(8,128)(2,1)} fusion(s32[4160]{0:T(1024)} %copy-done.91, bf16[4160,16]{1,0:T(8,128)(2,1)S(1)} %reshape.853, bf16[]{:T(256)} %constant.90.clone.1), kind=kCustom, calls=%fused_computation.93 | custom fusion | bytes 266752 | tf_op jit(solution)/shard_map/scatter | solution.py:184
  665.8 18.0 %scatter_custom_fusion.7 = bf16[8320,16]{1,0:T(8,128)(2,1)S(1)} fusion(s32[4160]{0:T(1024)} %copy-done.90, bf16[4160,16]{1,0:T(8,128)(2,1)} %reshape.829, bf16[]{:T(256)} %constant.90.clone.1), kind=kCustom, calls=%fused_computation.95 | custom fusion | bytes 266752 | tf_op jit(solution)/shard_map/scatter | solution.py:184
  694.5 18.0 %scatter_custom_fusion.4 = bf16[8320,16]{1,0:T(8,128)(2,1)S(1)} fusion(s32[4160]{0:T(1024)} %copy-done.89, bf16[4160,16]{1,0:T(8,128)(2,1)} %reshape.805, bf16[]{:T(256)} %constant.90.clone.1), kind=kCustom, calls=%fused_computation.97 | custom fusion | bytes 266752 | tf_op jit(solution)/shard_map/scatter | solution.py:184
  720.3 22.2 %all-reduce.5 = (bf16[1,256]{1,0:T(2,128)(2,1)S(1)}, bf16[1,128]{1,0:T(2,128)(2,1)S(1)}) all-reduce(bf16[1,256]{1,0:T(2,128)(2,1)S(1)} %convert_element_type.435, bf16[1,128]{1,0:T(2,128)(2,1)S(1)} %convert_bitcast_fusion.4), channel_id=1, replica_groups=mesh['batch'=8,'expert'=4] {'batch'}, use_global_device_ids=true, to_apply=%region_64.66 | all-reduce | flops 384 | bytes 1536 | tf_op jit(solution)/shard_map/psum | solution.py:199
  743.7 43.1 %all-reduce.13.cloned.1.call-done = f32[128,128]{0,1:T(8,128)} async-done(((f32[128,128]{0,1:T(8,128)}), f32[128,128]{0,1:T(8,128)}) %all-reduce.13.cloned.1.call-update) | async-done | bytes 65552 | tf_op jit(solution)/shard_map/psum | solution.py:203
  788.4 73.8 %all-reduce.15.cloned.1.call-done = (bf16[1,512,256]{2,1,0:T(8,128)(2,1)}, bf16[1,256,128]{2,1,0:T(8,128)(2,1)}) async-done(((bf16[1,512,256]{2,1,0:T(8,128)(2,1)}, bf16[1,256,128]{2,1,0:T(8,128)(2,1)}), (bf16[1,512,256]{2,1,0:T(8,128)(2,1)}, bf16[1,256,128]{2,1,0:T(8,128)(2,1)})) %all-reduce.15.cloned.1.call-update) | async-done | bytes 327696 | tf_op jit(solution)/shard_map/psum | solution.py:198
  865.5 20.9 %reduce-scatter.11.cloned.1.call-done = bf16[160,512]{1,0:T(8,128)(2,1)} async-done(((bf16[640,512]{1,0:T(8,128)(2,1)}), bf16[160,512]{1,0:T(8,128)(2,1)}) %reduce-scatter.11.cloned.1.call-update) | async-done | bytes 163856 | tf_op jit(solution)/shard_map/reduce_scatter | solution.py:171
  919.0 60.5 %scatter_custom_fusion.11 = f32[65537,16]{1,0:T(8,128)} fusion(s32[8320]{0:T(1024)} %fusion.120, f32[8320,16]{1,0:T(8,128)} %bitcast.359, f32[]{:T(128)} %constant.83.clone.1), kind=kCustom, calls=%fused_computation.24 | custom fusion | flops 133120 | bytes 4194880 | tf_op jit(solution)/shard_map/scatter-add | solution.py:193
  982.8 60.5 %scatter_custom_fusion.8 = f32[65537,16]{1,0:T(8,128)} fusion(s32[8320]{0:T(1024)} %fusion.119, f32[8320,16]{1,0:T(8,128)} %bitcast.360, f32[]{:T(128)} %constant.83.clone.1), kind=kCustom, calls=%fused_computation.26 | custom fusion | flops 133120 | bytes 4194880 | tf_op jit(solution)/shard_map/scatter-add | solution.py:193
  1045.7 60.4 %scatter_custom_fusion.5 = f32[65537,16]{1,0:T(8,128)} fusion(s32[8320]{0:T(1024)} %fusion.118, f32[8320,16]{1,0:T(8,128)} %bitcast.361, f32[]{:T(128)} %constant.83.clone.1), kind=kCustom, calls=%fused_computation.28 | custom fusion | flops 133120 | bytes 4194880 | tf_op jit(solution)/shard_map/scatter-add | solution.py:193
  1108.4 60.6 %scatter_custom_fusion.2 = f32[65537,16]{1,0:T(8,128)} fusion(s32[8320]{0:T(1024)} %fusion.117, f32[8320,16]{1,0:T(8,128)} %bitcast.358, f32[]{:T(128)} %constant.83.clone.1), kind=kCustom, calls=%fused_computation.30 | custom fusion | flops 133120 | bytes 4194880 | tf_op jit(solution)/shard_map/scatter-add | solution.py:193
  1169.0 46.7 %fusion = bf16[65536,16]{1,0:T(8,128)(2,1)} fusion(f32[65537,16]{1,0:T(8,128)} %scatter_custom_fusion.11, f32[65537,16]{1,0:T(8,128)} %scatter_custom_fusion.8, f32[65537,16]{1,0:T(8,128)} %scatter_custom_fusion.5, f32[65537,16]{1,0:T(8,128)} %scatter_custom_fusion.2), kind=kLoop, calls=%fused_computation.21 | loop fusion | flops 4194304 | bytes 18874368 | tf_op jit(solution)/shard_map/convert_element_type | solution.py:214
  1216.8 79.5 %all-reduce.4 = (f32[13,96]{1,0:T(8,128)}, f32[512,8]{0,1:T(8,128)}, f32[128]{0:T(128)}, f32[128]{0:T(128)}, f32[2]{0:T(128)}) all-reduce(f32[13,96]{1,0:T(8,128)S(1)} %fusion.21, f32[512,8]{0,1:T(8,128)S(1)} %broadcast_multiply_fusion, f32[128]{0:T(128)S(1)} %add.697, ...), channel_id=1, replica_groups=mesh['batch'=8,'expert'=4] {'batch','expert'}, use_global_device_ids=true, to_apply=%region_57.59 | all-reduce | flops 5602 | bytes 44816 | tf_op jit(solution)/shard_map/psum | solution.py:203
  1299.5 243.5 %all-reduce.11.cloned.1.call-done = bf16[65536,16]{1,0:T(8,128)(2,1)} async-done(((bf16[65536,16]{1,0:T(8,128)(2,1)}), bf16[65536,16]{1,0:T(8,128)(2,1)}) %all-reduce.11.cloned.1.call-update) | async-done | bytes 2097168 | tf_op jit(solution)/shard_map/psum | solution.py:214
  (626 shorter events, 499.1 us)
Async XLA Ops:
  34.5 98.1 %all-to-all-start = ((s32[8,1,1040]{2,1,0:T(1,128)}), s32[8,1,1040]{2,1,0:T(1,128)S(1)}, u32[]{:S(2)}, u32[]{:S(2)}) async-start(s32[8,1,1040]{2,1,0:T(1,128)} %all_to_all.56), calls=%async_computation | async-start | bytes 73728 | tf_op jit(solution)/shard_map/all_to_all | solution.py:76
  45.3 453.6 %copy-start.100 = (f32[2,64]{1,0:T(2,128)}, f32[2,64]{1,0:T(2,128)S(1)}, u32[]{:S(2)}) copy-start(f32[2,64]{1,0:T(2,128)S(1)} %add.603) | copy-start | bytes 1540
  132.6 12.7 all-to-all-start.6
  145.3 10.0 all-to-all-start.9
  155.3 10.3 all-to-all-start.3
  201.3 100.5 %all-to-all-start.10 = ((bf16[8,1040,16]{1,2,0:T(8,128)(2,1)}), bf16[8,1040,16]{1,2,0:T(8,128)(2,1)S(1)}, u32[]{:S(2)}, u32[]{:S(2)}) async-start(bf16[8,1040,16]{1,2,0:T(8,128)(2,1)} %broadcast_select_fusion.4), calls=%async_computation.16 | async-start | bytes 589824 | tf_op jit(solution)/shard_map/all_to_all | solution.py:81
  301.8 37.9 %all-to-all-start.7 = ((bf16[8,1040,16]{1,2,0:T(8,128)(2,1)}), bf16[8,1040,16]{1,2,0:T(8,128)(2,1)}, u32[]{:S(2)}, u32[]{:S(2)}) async-start(bf16[8,1040,16]{1,2,0:T(8,128)(2,1)} %broadcast_select_fusion.5), calls=%async_computation.11 | async-start | bytes 589824 | tf_op jit(solution)/shard_map/all_to_all | solution.py:81
  339.7 30.3 %all-to-all-start.4 = ((bf16[8,1040,16]{1,2,0:T(8,128)(2,1)}), bf16[8,1040,16]{1,2,0:T(8,128)(2,1)S(1)}, u32[]{:S(2)}, u32[]{:S(2)}) async-start(bf16[8,1040,16]{1,2,0:T(8,128)(2,1)} %broadcast_select_fusion.6), calls=%async_computation.6 | async-start | bytes 589824 | tf_op jit(solution)/shard_map/all_to_all | solution.py:81
  370.7 38.1 %all-to-all-start.1 = ((bf16[8,1040,16]{1,2,0:T(8,128)(2,1)}), bf16[8,1040,16]{1,2,0:T(8,128)(2,1)S(1)}, u32[]{:S(2)}, u32[]{:S(2)}) async-start(bf16[8,1040,16]{1,2,0:T(8,128)(2,1)} %broadcast_select_fusion.7), calls=%async_computation.1 | async-start | bytes 589824 | tf_op jit(solution)/shard_map/all_to_all | solution.py:81
  376.4 57.9 %reduce-scatter.21.cloned.1.call-start = ((), (), s32[]{:S(2)}) async-start(), calls=%async_computation.26 | async-start | bytes 409600 | tf_op jit(solution)/shard_map/reduce_scatter | solution.py:97
  402.9 47.9 %reduce-scatter.17.cloned.1.call-start = ((), (), s32[]{:S(2)}) async-start(), calls=%async_computation.24 | async-start | bytes 409600 | tf_op jit(solution)/shard_map/reduce_scatter | solution.py:97
  429.6 44.2 %reduce-scatter.13.cloned.1.call-start = ((), (), s32[]{:S(2)}) async-start(), calls=%async_computation.22 | async-start | bytes 409600 | tf_op jit(solution)/shard_map/reduce_scatter | solution.py:97
  430.4 66.4 %reduce-scatter.9.cloned.1.call-start = ((), (), s32[]{:S(2)}) async-start(), calls=%async_computation.20 | async-start | bytes 409600 | tf_op jit(solution)/shard_map/reduce_scatter | solution.py:97
  434.3 199.1 %reduce-scatter.23.cloned.1.call-start = ((), (), s32[]{:S(2)}) async-start(), calls=%async_computation.27 | async-start | bytes 819200 | tf_op jit(solution)/shard_map/reduce_scatter | solution.py:171
  589.9 73.0 %reduce-scatter.19.cloned.1.call-start = ((), (), s32[]{:S(2)}) async-start(), calls=%async_computation.25 | async-start | bytes 819200 | tf_op jit(solution)/shard_map/reduce_scatter | solution.py:171
  601.2 90.4 %reduce-scatter.15.cloned.1.call-start = ((), (), s32[]{:S(2)}) async-start(), calls=%async_computation.23 | async-start | bytes 819200 | tf_op jit(solution)/shard_map/reduce_scatter | solution.py:171
  612.7 174.1 %all-reduce.13.cloned.1.call-start = ((), (), s32[]{:S(2)}) async-start(), calls=%async_computation.29 | async-start | bytes 131072 | tf_op jit(solution)/shard_map/psum | solution.py:203
  627.0 235.2 %all-reduce.15.cloned.1.call-start = ((), (), s32[]{:S(2)}) async-start(), calls=%async_computation.30 | async-start | bytes 655360 | tf_op jit(solution)/shard_map/psum | solution.py:198
  629.1 257.3 %reduce-scatter.11.cloned.1.call-start = ((), (), s32[]{:S(2)}) async-start(), calls=%async_computation.21 | async-start | bytes 819200 | tf_op jit(solution)/shard_map/reduce_scatter | solution.py:171
  656.9 28.4 %all-to-all-start.11 = ((bf16[8,1040,16]{1,2,0:T(8,128)(2,1)}), bf16[8,1040,16]{1,2,0:T(8,128)(2,1)S(1)}, u32[]{:S(2)}, u32[]{:S(2)}) async-start(bf16[8,1040,16]{1,2,0:T(8,128)(2,1)} %copy.219), calls=%async_computation.19 | async-start | bytes 589824 | tf_op jit(solution)/shard_map/all_to_all | solution.py:185
  685.3 28.7 %all-to-all-start.8 = ((bf16[8,1040,16]{1,2,0:T(8,128)(2,1)}), bf16[8,1040,16]{1,2,0:T(8,128)(2,1)}, u32[]{:S(2)}, u32[]{:S(2)}) async-start(bf16[8,1040,16]{1,2,0:T(8,128)(2,1)} %copy.204), calls=%async_computation.14 | async-start | bytes 589824 | tf_op jit(solution)/shard_map/all_to_all | solution.py:185
  714.1 194.7 %all-to-all-start.5 = ((bf16[8,1040,16]{1,2,0:T(8,128)(2,1)}), bf16[8,1040,16]{1,2,0:T(8,128)(2,1)S(1)}, u32[]{:S(2)}, u32[]{:S(2)}) async-start(bf16[8,1040,16]{1,2,0:T(8,128)(2,1)} %copy.189), calls=%async_computation.9 | async-start | bytes 589824 | tf_op jit(solution)/shard_map/all_to_all | solution.py:185
  908.8 197.3 %all-to-all-start.2 = ((bf16[8,1040,16]{1,2,0:T(8,128)(2,1)}), bf16[8,1040,16]{1,2,0:T(8,128)(2,1)S(1)}, u32[]{:S(2)}, u32[]{:S(2)}) async-start(bf16[8,1040,16]{1,2,0:T(8,128)(2,1)} %copy.174), calls=%async_computation.4 | async-start | bytes 589824 | tf_op jit(solution)/shard_map/all_to_all | solution.py:185
  914.3 628.7 %all-reduce.11.cloned.1.call-start = ((), (), s32[]{:S(2)}) async-start(), calls=%async_computation.28 | async-start | bytes 33554432 | tf_op jit(solution)/shard_map/psum | solution.py:214
  (129 other events, 2564.0 us)
Sparse Core Ops, SparseCore 0:
  403.0 21.0 reduce-scatter.20
  429.7 21.0 reduce-scatter.16
  453.3 20.4 reduce-scatter.12
  476.3 20.4 reduce-scatter.8
  590.0 22.9 reduce-scatter.22
  615.4 22.4 reduce-scatter.18
  640.4 22.4 reduce-scatter.14
  668.5 118.2 all-reduce.12
  790.2 71.9 all-reduce.14
  864.8 21.6 reduce-scatter.10
  1215.9 327.0 all-reduce.10
where the time goes:
time: 1570 us; the launch traced here: 1560 us
  waiting for transfers between devices  457 us (29%)
  local copies, waits for them, and re-layouts  390 us (25%)
  other arithmetic  383 us (24%)
  blocking collectives  180 us (11%)
  starting transfers between devices  76.7 us (5%)
  matrix products  60 us (4%)
  between operations  16.6 us (1%)
    psum x1, waiting for transfers between devices, shards(): lax.psum(acc_table.astype(jnp.bfloat16), 'expert').astype(jnp.float32)  243 us
    scatter-add x4, other arithmetic, shards(): jax.ops.segment_sum(incoming.reshape(-1, EMB).astype(fp32), target_rows,...  242 us
    gather x4, local copies, waits for them, and re-layouts, shards(): jnp.take(emb_table, jnp.clip(asked, 0, table_rows - 1).reshape(-1), axis=0)  97.1 us
    scatter x4, local copies, waits for them, and re-layouts, shards(): jnp.full((owners * capacity,), -1, jnp.int32).at[slot_index].set(local_part)  82.2 us
    psum x1, blocking collectives, shards(): lax.psum((acc_gate.reshape(D_IN, TASKS * experts), acc_dense_w, acc_tower...  79.5 us
    psum x1, waiting for transfers between devices, shards(): lax.psum(acc_hidden_w.astype(jnp.bfloat16), 'batch').astype(jnp.float32)  73.8 us
    scatter x4, local copies, waits for them, and re-layouts, shards(): jnp.zeros((owners * capacity, EMB), jnp.bfloat16).at[slot_index]  73.1 us
    reduce_scatter x4, waiting for transfers between devices, shards(): lax.psum_scatter(weighted.astype(jnp.bfloat16), 'expert', scatter_dimensi...  56.2 us
  transfers between devices with their start and end apart: 23, of which 10 were waited for; matrix products, arithmetic and copies ran while one was open for 38% of the time, Pallas kernels for 0%

commit v1 on v0

v1 whole, which is shorter than its diff:
```python
import functools
import math

import jax
import jax.numpy as jnp
from jax import lax
from jax.experimental import pallas as pl
from jax.experimental.pallas import tpu as pltpu
from jax.sharding import PartitionSpec as P

FIELDS = 26
EMB = 16
DENSE = 13
BOTTOM = 96
D_IN = 512
H1 = 256
H2 = 128
TOWER = 64
TASKS = 2
LANES = 128
GROUPS = LANES // EMB
EMB_WIDTH = FIELDS * EMB
BIAS_ROWS = 16
WEIGHT_ROWS = 2 * D_IN + H1 + BIAS_ROWS
STREAMS = 8
PARTS = 2
CHUNK_ROWS = 64
VMEM_BYTES = 56 << 20

F32 = jnp.float32
BF16 = jnp.bfloat16
I32 = jnp.int32


def iota(shape, axis):
    return lax.broadcasted_iota(I32, shape, axis)


def matmul(a, b):
    return lax.dot_general(a, b, (((1,), (0,)), ((), ())), preferred_element_type=F32)


def matmul_nt(a, b):
    return lax.dot_general(a, b, (((1,), (1,)), ((), ())), preferred_element_type=F32)


def matmul_tn(a, b):
    return lax.dot_general(a, b, (((0,), (0,)), ((), ())), preferred_element_type=F32)


def identity():
    return (iota((LANES, LANES), 0) == iota((LANES, LANES), 1)).astype(BF16)


def aligned(value, step):
    return pl.multiple_of(value, step)


def silu_parts(values):
    sig = jax.nn.sigmoid(values)
    return values * sig, sig * (1.0 + values * (1.0 - sig))


def route_kernel(
    owners, part_lookups, packed, table_lanes, owner_ref, local_ref, request_ref, back_ref, out_ref,
    high_ref, low_ref, value_ref, total_ref
):
    rows = high_ref.shape[0]
    filled = owner_ref.shape[0]
    slot_rows = request_ref.shape[0]
    shape = (rows, LANES)
    high_ref[...] = jnp.full(shape, -1, I32)
    high_ref[0:filled, :] = owner_ref[...]
    owner = high_ref[...]
    low_ref[...] = jnp.zeros(shape, I32)
    low_ref[0:filled, :] = local_ref[...]
    local = low_ref[...]
    row_id = iota(shape, 0)
    tri = (iota((LANES, LANES), 0) <= iota((LANES, LANES), 1)).astype(BF16)
    ones = jnp.ones((LANES, LANES), BF16)
    before = (iota((rows, rows), 1) < iota((rows, rows), 0)).astype(BF16)
    part_rows = part_lookups // LANES
    rank = jnp.zeros(shape, F32)
    part_id = jnp.zeros(shape, I32)
    for part in range(1, PARTS):
        part_id = part_id + jnp.where(row_id >= part * part_rows, 1, 0)
    for part in range(PARTS):
        for one in range(owners):
            hit = (part_id == part) & (owner == one)
            hits = jnp.where(hit, 1.0, 0.0).astype(BF16)
            upto = matmul(hits, tri)
            ahead = matmul(before, matmul(hits, ones).astype(BF16))
            rank = jnp.where(hit, upto + ahead - 1.0, rank)
    rank = rank.astype(I32)
    group = jnp.zeros(shape, I32)
    for step in range(1, GROUPS):
        group = group + jnp.where(rank >= step * packed, 1, 0)
    place = rank - group * packed
    held = jnp.maximum(owner, 0)
    block = (held * PARTS + part_id) * (packed // 16) + lax.shift_right_logical(place, 4)
    inside = group * 16 + (place & 15)
    table_group = lax.shift_right_logical(local, table_lanes)
    table_row = local & ((1 << table_lanes) - 1)
    high_ref[...] = jnp.where(owner < 0, -1, block)
    low_ref[...] = inside
    value_ref[...] = table_row + (((group - table_group) & (GROUPS - 1)) << table_lanes)
    lookup = row_id * LANES + iota(shape, 1)
    quotient = jnp.floor((lookup.astype(F32) + 0.5) * (1.0 / FIELDS)).astype(I32)
    field_group = (lookup - quotient * FIELDS) & (GROUPS - 1)
    offset = 8 - (quotient & 7)
    turn = (field_group - group) & (GROUPS - 1)
    back_ref[...] = (turn * owners + held) * packed + place + offset
    out_ref[...] = block * LANES + inside + offset
    total_ref[...] = jnp.zeros_like(total_ref)

    def gather_requests(step, carry):
        base = aligned(step * 8, 8)
        high = high_ref[pl.ds(base, 8), :]
        low = low_ref[pl.ds(base, 8), :]
        values = value_ref[pl.ds(base, 8), :]
        upper = lax.shift_right_logical(values, 8).astype(F32)
        lower = (values & 255).astype(F32)
        at_high = []
        at_low = []
        for k in range(8):
            line = slice(k, k + 1)
            at_high.append(jnp.where(iota((slot_rows, LANES), 0) == high[line], 1.0, 0.0).astype(BF16))
            same = iota((LANES, LANES), 0) == low[line]
            at_low.append(
                jnp.concatenate(
                    [jnp.where(same, upper[line], 0.0), jnp.where(same, lower[line], 0.0)], axis=0
                ).astype(BF16)
            )
        total_ref[...] += matmul_nt(
            jnp.concatenate(at_high, axis=1), jnp.concatenate(at_low, axis=1)
        )
        return carry

    lax.fori_loop(0, rows // 8, gather_requests, 0, unroll=2)
    request_ref[...] = (total_ref[:, :LANES] * 256.0 + total_ref[:, LANES:]).astype(I32)


def pack_kernel(
    table_ref, hidden_w_ref, output_w_ref, hidden_b_ref, output_b_ref, packed_ref, weight_ref
):
    lines = []
    for values in (hidden_b_ref[:, :LANES], hidden_b_ref[:, LANES:], output_b_ref[...]):
        for _ in range(3):
            term = values.astype(BF16).astype(F32)
            lines.append(term)
            values = values - term
    lines.append(jnp.zeros((BIAS_ROWS - len(lines), LANES), F32))
    for half in range(H1 // LANES):
        weight_ref[half * D_IN : (half + 1) * D_IN, :] = hidden_w_ref[
            0, :, half * LANES : (half + 1) * LANES
        ]
    weight_ref[2 * D_IN : 2 * D_IN + H1, :] = output_w_ref[0]
    weight_ref[2 * D_IN + H1 :, :] = jnp.concatenate(lines, axis=0).astype(BF16)
    rows = table_ref.shape[1] // GROUPS
    eye = identity()

    def step(block, carry):
        pieces = []
        for group in range(GROUPS):
            start = aligned(group * rows + block * LANES, LANES)
            pieces.append(table_ref[:, pl.ds(start, LANES)])
        packed_ref[pl.ds(aligned(8 + block * LANES, 8), LANES), :] = matmul_nt(
            eye, jnp.concatenate(pieces, axis=0)
        )
        return carry

    packed_ref[0:8, :] = jnp.zeros((8, LANES), F32)
    packed_ref[8 + rows : 16 + rows, :] = jnp.zeros((8, LANES), F32)

    lax.fori_loop(0, rows // LANES, step, 0, unroll=8)


def masks():
    line = iota((8, LANES), 0)
    group = lax.shift_right_logical(iota((8, LANES), 1), 4)
    return [line == k for k in range(8)], [group == one for one in range(GROUPS)]


def turn_copies(rows_ref, wide_ref):
    rows = rows_ref.shape[0]
    half = GROUPS // 2
    from_lane = iota((LANES, half * LANES), 0)
    to_lane = iota((LANES, half * LANES), 1)
    turn = (lax.shift_right_logical(to_lane, 7) + half) * EMB
    turns = jnp.where(((from_lane + turn - to_lane) & (LANES - 1)) == 0, 1.0, 0.0).astype(BF16)

    def step(block, carry):
        start = aligned(block * LANES, LANES)
        piece = rows_ref[pl.ds(start, LANES), :]
        moved = matmul(piece, turns)
        piece = piece.astype(F32)
        for turn in range(GROUPS):
            if turn >= half:
                one = moved[:, (turn - half) * LANES : (turn - half + 1) * LANES]
            else:
                one = pltpu.roll(piece, turn * EMB, 1) if turn else piece
            wide_ref[pl.ds(aligned(8 + turn * rows + start, 8), LANES), :] = one
        return carry

    blocks = rows // LANES
    unroll = [count for count in (4, 3, 2, 1) if blocks % count == 0][0]
    lax.fori_loop(0, blocks, step, 0, unroll=unroll)


def assemble(wide_ref, word, groups, lines, lanes):
    block = jnp.zeros((8, LANES), F32)
    for place, group in groups:
        piece = wide_ref[pl.ds(word(0, place), 8), :]
        for k in range(1, 8):
            piece = jnp.where(lines[k], wide_ref[pl.ds(word(k, place), 8), :], piece)
        block = jnp.where(lanes[group], piece, block)
    return block


def word_stream(word_ref, buffers, sems, first, stride, count, process):
    slots = len(buffers)
    size = buffers[0].shape[0]

    def copy(at, slot):
        start = aligned(first + at * stride, LANES)
        return pltpu.make_async_copy(
            word_ref.at[pl.ds(start, size)], buffers[slot], sems.at[slot]
        )

    for slot in range(min(slots, count)):
        copy(slot, slot).start()

    def step(turn, carry):
        for slot in range(slots):
            at = turn * slots + slot
            copy(at, slot).wait()
            process(at, buffers[slot])

            @pl.when(at + slots < count)
            def _():
                copy(at + slots, slot).start()

        return carry

    lax.fori_loop(0, count // slots, step, 0)
    for slot in range(count % slots):
        at = count // slots * slots + slot
        copy(at, slot).wait()
        process(at, buffers[slot])


def slot_lines(numbers):
    own = (iota((16, LANES), 1) & 15) == iota((16, LANES), 0)
    return jnp.concatenate(
        [jnp.where(own, numbers[row : row + 1], 0.0) for row in range(numbers.shape[0])], axis=0
    ).astype(BF16)


def same_group():
    return (
        lax.shift_right_logical(iota((LANES, LANES), 0), 4)
        == lax.shift_right_logical(iota((LANES, LANES), 1), 4)
    ).astype(BF16)


def fetch_kernel(
    owners, part, packed, table_lanes, request_ref, asked_ref, table_ref, found_ref, turn_ref,
    left_ref, right_ref, sems
):
    lines, lanes = masks()
    chunks = packed // 16
    within = same_group()

    def turn_step(source, carry):
        at = (source * PARTS + part) * chunks
        numbers = lax.shift_right_logical(asked_ref[pl.ds(at, chunks), :], table_lanes)
        turn_ref[pl.ds(aligned(source * packed, 16), packed), :] = matmul(
            slot_lines(numbers.astype(F32)), within
        )
        return carry

    lax.fori_loop(0, owners, turn_step, 0)

    def process(source, words):
        for chunk in range(chunks):
            start = aligned(source * packed + chunk * 16, 16)
            turns = turn_ref[pl.ds(start, 16), :]
            halves = []
            for half in range(2):
                pieces = []
                for group in range(GROUPS):
                    base = chunk * LANES + group * 16 + half * 8
                    piece = table_ref[pl.ds(words[base], 8), :]
                    for k in range(1, 8):
                        piece = jnp.where(lines[k], table_ref[pl.ds(words[base + k], 8), :], piece)
                    pieces.append(piece)
                wanted = turns[half * 8 : (half + 1) * 8]
                block = jnp.zeros((8, LANES), F32)
                for turn in range(GROUPS):
                    mixed = pieces[turn]
                    for group in range(1, GROUPS):
                        mixed = jnp.where(lanes[group], pieces[(group + turn) % GROUPS], mixed)
                    if turn:
                        mixed = pltpu.roll(mixed, turn * EMB, 1)
                    block = jnp.where(wanted == float(turn), mixed, block)
                halves.append(block)
            found_ref[pl.ds(start, 16), :] = jnp.concatenate(halves, axis=0).astype(BF16)

    size = chunks * LANES
    word_stream(
        request_ref, (left_ref, right_ref), sems, part * size, PARTS * size, owners, process
    )


def unpermute(
    part, part_rows, back_ref, returned_ref, feature_ref, first_row, wide_ref, buffers, sems
):
    lines, lanes = masks()
    turn_copies(returned_ref, wide_ref)
    size = buffers[0].shape[0]
    chunk_rows = size // FIELDS

    def process(chunk, words):
        for block in range(chunk_rows // 16):
            start_row = aligned(first_row + chunk * chunk_rows + block * 16, 16)
            for lane_block in range(D_IN // LANES):
                fields = range(lane_block * GROUPS, min((lane_block + 1) * GROUPS, FIELDS))
                halves = [
                    assemble(
                        wide_ref,
                        lambda k, field, half=half: words[
                            (block * 16 + half * 8 + k) * FIELDS + field
                        ],
                        [(field, field % GROUPS) for field in fields],
                        lines,
                        lanes,
                    )
                    for half in range(2)
                ]
                feature_ref[
                    pl.ds(start_row, 16), lane_block * LANES : (lane_block + 1) * LANES
                ] = jnp.concatenate(halves, axis=0).astype(BF16)

    first = part * part_rows * FIELDS
    word_stream(back_ref, buffers, sems, first, size, part_rows // chunk_rows, process)


def unpermute_kernel(
    part, part_rows, back_ref, returned_ref, feature_ref, wide_ref, left_ref, right_ref, sems
):
    unpermute(
        part,
        part_rows,
        back_ref,
        returned_ref,
        feature_ref,
        0,
        wide_ref,
        (left_ref, right_ref),
        sems,
    )


def dense_kernel(
    part_rows,
    experts,
    scale,
    back_ref,
    out_ref,
    returned_ref,
    weight_ref,
    gate_ref,
    dense_ref,
    dense_w_ref,
    tower_ref,
    vector_ref,
    head_b_ref,
    label_ref,
    *refs,
):
    early = refs[: PARTS - 1]
    (
        sent_ref,
        grad_dense_ref,
        grad_weight_ref,
        grad_shared_ref,
        wide_ref,
        feature_ref,
        turned_ref,
        hidden_ref,
        hidden_slope_ref,
        output_ref,
        output_slope_ref,
        gates_ref,
        mixed_ref,
        mixed_grad_ref,
        dot_ref,
        logit_ref,
        input_ref,
        low_ref,
        tiled_ref,
        left_ref,
        right_ref,
        sems,
    ) = refs[PARTS - 1 :]
    buffers = (left_ref, right_ref)
    width = turned_ref.shape[1]
    blocks = width // LANES
    slot_blocks = sent_ref.shape[0] // 16
    eye = identity()
    lines, lanes = masks()

    def put_weight(expert, cut, value):
        grad_weight_ref[expert, cut, :] = value.astype(BF16)

    def put_shared(rows, cut, value):
        grad_shared_ref[rows, cut] = value

    whole = slice(None)
    for part in range(PARTS - 1):
        feature_ref[part * part_rows : (part + 1) * part_rows, :] = early[part][...]
    unpermute(
        PARTS - 1,
        part_rows,
        back_ref,
        returned_ref,
        feature_ref,
        (PARTS - 1) * part_rows,
        wide_ref,
        buffers,
        sems,
    )

    for lane_block in range(D_IN // LANES):
        for block in range(blocks):
            piece = feature_ref[
                block * LANES : (block + 1) * LANES, lane_block * LANES : (lane_block + 1) * LANES
            ]
            turned_ref[
                lane_block * LANES : (lane_block + 1) * LANES, block * LANES : (block + 1) * LANES
            ] = matmul_nt(eye, piece).astype(BF16)
    dense = dense_ref[...]
    dense_w = dense_w_ref[...]
    turned_ref[EMB_WIDTH:, :] = matmul_tn(dense_w, dense).astype(BF16)

    features = turned_ref[...]
    logits = matmul(gate_ref[...], features)
    for task in range(TASKS):
        part_logits = logits[task * experts : (task + 1) * experts]
        powers = jnp.exp(part_logits - jnp.max(part_logits, axis=0, keepdims=True))
        gates_ref[task * experts : (task + 1) * experts, :] = powers / jnp.sum(
            powers, axis=0, keepdims=True
        )

    mixed_ref[...] = jnp.zeros_like(mixed_ref)

    def column(line):
        tall = jnp.transpose(jnp.broadcast_to(line, (LANES, LANES)))
        return jnp.concatenate([tall] * blocks, axis=1)

    def bias_line(expert, rows):
        lines = [weight_ref[expert, 2 * D_IN + H1 :, :].astype(F32)[row : row + 1] for row in rows]
        return functools.reduce(jnp.add, lines)

    def forward(expert, carry):
        turned = turned_ref[...]
        for half in range(H1 // LANES):
            weights = weight_ref[expert, half * D_IN : (half + 1) * D_IN, :]
            bias = column(bias_line(expert, range(half * 3, half * 3 + 3)))
            value, slope = silu_parts(matmul_tn(weights, turned) + bias)
            hidden_ref[expert, half * LANES : (half + 1) * LANES, :] = value.astype(BF16)
            hidden_slope_ref[expert, half * LANES : (half + 1) * LANES, :] = slope
        weights = weight_ref[expert, 2 * D_IN : 2 * D_IN + H1, :]
        bias = column(bias_line(expert, (6, 7, 8)))
        value, slope = silu_parts(matmul_tn(weights, hidden_ref[expert]) + bias)
        output_ref[expert] = value
        output_slope_ref[expert] = slope
        for task in range(TASKS):
            mixed_ref[task * H2 : (task + 1) * H2, :] += (
                gates_ref[pl.ds(task * experts + expert, 1), :] * value
            )
        return carry

    lax.fori_loop(0, experts, forward, 0, unroll=2)

    tower_bias = column(vector_ref[0:1, :])
    head_w = column(vector_ref[1:2, :])
    tower = tower_ref[...]
    act_sums = []
    grad_sums = []
    head_sums = []
    for task in range(TASKS):
        units = slice(task * TOWER, (task + 1) * TOWER)
        outs = slice(task * H2, (task + 1) * H2)
        mixed = mixed_ref[outs, :]
        mixed_low = mixed.astype(BF16)
        tower_part = tower[:, units]
        act, slope = silu_parts(matmul_tn(tower_part, mixed_low) + tower_bias[units])
        score = jnp.sum(act * head_w[units], axis=0, keepdims=True) + head_b_ref[task]
        target = label_ref[task : task + 1, :].astype(F32)
        score_grad = (jax.nn.sigmoid(score) - target) * scale
        tower_grad = (score_grad * head_w[units] * slope).astype(BF16)
        act_sums.append(jnp.sum(score_grad * act, axis=1, keepdims=True))
        grad_sums.append(jnp.sum(tower_grad.astype(F32), axis=1, keepdims=True))
        head_sums.append(jnp.sum(score_grad, axis=1, keepdims=True))
        put_shared(slice(0, H2), units, matmul_nt(mixed_low, tower_grad))
        mixed_grad = matmul(tower_part, tower_grad).astype(BF16).astype(F32)
        mixed_grad_ref[outs, :] = mixed_grad
        dot_ref[task : task + 1, :] = jnp.sum(mixed_grad * mixed, axis=0, keepdims=True)
    column_sums = jnp.concatenate(
        [
            jnp.broadcast_to(jnp.concatenate(sums, axis=0), (LANES, LANES))
            for sums in (act_sums, grad_sums)
        ],
        axis=1,
    )
    put_shared(slice(H2, H2 + 8), whole, jnp.transpose(column_sums[:, :LANES])[0:8])
    put_shared(slice(H2 + 8, H2 + 16), whole, jnp.transpose(column_sums[:, LANES:])[0:8])
    head_line = jnp.zeros((8, LANES), F32)
    for task in range(TASKS):
        head_line = jnp.where(iota((8, LANES), 1) == task, head_sums[task], head_line)
    put_shared(slice(H2 + 16, H2 + 24), whole, head_line)

    input_ref[...] = jnp.zeros_like(input_ref)
    ones = jnp.ones((BIAS_ROWS, width), BF16)

    def backward(expert, carry):
        value = output_ref[expert]
        grad = jnp.zeros((H2, width), F32)
        for task in range(TASKS):
            mixed_grad = mixed_grad_ref[task * H2 : (task + 1) * H2, :]
            gate = gates_ref[pl.ds(task * experts + expert, 1), :]
            grad = grad + gate * mixed_grad
            along = jnp.sum(mixed_grad * value, axis=0, keepdims=True)
            logit_ref[pl.ds(task * experts + expert, 1), :] = gate * (
                along - dot_ref[task : task + 1, :]
            )
        output_grad = (grad * output_slope_ref[expert]).astype(BF16)
        hidden = hidden_ref[expert]
        put_weight(expert, slice(2 * D_IN, 2 * D_IN + H1), matmul_nt(hidden, output_grad))
        weights = weight_ref[expert, 2 * D_IN : 2 * D_IN + H1, :]
        hidden_grad = (matmul(weights, output_grad) * hidden_slope_ref[expert]).astype(BF16)
        turned = turned_ref[...]
        sums = []
        for half in range(H1 // LANES):
            half_grad = hidden_grad[half * LANES : (half + 1) * LANES]
            put_weight(
                expert, slice(half * D_IN, (half + 1) * D_IN), matmul_nt(turned, half_grad)
            )
            weights = weight_ref[expert, half * D_IN : (half + 1) * D_IN, :]
            input_ref[...] += matmul(weights, half_grad)
            sums.append(matmul_nt(ones, half_grad)[0:1])
        sums.append(matmul_nt(ones, output_grad)[0:1])
        sums.append(jnp.zeros((BIAS_ROWS - 3, LANES), F32))
        put_weight(expert, slice(2 * D_IN + H1, WEIGHT_ROWS), jnp.concatenate(sums, axis=0))
        return carry

    lax.fori_loop(0, experts, backward, 0, unroll=2)

    logit_grad = logit_ref[...].astype(BF16)
    gate_grad = matmul_nt(logit_grad, turned_ref[...])
    gate_base = H2 + 24
    pairs = TASKS * experts
    for lane_block in range(D_IN // LANES):
        put_shared(
            slice(gate_base + lane_block * pairs, gate_base + (lane_block + 1) * pairs),
            whole,
            gate_grad[:, lane_block * LANES : (lane_block + 1) * LANES],
        )
    low_ref[...] = (input_ref[...] + matmul_tn(gate_ref[...], logit_grad)).astype(BF16)
    bottom_grad = low_ref[EMB_WIDTH:, :]
    dense_base = gate_base + D_IN // LANES * pairs
    grad_dense_w = jnp.concatenate(
        [matmul_nt(dense, bottom_grad), jnp.zeros((DENSE, LANES - BOTTOM), F32)], axis=1
    )
    put_shared(
        slice(dense_base, dense_base + 16),
        whole,
        jnp.concatenate([grad_dense_w, jnp.zeros((16 - DENSE, LANES), F32)], axis=0),
    )
    grad_dense_ref[...] = matmul(dense_w, bottom_grad)

    def clear(step, carry):
        wide_ref[pl.ds(aligned(8 + step * LANES, 8), LANES), :] = jnp.zeros((LANES, LANES), F32)
        return carry

    lax.fori_loop(0, slot_blocks, clear, 0)
    chunk_rows = left_ref.shape[0] // FIELDS

    def permute(chunk, words):
        block = lax.div(chunk * chunk_rows, LANES)
        first = chunk * chunk_rows - block * LANES
        span = pl.ds(aligned(block * LANES, LANES), LANES)

        @pl.when(first == 0)
        def _():
            for field in range(FIELDS):
                piece = low_ref[field * EMB : (field + 1) * EMB, span]
                tiled_ref[field] = matmul_nt(eye, jnp.concatenate([piece] * GROUPS, axis=0))

        for step in range(chunk_rows // 8):
            start_row = aligned(first + step * 8, 8)
            for field in range(FIELDS):
                tile = tiled_ref[field, pl.ds(start_row, 8), :]
                for k in range(8):
                    start = words[(step * 8 + k) * FIELDS + field]
                    pltpu.store(wide_ref.at[pl.ds(start, 8), :], tile, mask=lines[k])

    word_stream(
        out_ref, buffers, sems, 0, chunk_rows * FIELDS, width // chunk_rows, permute
    )

    def merge(block, carry):
        halves = []
        for half in range(2):
            piece = jnp.zeros((8, LANES), F32)
            for group in range(GROUPS):
                start = aligned(block * LANES + group * 16 + (half + 1) * 8, 8)
                piece = jnp.where(lanes[group], wide_ref[pl.ds(start, 8), :], piece)
            halves.append(piece)
        start = aligned(block * 16, 16)
        sent_ref[pl.ds(start, 16), :] = jnp.concatenate(halves, axis=0).astype(BF16)
        return carry

    lax.fori_loop(0, slot_blocks, merge, 0, unroll=4 if slot_blocks % 4 == 0 else 1)


def add_kernel(
    packed,
    table_lanes,
    core_ref,
    request_ref,
    asked_ref,
    received_ref,
    total_ref,
    left_grad_ref,
    right_grad_ref,
    left_ref,
    right_ref,
    sems,
    *sums,
):
    rows = sums[0].shape[0] - 16
    core = core_ref[0]
    sources = received_ref.shape[0] // packed
    chunks = packed // 16
    lines, _ = masks()
    eye = identity()
    own_group = lax.shift_right_logical(iota((1, LANES), 1), 4)
    from_lane = iota((LANES, 2 * LANES), 0)
    to_lane = iota((LANES, 2 * LANES), 1)
    spread_names = []
    spread_grads = []
    for pair in range(GROUPS // 2):
        group = pair * 2 + lax.shift_right_logical(to_lane, 7)
        spread_names.append(
            jnp.where(lax.shift_right_logical(from_lane, 4) == group, 1.0, 0.0).astype(BF16)
        )
        wanted = group * EMB + (to_lane & (EMB - 1))
        spread_grads.append(jnp.where(from_lane == wanted, 1.0, 0.0).astype(BF16))

    def spread(source, grad_ref):
        asked = asked_ref[pl.ds(source * chunks, chunks), :]
        names = (own_group - lax.shift_right_logical(asked, table_lanes)) & (GROUPS - 1)
        names = names.astype(F32)
        for first in range(0, chunks, 8):
            count = min(8, chunks - first)
            held = slot_lines(names[first : first + count])
            start = aligned(source * packed + first * 16, 16)
            grads = received_ref[pl.ds(start, count * 16), :]
            lane_group = lax.shift_right_logical(iota((count * 16, LANES), 1), 4).astype(F32)
            for pair in range(GROUPS // 2):
                wide_names = matmul(held, spread_names[pair])
                wide_grads = matmul(grads, spread_grads[pair])
                for side in range(2):
                    half = slice(side * LANES, (side + 1) * LANES)
                    masked = jnp.where(wide_names[:, half] == lane_group, wide_grads[:, half], 0.0)
                    for chunk in range(count):
                        start = (first + chunk) * LANES + (pair * 2 + side) * 16
                        grad_ref[start : start + 16, :] = masked[chunk * 16 : (chunk + 1) * 16]

    def clear(step, carry):
        start = aligned(step * 16, 16)
        for total in sums:
            total[pl.ds(start, 16), :] = jnp.zeros((16, LANES), F32)
        return carry

    lax.fori_loop(0, (rows + 16) // 16, clear, 0)
    spread(0, left_grad_ref)

    def process(source, words):
        now, later = left_grad_ref, right_grad_ref
        if words is right_ref:
            now, later = later, now
        spread(jnp.minimum(source + 1, sources - 1), later)
        for row in range(GROUPS * packed // 8):
            grads = now[row * 8 : (row + 1) * 8, :]
            for k in range(8):
                place = pl.ds(words[row * 8 + k], 8)
                total = sums[k % STREAMS]
                pltpu.store(total.at[place, :], total[place, :] + grads, mask=lines[k])

    size = GROUPS * packed
    word_stream(request_ref, (left_ref, right_ref), sems, 0, size, sources, process)

    def finish(block, carry):
        start = aligned(8 + block * LANES, 8)
        total = functools.reduce(jnp.add, [one[pl.ds(start, LANES), :] for one in sums])
        turned = matmul_nt(eye, total.astype(BF16)).astype(BF16)
        for group in range(GROUPS):
            half, column = divmod(group, GROUPS // 2)
            column = aligned(column * rows + block * LANES, LANES)
            total_ref[half ^ core, :, pl.ds(column, LANES)] = turned[
                group * EMB : (group + 1) * EMB
            ]
        return carry

    lax.fori_loop(0, rows // LANES, finish, 0, unroll=8)


def unpack_kernel(weight_piece, shared_piece, pairs, piece_ref, *refs):
    (
        dense_w_ref,
        gate_ref,
        hidden_w_ref,
        hidden_b_ref,
        output_w_ref,
        output_b_ref,
        tower_w_ref,
        tower_b_ref,
        head_w_ref,
        head_b_ref,
        weight_ref,
        shared_ref,
    ) = refs
    for owner in range(piece_ref.shape[0]):
        weight_ref[owner * weight_piece : (owner + 1) * weight_piece, :] = piece_ref[
            owner, :weight_piece, :
        ].astype(F32)
        high = piece_ref[owner, weight_piece : weight_piece + shared_piece, :].astype(F32)
        low = piece_ref[owner, weight_piece + shared_piece :, :].astype(F32)
        shared_ref[owner * shared_piece : (owner + 1) * shared_piece, :] = high + low
    bias = 2 * D_IN + H1
    for half in range(H1 // LANES):
        span = slice(half * LANES, (half + 1) * LANES)
        hidden_w_ref[0, :, span] = weight_ref[half * D_IN : (half + 1) * D_IN, :]
        hidden_b_ref[:, span] = weight_ref[bias + half : bias + half + 1, :]
    output_w_ref[0] = weight_ref[2 * D_IN : bias, :]
    output_b_ref[...] = weight_ref[bias + 2 : bias + 3, :]
    tower_w_ref[...] = shared_ref[:H2, :]
    head_w_ref[...] = shared_ref[H2 : H2 + 1, :]
    tower_b_ref[...] = shared_ref[H2 + 8 : H2 + 9, :]
    head_b_ref[...] = shared_ref[H2 + 16 : H2 + 17, :TASKS]
    gate_base = H2 + 24
    for block in range(D_IN // LANES):
        gate_ref[:, block * LANES : (block + 1) * LANES] = shared_ref[
            gate_base + block * pairs : gate_base + (block + 1) * pairs, :
        ]
    dense_base = gate_base + D_IN // LANES * pairs
    dense_w_ref[...] = shared_ref[dense_base : dense_base + DENSE, :BOTTOM]


SMEM = pl.BlockSpec(memory_space=pltpu.SMEM)
VMEM = pl.BlockSpec(memory_space=pltpu.VMEM)
ANY = pl.BlockSpec(memory_space=pl.ANY)


def call(kernel, outs, ins, scratch, name, micros):
    return pl.pallas_call(
        kernel,
        out_shape=outs,
        in_specs=ins,
        out_specs=jax.tree.map(lambda _: VMEM, outs),
        scratch_shapes=scratch,
        name=name,
        cost_estimate=pl.CostEstimate(
            flops=int(micros * 1.15e9), bytes_accessed=int(micros * 3e6), transcendentals=0
        ),
        compiler_params=pltpu.CompilerParams(vmem_limit_bytes=VMEM_BYTES),
    )


def shards(
    emb_table,
    dense_feats,
    dense_w,
    gate_w,
    hidden_w,
    hidden_b,
    output_w,
    output_b,
    tower_w,
    tower_b,
    head_w,
    head_b,
    row_owner,
    local_row,
    labels,
):
    owners = lax.axis_size("batch")
    experts = lax.axis_size("expert")
    expert_index = lax.axis_index("expert")
    core = expert_index & 1
    row_total = dense_feats.shape[1]
    part_rows = row_total // PARTS
    lookups = row_total * FIELDS
    part_lookups = lookups // PARTS
    capacity = 2 * part_lookups // owners
    packed = -(-capacity // (GROUPS * 16)) * 16
    table_rows = emb_table.shape[0]
    table_packed = table_rows // GROUPS
    table_lanes = table_packed.bit_length() - 1
    scale = 1.0 / math.sqrt(row_total * owners * experts)
    slots = owners * PARTS * GROUPS * packed
    part_slots = owners * packed
    lookup_rows = lookups // LANES
    list_rows = -(-lookup_rows // 16) * 16

    def tie(*values):
        return lax.optimization_barrier(values)

    def exchange(values, axis):
        return lax.all_to_all(values, axis, split_axis=0, concat_axis=0, tiled=True)

    owner_list = row_owner.reshape(lookup_rows, LANES)
    local_list = local_row.reshape(lookup_rows, LANES)
    slot_rows = slots // LANES
    list_shape = jax.ShapeDtypeStruct((list_rows, LANES), I32)
    requests, back, out = call(
        functools.partial(route_kernel, owners, part_lookups, packed, table_lanes),
        (jax.ShapeDtypeStruct((slot_rows, LANES), I32), list_shape, list_shape),
        [VMEM, VMEM],
        [pltpu.VMEM((list_rows, LANES), I32)] * 3 + [pltpu.VMEM((slot_rows, 2 * LANES), F32)],
        "route",
        9,
    )(owner_list, local_list)
    asked = exchange(requests.reshape(owners, slots // owners), "batch")
    asked = asked.reshape(slot_rows, LANES)
    offset = 8 - (jnp.arange(LANES, dtype=I32) & 7)
    words = ((asked & (table_packed - 1)) + offset).reshape(-1)
    back = back.reshape(-1)
    out = out.reshape(-1)

    table, weights = call(
        pack_kernel,
        (
            jax.ShapeDtypeStruct((table_packed + 16, LANES), F32),
            jax.ShapeDtypeStruct((WEIGHT_ROWS, LANES), BF16),
        ),
        [VMEM] * 5,
        [],
        "pack",
        5,
    )(emb_table.T, hidden_w, output_w, hidden_b, output_b)
    weights = lax.all_gather(weights, "expert", axis=0, tiled=False)

    slot_words = [pltpu.SMEM((GROUPS * packed,), I32)] * 2 + [pltpu.SemaphoreType.DMA((2,))]
    row_words = [pltpu.SMEM((CHUNK_ROWS * FIELDS,), I32)] * 2 + [pltpu.SemaphoreType.DMA((2,))]
    returned = []
    for part in range(PARTS):
        found = call(
            functools.partial(fetch_kernel, owners, part, packed, table_lanes),
            jax.ShapeDtypeStruct((part_slots, LANES), BF16),
            [ANY, VMEM, VMEM],
            [pltpu.VMEM((part_slots, LANES), F32)] + slot_words,
            "fetch",
            24 // PARTS,
        )(words, asked, table)
        found = exchange(found.reshape(owners, packed, LANES), "batch")
        returned.append(found.reshape(part_slots, LANES))
    early = []
    for part in range(PARTS - 1):
        early.append(
            call(
                functools.partial(unpermute_kernel, part, part_rows),
                jax.ShapeDtypeStruct((part_rows, D_IN), BF16),
                [ANY, VMEM],
                [pltpu.VMEM((GROUPS * part_slots + 16, LANES), F32), *row_words],
                "unpermute",
                15,
            )(back, returned[part])
        )

    pairs = TASKS * experts
    shared_rows = H2 + 24 + D_IN // LANES * pairs + 16
    vectors = jnp.stack([tower_b, head_w])
    sent, grad_dense, grad_weight, grad_shared = call(
        functools.partial(dense_kernel, part_rows, experts, scale),
        (
            jax.ShapeDtypeStruct((PARTS * part_slots, LANES), BF16),
            jax.ShapeDtypeStruct((DENSE, row_total), F32),
            jax.ShapeDtypeStruct((experts, WEIGHT_ROWS, LANES), BF16),
            jax.ShapeDtypeStruct((shared_rows, LANES), F32),
        ),
        [ANY, ANY] + [VMEM] * 7 + [SMEM, VMEM] + [VMEM] * (PARTS - 1),
        [
            pltpu.VMEM((slots + 16, LANES), F32),
            pltpu.VMEM((row_total, D_IN), BF16),
            pltpu.VMEM((D_IN, row_total), BF16),
            pltpu.VMEM((experts, H1, row_total), BF16),
            pltpu.VMEM((experts, H1, row_total), F32),
            pltpu.VMEM((experts, H2, row_total), F32),
            pltpu.VMEM((experts, H2, row_total), F32),
            pltpu.VMEM((pairs, row_total), F32),
            pltpu.VMEM((TASKS * H2, row_total), F32),
            pltpu.VMEM((TASKS * H2, row_total), F32),
            pltpu.VMEM((8, row_total), F32),
            pltpu.VMEM((pairs, row_total), F32),
            pltpu.VMEM((D_IN, row_total), F32),
            pltpu.VMEM((D_IN, row_total), BF16),
            pltpu.VMEM((FIELDS, LANES, LANES), F32),
            *row_words,
        ],
        "dense",
        45,
    )(
        back,
        out,
        returned[-1],
        weights,
        gate_w.T,
        dense_feats,
        dense_w,
        tower_w,
        vectors,
        head_b,
        labels,
        *early,
    )
    received = exchange(sent.reshape(owners, PARTS * packed, LANES), "batch")
    received = received.reshape(PARTS * part_slots, LANES)

    def split(values):
        high = lax.reduce_precision(values, exponent_bits=8, mantissa_bits=7)
        return high.astype(BF16), (values - high).astype(BF16)

    weight_piece = -(-WEIGHT_ROWS // (16 * owners)) * 16
    shared_piece = -(-shared_rows // (16 * owners)) * 16
    piece_rows = weight_piece + 2 * shared_piece
    weight = jnp.pad(
        grad_weight, ((0, 0), (0, weight_piece * owners - WEIGHT_ROWS), (0, 0))
    ).reshape(experts, owners, weight_piece, LANES)
    shared = jnp.pad(grad_shared, ((0, shared_piece * owners - shared_rows), (0, 0)))
    pieces = jnp.concatenate(
        [weight.transpose(1, 0, 2, 3)]
        + [
            jnp.broadcast_to(
                one.reshape(owners, 1, shared_piece, LANES), (owners, experts, shared_piece, LANES)
            )
            for one in split(shared)
        ],
        axis=2,
    )
    received, pieces = tie(received, pieces)
    pieces = exchange(pieces.reshape(owners * experts, piece_rows, LANES), ("batch", "expert"))

    table_part = call(
        functools.partial(add_kernel, packed, table_lanes),
        jax.ShapeDtypeStruct((2, EMB, table_rows // 2), BF16),
        [SMEM, ANY, VMEM, VMEM],
        [pltpu.VMEM((GROUPS * packed, LANES), F32)] * 2
        + slot_words
        + [pltpu.VMEM((table_packed + 16, LANES), F32)] * STREAMS,
        "add",
        60,
    )(core.reshape(1), words, asked, received)

    table_part, pieces = tie(table_part, pieces)
    def swap(values, axis, bits):
        size = lax.axis_size(axis)
        return lax.ppermute(values, axis, [(one, one ^ bits) for one in range(size)])

    def add_low(left, right):
        return (left.astype(F32) + right.astype(F32)).astype(BF16)

    chunks = 2
    columns = table_rows // 2 // chunks
    kept = []
    for chunk in range(chunks):
        cut = slice(chunk * columns, (chunk + 1) * columns)
        kept.append(add_low(table_part[0, :, cut], swap(table_part[1, :, cut], "expert", 1)))
    sums = jnp.sum(pieces.astype(F32), axis=0)
    shared = sums[weight_piece : weight_piece + shared_piece] + sums[weight_piece + shared_piece :]
    piece = jnp.concatenate([sums[:weight_piece].astype(BF16), *split(shared)], axis=0)
    *kept, piece = tie(*kept, piece)
    pieces = exchange(jnp.broadcast_to(piece[None], (owners, piece_rows, LANES)), "batch")

    bit = 2
    while bit < experts:
        kept = [add_low(one, swap(one, "expert", bit)) for one in kept]
        bit *= 2
    small = call(
        functools.partial(unpack_kernel, weight_piece, shared_piece, pairs),
        tuple(
            jax.ShapeDtypeStruct(shape, F32)
            for shape in (
                (DENSE, BOTTOM),
                (pairs, D_IN),
                (1, D_IN, H1),
                (1, H1),
                (1, H1, H2),
                (1, H2),
                (H2, TASKS * TOWER),
                (1, TASKS * TOWER),
                (1, TASKS * TOWER),
                (1, TASKS),
            )
        ),
        [VMEM],
        [
            pltpu.VMEM((owners * weight_piece, LANES), F32),
            pltpu.VMEM((owners * shared_piece, LANES), F32),
        ],
        "unpack",
        3,
    )(pieces)
    *kept, small = tie(*kept, small)
    others = [swap(one, "expert", 1) for one in kept]
    lower = [jnp.where(core == 0, one, other) for one, other in zip(kept, others)]
    upper = [jnp.where(core == 0, other, one) for one, other in zip(kept, others)]
    table_total = jnp.concatenate(lower + upper, axis=1).astype(F32).T
    grad_dense_w, gate, hidden, hidden_bias, output, output_bias, tower, tower_bias, head, head_bias = (
        small
    )
    return (
        table_total,
        grad_dense,
        grad_dense_w,
        gate.T,
        hidden,
        hidden_bias,
        output,
        output_bias,
        tower,
        tower_bias.reshape(-1),
        head.reshape(-1),
        head_bias.reshape(-1),
    )


def solution(mesh):
    in_specs = (
        P("batch", None),
        P(None, ("batch", "expert")),
        P(),
        P(),
        P("expert", None, None),
        P("expert", None),
        P("expert", None, None),
        P("expert", None),
        P(),
        P(),
        P(),
        P(),
        P(("batch", "expert"), None),
        P(("batch", "expert")),
        P(None, ("batch", "expert")),
    )
    out_specs = (
        P("batch", None),
        P(None, ("batch", "expert")),
        P(),
        P(),
        P("expert", None, None),
        P("expert", None),
        P("expert", None, None),
        P("expert", None),
        P(),
        P(),
        P(),
        P(),
    )
    return jax.shard_map(shards, mesh=mesh, in_specs=in_specs, out_specs=out_specs, check_vma=False)
```

time: 1570 us -> 261 us (0.17)
  waiting for transfers between devices: 457 us -> 55.1 us
  local copies, waits for them, and re-layouts: 390 us -> 4.94 us
  other arithmetic: 383 us -> 7.69 us
  blocking collectives: 180 us -> 0 us
  Pallas kernels: 0 us -> 145 us
  matrix products: 60 us -> 0 us
  starting transfers between devices: 76.7 us -> 32.8 us
    psum x3 -> x0, waiting for transfers between devices: 360 us -> none  [the longest x1 243 us: shards(): lax.psum(acc_table.astype(jnp.bfloat16), 'expert').astype(jnp.float32)]
    scatter-add x4 -> x0, other arithmetic: 242 us -> none  [shards(): jax.ops.segment_sum(incoming.reshape(-1, EMB).astype(fp32), target_rows,...]
    scatter x8 -> x0, local copies, waits for them, and re-layouts: 155 us -> none  [the longest x4 82.2 us: shards(): jnp.full((owners * capacity,), -1, jnp.int32).at[slot_index].set(local_part)]
    pallas_call x0 -> x8, Pallas kernels: none -> 145 us  [the longest x1 42 us: shards(): call(functools.partial(add_kernel, packed, table_lanes), jax.ShapeDtypeSt...]
    gather x8 -> x0, local copies, waits for them, and re-layouts: 136 us -> none  [the longest x4 97.1 us: shards(): jnp.take(emb_table, jnp.clip(asked, 0, table_rows - 1).reshape(-1), axis=0)]
    psum x2 -> x0, blocking collectives: 102 us -> none  [the longest x1 79.5 us: shards(): lax.psum((acc_gate.reshape(D_IN, TASKS * experts), acc_dense_w, acc_tower...]
    all_gather x12 -> x0, blocking collectives: 78.2 us -> none  [the longest x4 31.4 us: shards(): gathered = lax.all_gather(features, 'expert', axis=0, tiled=True)]
    reduce_scatter x8 -> x0, waiting for transfers between devices: 77.1 us -> none  [the longest x4 56.2 us: shards(): lax.psum_scatter(weighted.astype(jnp.bfloat16), 'expert', scatter_dimensi...]
  transfers between devices with their start and end apart: 23 -> 13, of which waited for: 10 -> 10; matrix products, arithmetic and copies ran while one was open for 38% -> 2% of each run, Pallas kernels for 0% -> 37%
where the time goes in v1:
time: 261 us; the launch traced here: 260 us
  Pallas kernels  145 us (56%)
  waiting for transfers between devices  55.1 us (21%)
  starting transfers between devices  32.8 us (13%)
  between operations  14.3 us (5%)
  other arithmetic  7.69 us (3%)
  local copies, waits for them, and re-layouts  4.94 us (2%)
    pallas_call x1, Pallas kernels, shards(): call(functools.partial(add_kernel, packed, table_lanes), jax.ShapeDtypeSt...  42 us
    pallas_call x1, Pallas kernels, shards(): call(functools.partial(dense_kernel, part_rows, experts, scale), (jax.Sha...  37.8 us
    pallas_call x2, Pallas kernels, shards(): call(functools.partial(fetch_kernel, owners, part, packed, table_lanes),...  37 us
    all_to_all x6, waiting for transfers between devices, exchange(): return lax.all_to_all(values, axis, split_axis=0, concat_axis=0, tiled=True)  32.6 us
    all_to_all x6, starting transfers between devices, exchange(): return lax.all_to_all(values, axis, split_axis=0, concat_axis=0, tiled=True)  30 us
    ppermute x6, waiting for transfers between devices, swap(): lax.ppermute(values, axis, [(one, one ^ bits) for one in range(size)])  22.5 us
    pallas_call x1, Pallas kernels, shards(): call(functools.partial(unpermute_kernel, part, part_rows), jax.ShapeDtype...  9.93 us
    pallas_call x1, Pallas kernels, shards(): call(functools.partial(route_kernel, owners, part_lookups, packed, table_...  9.77 us
  transfers between devices with their start and end apart: 13, of which 10 were waited for; matrix products, arithmetic and copies ran while one was open for 2% of the time, Pallas kernels for 37%

profile of v1, /device:TPU:0, one launch (start us, length us, event | category | flops | bytes accessed | tf_op | source)
XLA Modules:
  0.0 259.6 jit_solution(1723296530817472870)
XLA Ops:
  7.2 1.7 reduce
  8.9 9.8 %route.1 = (s32[272,128]{1,0:T(8,128)}, s32[144,128]{1,0:T(8,128)}, s32[144,128]{1,0:T(8,128)}) custom-call(s32[130,128]{1,0:T(8,128)} %bitcast.60, s32[130,128]{1,0:T(8,128)} %bitcast.65), custom_call_target="tpu_custom_call" | custom-call | flops 10350000128 | bytes 27000000 | tf_op jit(solution)/shard_map/route/pallas_call | solution.py:829
  18.6 7.3 %all-to-all-start = ((s32[8,1,4352]{2,1,0:T(1,128)}), s32[8,1,4352]{2,1,0:T(1,128)S(1)}, u32[]{:S(2)}, u32[]{:S(2)}) async-start(s32[8,1,4352]{2,1,0:T(1,128)} %bitcast.59), calls=%async_computation | async-start | bytes 278528 | tf_op jit(solution)/shard_map/all_to_all | solution.py:823
  25.9 6.2 %pack.1 = (f32[8208,128]{1,0:T(8,128)}, bf16[1296,128]{1,0:T(8,128)(2,1)}) custom-call(bf16[16,65536]{1,0:T(8,128)(2,1)} %bitcast.63, bf16[1,512,256]{2,1,0:T(8,128)(2,1)} %hidden_w_ref.1, bf16[1,256,128]{2,1,0:T(8,128)(2,1)} %output_w_ref.1, f32[1,256]{1,0:T(1,128)} %hidden_b_ref.1, f32[1,128]{1,0:T(1,128)} %output_b_ref.1), custom_call_target="tpu_custom_call" | custom-call | flops 5750000128 | bytes 15000000 | tf_op jit(solution)/shard_map/pack/pallas_call | solution.py:844
  34.1 18.5 %fetch.3 = bf16[2176,128]{1,0:T(8,128)(2,1)} custom-call(s32[34816]{0:T(1024)} %bitcast_add_fusion.request_ref, s32[272,128]{1,0:T(8,128)} %bitcast.53, f32[8208,128]{1,0:T(8,128)} %get-tuple-element.53.table_ref), custom_call_target="tpu_custom_call" | custom-call | flops 13799999488 | bytes 36000000 | tf_op jit(solution)/shard_map/fetch/pallas_call | solution.py:861
  52.6 5.4 %all-to-all-start.2 = ((bf16[8,272,128]{2,1,0:T(8,128)(2,1)}), bf16[8,272,128]{2,1,0:T(8,128)(2,1)S(1)}, u32[]{:S(2)}, u32[]{:S(2)}) async-start(bf16[8,272,128]{2,1,0:T(8,128)(2,1)} %bitcast.52), calls=%async_computation.2 | async-start | bytes 1114112 | tf_op jit(solution)/shard_map/all_to_all | solution.py:823
  58.1 18.5 %fetch.2 = bf16[2176,128]{1,0:T(8,128)(2,1)} custom-call(s32[34816]{0:T(1024)} %bitcast_add_fusion.request_ref, s32[272,128]{1,0:T(8,128)} %bitcast.54, f32[8208,128]{1,0:T(8,128)} %get-tuple-element.53.table_ref), custom_call_target="tpu_custom_call" | custom-call | flops 13799999488 | bytes 36000000 | tf_op jit(solution)/shard_map/fetch/pallas_call | solution.py:861
  76.6 6.0 %all-to-all-start.1 = ((bf16[8,272,128]{2,1,0:T(8,128)(2,1)}), bf16[8,272,128]{2,1,0:T(8,128)(2,1)S(1)}, u32[]{:S(2)}, u32[]{:S(2)}) async-start(bf16[8,272,128]{2,1,0:T(8,128)(2,1)} %bitcast.51), calls=%async_computation.1 | async-start | bytes 1114112 | tf_op jit(solution)/shard_map/all_to_all | solution.py:823
  82.6 9.9 %unpermute.1.refs_0_ = bf16[320,512]{1,0:T(8,128)(2,1)} custom-call(s32[18432]{0:T(1024)} %bitcast.67, bf16[2176,128]{1,0:T(8,128)(2,1)} %bitcast.50), custom_call_target="tpu_custom_call" | custom-call | flops 17250000896 | bytes 45000000 | tf_op jit(solution)/shard_map/unpermute/pallas_call | solution.py:874
  92.5 4.2 %all-to-all-done.1 = bf16[8,272,128]{2,1,0:T(8,128)(2,1)S(1)} async-done(((bf16[8,272,128]{2,1,0:T(8,128)(2,1)}), bf16[8,272,128]{2,1,0:T(8,128)(2,1)S(1)}, u32[]{:S(2)}, u32[]{:S(2)}) %all-to-all-start.1) | async-done | bytes 557088 | tf_op jit(solution)/shard_map/all_to_all | solution.py:823
  97.5 37.8 %dense.1 = (bf16[4352,128]{1,0:T(8,128)(2,1)}, f32[13,640]{1,0:T(8,128)}, bf16[4,1296,128]{2,1,0:T(8,128)(2,1)}, f32[200,128]{1,0:T(8,128)}) custom-call(s32[18432]{0:T(1024)} %bitcast.68, s32[18432]{0:T(1024)} %bitcast.69, bf16[2176,128]{1,0:T(8,128)(2,1)} %bitcast.49, bf16[4,1296,128]{2,1,0:T(8,128)(2,1)} %bitcast.64, bf16[8,512]{1,0:T(8,128)(2,1)} %bitcast.66, ...), custom_call_target="tpu_custom_call" | custom-call | flops 51749998592 | bytes 135000000 | tf_op jit(solution)/shard_map/dense/pallas_call | solution.py:887
  135.4 3.8 %all-to-all-start.3 = ((bf16[8,544,128]{2,1,0:T(8,128)(2,1)}), bf16[8,544,128]{2,1,0:T(8,128)(2,1)S(1)}, u32[]{:S(2)}, u32[]{:S(2)}) async-start(bf16[8,544,128]{2,1,0:T(8,128)(2,1)} %bitcast.48), calls=%async_computation.3 | async-start | bytes 2228224 | tf_op jit(solution)/shard_map/all_to_all | solution.py:823
  140.3 1.4 pad_maximum_fusion
  141.8 24.0 %all-to-all-done.3 = bf16[8,544,128]{2,1,0:T(8,128)(2,1)S(1)} async-done(((bf16[8,544,128]{2,1,0:T(8,128)(2,1)}), bf16[8,544,128]{2,1,0:T(8,128)(2,1)S(1)}, u32[]{:S(2)}, u32[]{:S(2)}) %all-to-all-start.3) | async-done | bytes 1114144 | tf_op jit(solution)/shard_map/all_to_all | solution.py:823
  165.8 3.4 %all-to-all-start.4 = ((bf16[32,240,128]{2,1,0:T(8,128)(2,1)}), bf16[32,240,128]{2,1,0:T(8,128)(2,1)S(1)}, u32[]{:S(2)}, u32[]{:S(2)}) async-start(bf16[32,240,128]{2,1,0:T(8,128)(2,1)} %bitcast.44), calls=%async_computation.4 | async-start | bytes 3932160 | tf_op jit(solution)/shard_map/all_to_all | solution.py:823
  169.2 42.0 %add.55 = bf16[2,16,32768]{2,1,0:T(8,128)(2,1)} custom-call(s32[1]{0:T(128)} %bitcast.core_ref, s32[34816]{0:T(1024)} %bitcast_add_fusion.request_ref, s32[272,128]{1,0:T(8,128)} %bitcast.55, bf16[4352,128]{1,0:T(8,128)(2,1)} %bitcast.47), custom_call_target="tpu_custom_call" | custom-call | flops 69000003584 | bytes 180000000 | tf_op jit(solution)/shard_map/add/pallas_call | solution.py:957
  211.2 3.9 %all-to-all-done.4 = bf16[32,240,128]{2,1,0:T(8,128)(2,1)S(1)} async-done(((bf16[32,240,128]{2,1,0:T(8,128)(2,1)}), bf16[32,240,128]{2,1,0:T(8,128)(2,1)S(1)}, u32[]{:S(2)}, u32[]{:S(2)}) %all-to-all-start.4) | async-done | bytes 1966112 | tf_op jit(solution)/shard_map/all_to_all | solution.py:823
  215.1 1.4 slice_bitcast_fusion
  219.5 1.5 collective-permute-start.2
  221.9 4.0 %all-to-all-start.5 = ((bf16[8,240,128]{2,1,0:T(8,128)(2,1)}), bf16[8,240,128]{2,1,0:T(8,128)(2,1)S(1)}, u32[]{:S(2)}, u32[]{:S(2)}) async-start(bf16[8,240,128]{2,1,0:T(8,128)(2,1)} %broadcast_in_dim.25), calls=%async_computation.5 | async-start | bytes 983040 | tf_op jit(solution)/shard_map/all_to_all | solution.py:823
  226.1 8.3 %collective-permute-done.2 = bf16[16,16384]{1,0:T(8,128)(2,1)S(1)} collective-permute-done((bf16[16,16384]{1,0:T(8,128)(2,1)S(1)}, bf16[16,16384]{1,0:T(8,128)(2,1)S(1)}, u32[]{:S(2)}, u32[]{:S(2)}) %collective-permute-start.2) | collective-permute-done | bytes 524320 | tf_op jit(solution)/shard_map/ppermute | solution.py:971
  234.5 10.3 %collective-permute-done.3 = bf16[16,16384]{1,0:T(8,128)(2,1)S(1)} collective-permute-done((bf16[16,16384]{1,0:T(8,128)(2,1)S(1)}, bf16[16,16384]{1,0:T(8,128)(2,1)S(1)}, u32[]{:S(2)}, u32[]{:S(2)}) %collective-permute-start.3) | collective-permute-done | bytes 524320 | tf_op jit(solution)/shard_map/ppermute | solution.py:971
  245.7 1.9 unpack.1
  250.5 2.3 convert_bitcast_fusion
  (54 shorter events, 11.6 us)
Async XLA Ops:
  18.6 14.7 %all-to-all-start = ((s32[8,1,4352]{2,1,0:T(1,128)}), s32[8,1,4352]{2,1,0:T(1,128)S(1)}, u32[]{:S(2)}, u32[]{:S(2)}) async-start(s32[8,1,4352]{2,1,0:T(1,128)} %bitcast.59), calls=%async_computation | async-start | bytes 278528 | tf_op jit(solution)/shard_map/all_to_all | solution.py:823
  25.9 70.9 %all-gather.3.cloned.1.call-start = ((), (), s32[]{:S(2)}) async-start(), calls=%async_computation.6 | async-start | bytes 1658880 | tf_op jit(solution)/shard_map/all_gather | solution.py:855
  25.9 6.3 %copy-start.8 = (f32[128]{0:T(128)S(1)}, f32[128]{0:T(128)}, u32[]{:S(2)}) copy-start(f32[128]{0:T(128)} %param.25) | copy-start | bytes 1540
  25.9 6.3 %copy-start.9 = (f32[128]{0:T(128)S(1)}, f32[128]{0:T(128)}, u32[]{:S(2)}) copy-start(f32[128]{0:T(128)} %param.24) | copy-start | bytes 1540
  33.3 0.8 copy-start.5
  52.6 24.0 %all-to-all-start.2 = ((bf16[8,272,128]{2,1,0:T(8,128)(2,1)}), bf16[8,272,128]{2,1,0:T(8,128)(2,1)S(1)}, u32[]{:S(2)}, u32[]{:S(2)}) async-start(bf16[8,272,128]{2,1,0:T(8,128)(2,1)} %bitcast.52), calls=%async_computation.2 | async-start | bytes 1114112 | tf_op jit(solution)/shard_map/all_to_all | solution.py:823
  76.6 6.0 %copy-start.4 = (bf16[8,272,128]{2,1,0:T(8,128)(2,1)}, bf16[8,272,128]{2,1,0:T(8,128)(2,1)S(1)}, u32[]{:S(2)}) copy-start(bf16[8,272,128]{2,1,0:T(8,128)(2,1)S(1)} %all-to-all-done.2) | copy-start | bytes 1671172
  76.6 20.2 %all-to-all-start.1 = ((bf16[8,272,128]{2,1,0:T(8,128)(2,1)}), bf16[8,272,128]{2,1,0:T(8,128)(2,1)S(1)}, u32[]{:S(2)}, u32[]{:S(2)}) async-start(bf16[8,272,128]{2,1,0:T(8,128)(2,1)} %bitcast.51), calls=%async_computation.1 | async-start | bytes 1114112 | tf_op jit(solution)/shard_map/all_to_all | solution.py:823
  96.7 0.8 copy-start.3
  135.4 3.9 %copy-start.1 = (bf16[4,1296,128]{2,1,0:T(8,128)(2,1)S(1)}, bf16[4,1296,128]{2,1,0:T(8,128)(2,1)}, u32[]{:S(2)}) copy-start(bf16[4,1296,128]{2,1,0:T(8,128)(2,1)} %get-tuple-element.56) | copy-start | bytes 3981316
  135.4 30.4 %all-to-all-start.3 = ((bf16[8,544,128]{2,1,0:T(8,128)(2,1)}), bf16[8,544,128]{2,1,0:T(8,128)(2,1)S(1)}, u32[]{:S(2)}, u32[]{:S(2)}) async-start(bf16[8,544,128]{2,1,0:T(8,128)(2,1)} %bitcast.48), calls=%async_computation.3 | async-start | bytes 2228224 | tf_op jit(solution)/shard_map/all_to_all | solution.py:823
  139.3 0.9 copy-start.7
  165.8 3.4 %copy-start.2 = (bf16[8,544,128]{2,1,0:T(8,128)(2,1)}, bf16[8,544,128]{2,1,0:T(8,128)(2,1)S(1)}, u32[]{:S(2)}) copy-start(bf16[8,544,128]{2,1,0:T(8,128)(2,1)S(1)} %all-to-all-done.3) | copy-start | bytes 3342340
  165.8 49.4 %all-to-all-start.4 = ((bf16[32,240,128]{2,1,0:T(8,128)(2,1)}), bf16[32,240,128]{2,1,0:T(8,128)(2,1)S(1)}, u32[]{:S(2)}, u32[]{:S(2)}) async-start(bf16[32,240,128]{2,1,0:T(8,128)(2,1)} %bitcast.44), calls=%async_computation.4 | async-start | bytes 3932160 | tf_op jit(solution)/shard_map/all_to_all | solution.py:823
  215.1 4.2 %copy-start = (bf16[2,16,32768]{2,1,0:T(8,128)(2,1)S(1)}, bf16[2,16,32768]{2,1,0:T(8,128)(2,1)}, u32[]{:S(2)}) copy-start(bf16[2,16,32768]{2,1,0:T(8,128)(2,1)} %add.55) | copy-start | bytes 6291460
  216.6 2.0 collective-permute-start.1
  216.6 2.6 %collective-permute-start = (bf16[16,16384]{1,0:T(8,128)(2,1)S(1)}, bf16[16,16384]{1,0:T(8,128)(2,1)S(1)}, u32[]{:S(2)}, u32[]{:S(2)}) collective-permute-start(bf16[16,16384]{1,0:T(8,128)(2,1)S(1)} %get-tuple-element.91), channel_id=1, source_target_pairs={{0,1},{1,0},{2,3},{3,2},{4,5},{5,4},{6,7},{7,6},{8,9},{9,8},{10,11... | collective-permute-start | bytes 1572872 | tf_op jit(solution)/shard_map/ppermute | solution.py:971
  219.5 14.8 %collective-permute-start.2 = (bf16[16,16384]{1,0:T(8,128)(2,1)S(1)}, bf16[16,16384]{1,0:T(8,128)(2,1)S(1)}, u32[]{:S(2)}, u32[]{:S(2)}) collective-permute-start(bf16[16,16384]{1,0:T(8,128)(2,1)S(1)} %get-tuple-element.62), channel_id=1, source_target_pairs={{0,2},{1,3},{2,0},{3,1},{4,6},{5,7},{6,4},{7,5},{8,10},{9,11},{10,... | collective-permute-start | bytes 1572872 | tf_op jit(solution)/shard_map/ppermute | solution.py:971
  221.9 23.1 %all-to-all-start.5 = ((bf16[8,240,128]{2,1,0:T(8,128)(2,1)}), bf16[8,240,128]{2,1,0:T(8,128)(2,1)S(1)}, u32[]{:S(2)}, u32[]{:S(2)}) async-start(bf16[8,240,128]{2,1,0:T(8,128)(2,1)} %broadcast_in_dim.25), calls=%async_computation.5 | async-start | bytes 983040 | tf_op jit(solution)/shard_map/all_to_all | solution.py:823
  225.9 18.9 %collective-permute-start.3 = (bf16[16,16384]{1,0:T(8,128)(2,1)S(1)}, bf16[16,16384]{1,0:T(8,128)(2,1)S(1)}, u32[]{:S(2)}, u32[]{:S(2)}) collective-permute-start(bf16[16,16384]{1,0:T(8,128)(2,1)S(1)} %get-tuple-element.63), channel_id=1, source_target_pairs={{0,2},{1,3},{2,0},{3,1},{4,6},{5,7},{6,4},{7,5},{8,10},{9,11},{10,... | collective-permute-start | bytes 1572872 | tf_op jit(solution)/shard_map/ppermute | solution.py:971
  244.9 0.8 copy-start.6
  247.7 2.0 collective-permute-start.4
  247.8 2.6 %collective-permute-start.5 = (bf16[16,16384]{1,0:T(8,128)(2,1)S(1)}, bf16[16,16384]{1,0:T(8,128)(2,1)S(1)}, u32[]{:S(2)}, u32[]{:S(2)}) collective-permute-start(bf16[16,16384]{1,0:T(8,128)(2,1)S(1)} %add_convert_fusion), channel_id=1, source_target_pairs={{0,1},{1,0},{2,3},{3,2},{4,5},{5,4},{6,7},{7,6},{8,9},{9,8},{10,11... | collective-permute-start | bytes 1572872 | tf_op jit(solution)/shard_map/ppermute | solution.py:971
Sparse Core Ops, SparseCore 0:
  32.3 19.6 all-gather.2

commit v2 on v1

--- a/solution.py
+++ b/solution.py
@@ -21,11 +21,12 @@
 GROUPS = LANES // EMB
 EMB_WIDTH = FIELDS * EMB
 BIAS_ROWS = 16
-WEIGHT_ROWS = 2 * D_IN + H1 + BIAS_ROWS
+GRAD_ROWS = 2 * D_IN + H1
+WEIGHT_ROWS = GRAD_ROWS + BIAS_ROWS
 STREAMS = 8
 PARTS = 2
 CHUNK_ROWS = 64
-VMEM_BYTES = 56 << 20
+TABLE_CHUNKS = 2
 
 F32 = jnp.float32
 BF16 = jnp.bfloat16
@@ -62,59 +63,70 @@
 
 
 def route_kernel(
-    owners, part_lookups, packed, table_lanes, owner_ref, local_ref, request_ref, back_ref, out_ref,
-    high_ref, low_ref, value_ref, total_ref
+    owners, part_lookups, packed, table_lanes, batch_ref, owner_ref, local_ref, request_ref,
+    back_ref, out_ref, high_ref, low_ref, value_ref, total_ref
 ):
     rows = high_ref.shape[0]
-    filled = owner_ref.shape[0]
+    part_rows = rows // PARTS
+    filled = part_lookups // LANES
     slot_rows = request_ref.shape[0]
     shape = (rows, LANES)
     high_ref[...] = jnp.full(shape, -1, I32)
-    high_ref[0:filled, :] = owner_ref[...]
+    low_ref[...] = jnp.zeros(shape, I32)
+    for part in range(PARTS):
+        lines = slice(part * part_rows, part * part_rows + filled)
+        taken = slice(part * filled, (part + 1) * filled)
+        high_ref[lines, :] = owner_ref[taken, :]
+        low_ref[lines, :] = local_ref[taken, :]
     owner = high_ref[...]
-    low_ref[...] = jnp.zeros(shape, I32)
-    low_ref[0:filled, :] = local_ref[...]
     local = low_ref[...]
     row_id = iota(shape, 0)
     tri = (iota((LANES, LANES), 0) <= iota((LANES, LANES), 1)).astype(BF16)
     ones = jnp.ones((LANES, LANES), BF16)
-    before = (iota((rows, rows), 1) < iota((rows, rows), 0)).astype(BF16)
-    part_rows = part_lookups // LANES
-    rank = jnp.zeros(shape, F32)
-    part_id = jnp.zeros(shape, I32)
-    for part in range(1, PARTS):
-        part_id = part_id + jnp.where(row_id >= part * part_rows, 1, 0)
+    before = (iota((part_rows, part_rows), 1) < iota((part_rows, part_rows), 0)).astype(BF16)
+    ranks = []
     for part in range(PARTS):
+        own = owner[part * part_rows : (part + 1) * part_rows]
+        rank = jnp.zeros((part_rows, LANES), F32)
         for one in range(owners):
-            hit = (part_id == part) & (owner == one)
+            hit = own == one
             hits = jnp.where(hit, 1.0, 0.0).astype(BF16)
             upto = matmul(hits, tri)
             ahead = matmul(before, matmul(hits, ones).astype(BF16))
             rank = jnp.where(hit, upto + ahead - 1.0, rank)
+        ranks.append(rank)
+    rank = jnp.concatenate(ranks, axis=0)
+    part_id = jnp.zeros(shape, I32)
+    for part in range(1, PARTS):
+        part_id = part_id + jnp.where(row_id >= part * part_rows, 1, 0)
     rank = rank.astype(I32)
     group = jnp.zeros(shape, I32)
     for step in range(1, GROUPS):
         group = group + jnp.where(rank >= step * packed, 1, 0)
     place = rank - group * packed
     held = jnp.maximum(owner, 0)
-    block = (held * PARTS + part_id) * (packed // 16) + lax.shift_right_logical(place, 4)
+    chunks = packed // 16
+    chunk = lax.shift_right_logical(place, 4)
+    block = (held * PARTS + part_id) * chunks + chunk
     inside = group * 16 + (place & 15)
     table_group = lax.shift_right_logical(local, table_lanes)
     table_row = local & ((1 << table_lanes) - 1)
-    high_ref[...] = jnp.where(owner < 0, -1, block)
+    high_ref[...] = jnp.where(owner < 0, -1, held * chunks + chunk)
     low_ref[...] = inside
     value_ref[...] = table_row + (((group - table_group) & (GROUPS - 1)) << table_lanes)
-    lookup = row_id * LANES + iota(shape, 1)
+    lookup = (row_id - part_id * part_rows) * LANES + iota(shape, 1)
     quotient = jnp.floor((lookup.astype(F32) + 0.5) * (1.0 / FIELDS)).astype(I32)
     field_group = (lookup - quotient * FIELDS) & (GROUPS - 1)
     offset = 8 - (quotient & 7)
     turn = (field_group - group) & (GROUPS - 1)
     back_ref[...] = (turn * owners + held) * packed + place + offset
-    out_ref[...] = block * LANES + inside + offset
+    away = ((held ^ batch_ref[0]) - held) * (PARTS * GROUPS * packed)
+    out_ref[...] = block * LANES + inside + offset + away
     total_ref[...] = jnp.zeros_like(total_ref)
-
-    def gather_requests(step, carry):
-        base = aligned(step * 8, 8)
+    own_rows = slot_rows // PARTS
+
+    def gather_requests(part, step, carry):
+        base = aligned(part * part_rows + step * 8, 8)
         high = high_ref[pl.ds(base, 8), :]
         low = low_ref[pl.ds(base, 8), :]
         values = value_ref[pl.ds(base, 8), :]
@@ -124,20 +136,24 @@
         at_low = []
         for k in range(8):
             line = slice(k, k + 1)
-            at_high.append(jnp.where(iota((slot_rows, LANES), 0) == high[line], 1.0, 0.0).astype(BF16))
+            at_high.append(jnp.where(iota((own_rows, LANES), 0) == high[line], 1.0, 0.0).astype(BF16))
             same = iota((LANES, LANES), 0) == low[line]
             at_low.append(
                 jnp.concatenate(
                     [jnp.where(same, upper[line], 0.0), jnp.where(same, lower[line], 0.0)], axis=0
                 ).astype(BF16)
             )
-        total_ref[...] += matmul_nt(
+        total_ref[part] += matmul_nt(
             jnp.concatenate(at_high, axis=1), jnp.concatenate(at_low, axis=1)
         )
         return carry
 
-    lax.fori_loop(0, rows // 8, gather_requests, 0, unroll=2)
-    request_ref[...] = (total_ref[:, :LANES] * 256.0 + total_ref[:, LANES:]).astype(I32)
+    for part in range(PARTS):
+        lax.fori_loop(0, part_rows // 8, functools.partial(gather_requests, part), 0, unroll=3)
+        total = (total_ref[part, :, :LANES] * 256.0 + total_ref[part, :, LANES:]).astype(I32)
+        for one in range(owners):
+            start = (one * PARTS + part) * chunks
+            request_ref[start : start + chunks, :] = total[one * chunks : (one + 1) * chunks]
 
 
 def pack_kernel(
@@ -217,18 +233,20 @@
     return block
 
 
-def word_stream(word_ref, buffers, sems, first, stride, count, process):
+def word_stream(word_ref, buffers, sems, place, count, process, before=None):
     slots = len(buffers)
     size = buffers[0].shape[0]
 
     def copy(at, slot):
-        start = aligned(first + at * stride, LANES)
+        start = aligned(place(at), LANES)
         return pltpu.make_async_copy(
             word_ref.at[pl.ds(start, size)], buffers[slot], sems.at[slot]
         )
 
     for slot in range(min(slots, count)):
         copy(slot, slot).start()
+    if before is not None:
+        before()
 
     def step(turn, carry):
         for slot in range(slots):
@@ -265,11 +283,13 @@
 
 def fetch_kernel(
     owners, part, packed, table_lanes, request_ref, asked_ref, table_ref, found_ref, turn_ref,
-    left_ref, right_ref, sems
+    piece_ref, left_ref, right_ref, sems
 ):
-    lines, lanes = masks()
+    lines, _ = masks()
     chunks = packed // 16
     within = same_group()
+    group = lax.shift_right_logical(iota((8, LANES), 1), 4)
+    bits = [(group & (1 << bit)) != 0 for bit in range(3)]
 
     def turn_step(source, carry):
         at = (source * PARTS + part) * chunks
@@ -279,36 +299,48 @@
         )
         return carry
 
-    lax.fori_loop(0, owners, turn_step, 0)
+    def before():
+        lax.fori_loop(0, owners, turn_step, 0, unroll=4)
 
     def process(source, words):
         for chunk in range(chunks):
+            for line in range(LANES):
+                base = chunk * LANES + line // 8 * 8
+                pltpu.store(
+                    piece_ref.at[base : base + 8, :],
+                    table_ref[pl.ds(words[chunk * LANES + line], 8), :],
+                    mask=lines[line % 8],
+                )
             start = aligned(source * packed + chunk * 16, 16)
             turns = turn_ref[pl.ds(start, 16), :]
             halves = []
             for half in range(2):
-                pieces = []
+                mixed = []
                 for group in range(GROUPS):
                     base = chunk * LANES + group * 16 + half * 8
-                    piece = table_ref[pl.ds(words[base], 8), :]
-                    for k in range(1, 8):
-                        piece = jnp.where(lines[k], table_ref[pl.ds(words[base + k], 8), :], piece)
-                    pieces.append(piece)
+                    mixed.append(piece_ref[base : base + 8, :])
+                for bit in range(3):
+                    mixed = [
+                        jnp.where(bits[bit], mixed[(turn + (1 << bit)) % GROUPS], mixed[turn])
+                        for turn in range(GROUPS)
+                    ]
                 wanted = turns[half * 8 : (half + 1) * 8]
-                block = jnp.zeros((8, LANES), F32)
-                for turn in range(GROUPS):
-                    mixed = pieces[turn]
-                    for group in range(1, GROUPS):
-                        mixed = jnp.where(lanes[group], pieces[(group + turn) % GROUPS], mixed)
-                    if turn:
-                        mixed = pltpu.roll(mixed, turn * EMB, 1)
-                    block = jnp.where(wanted == float(turn), mixed, block)
+                block = mixed[0]
+                for turn in range(1, GROUPS):
+                    moved = pltpu.roll(mixed[turn], turn * EMB, 1)
+                    block = jnp.where(wanted == float(turn), moved, block)
                 halves.append(block)
             found_ref[pl.ds(start, 16), :] = jnp.concatenate(halves, axis=0).astype(BF16)
 
     size = chunks * LANES
     word_stream(
-        request_ref, (left_ref, right_ref), sems, part * size, PARTS * size, owners, process
+        request_ref,
+        (left_ref, right_ref),
+        sems,
+        lambda at: (at * PARTS + part) * size,
+        owners,
+        process,
+        before,
     )
 
 
@@ -316,7 +348,6 @@
     part, part_rows, back_ref, returned_ref, feature_ref, first_row, wide_ref, buffers, sems
 ):
     lines, lanes = masks()
-    turn_copies(returned_ref, wide_ref)
     size = buffers[0].shape[0]
     chunk_rows = size // FIELDS
 
@@ -341,8 +372,22 @@
                     pl.ds(start_row, 16), lane_block * LANES : (lane_block + 1) * LANES
                 ] = jnp.concatenate(halves, axis=0).astype(BF16)
 
-    first = part * part_rows * FIELDS
-    word_stream(back_ref, buffers, sems, first, size, part_rows // chunk_rows, process)
+    first = part * back_ref.shape[0] // PARTS
+    word_stream(
+        back_ref,
+        buffers,
+        sems,
+        lambda at: first + at * size,
+        part_rows // chunk_rows,
+        process,
+        lambda: turn_copies(returned_ref, wide_ref),
+    )
+
+
+def gather_blocks(block_refs, whole_ref):
+    rows = block_refs[0].shape[0]
+    for one, block_ref in enumerate(block_refs):
+        whole_ref[one * rows : (one + 1) * rows, :] = block_ref[...]
 
 
 def unpermute_kernel(
@@ -362,6 +407,7 @@
 
 
 def dense_kernel(
+    owners,
     part_rows,
     experts,
     scale,
@@ -379,10 +425,12 @@
     *refs,
 ):
     early = refs[: PARTS - 1]
+    refs = refs[PARTS - 1 :]
+    sent_refs = refs[:owners]
     (
-        sent_ref,
         grad_dense_ref,
         grad_weight_ref,
+        grad_bias_ref,
         grad_shared_ref,
         wide_ref,
         feature_ref,
@@ -402,7 +450,8 @@
         left_ref,
         right_ref,
         sems,
-    ) = refs[PARTS - 1 :]
+        sent_ref,
+    ) = refs[owners:]
     buffers = (left_ref, right_ref)
     width = turned_ref.shape[1]
     blocks = width // LANES
@@ -551,8 +600,8 @@
             input_ref[...] += matmul(weights, half_grad)
             sums.append(matmul_nt(ones, half_grad)[0:1])
         sums.append(matmul_nt(ones, output_grad)[0:1])
-        sums.append(jnp.zeros((BIAS_ROWS - 3, LANES), F32))
-        put_weight(expert, slice(2 * D_IN + H1, WEIGHT_ROWS), jnp.concatenate(sums, axis=0))
+        sums.append(jnp.zeros((8 - 3, LANES), F32))
+        grad_bias_ref[expert] = jnp.concatenate(sums, axis=0)
         return carry
 
     lax.fori_loop(0, experts, backward, 0, unroll=2)
@@ -584,7 +633,6 @@
         wide_ref[pl.ds(aligned(8 + step * LANES, 8), LANES), :] = jnp.zeros((LANES, LANES), F32)
         return carry
 
-    lax.fori_loop(0, slot_blocks, clear, 0)
     chunk_rows = left_ref.shape[0] // FIELDS
 
     def permute(chunk, words):
@@ -606,8 +654,19 @@
                     start = words[(step * 8 + k) * FIELDS + field]
                     pltpu.store(wide_ref.at[pl.ds(start, 8), :], tile, mask=lines[k])
 
+    def permute_place(at):
+        each = part_rows // chunk_rows
+        part = lax.div(at, each)
+        return part * (out_ref.shape[0] // PARTS) + (at - part * each) * (chunk_rows * FIELDS)
+
     word_stream(
-        out_ref, buffers, sems, 0, chunk_rows * FIELDS, width // chunk_rows, permute
+        out_ref,
+        buffers,
+        sems,
+        permute_place,
+        width // chunk_rows,
+        permute,
+        lambda: lax.fori_loop(0, slot_blocks, clear, 0, unroll=2),
     )
 
     def merge(block, carry):
@@ -623,25 +682,25 @@
         return carry
 
     lax.fori_loop(0, slot_blocks, merge, 0, unroll=4 if slot_blocks % 4 == 0 else 1)
-
-
-def add_kernel(
-    packed,
-    table_lanes,
-    core_ref,
-    request_ref,
-    asked_ref,
-    received_ref,
-    total_ref,
-    left_grad_ref,
-    right_grad_ref,
-    left_ref,
-    right_ref,
-    sems,
-    *sums,
-):
+    each = sent_ref.shape[0] // owners
+    for one in range(owners):
+        sent_refs[one][...] = sent_ref[one * each : (one + 1) * each, :]
+
+
+def add_kernel(owners, packed, table_lanes, index_ref, request_ref, asked_ref, *refs):
+    received_refs = refs[:owners]
+    table_refs = refs[owners : owners + 2 * TABLE_CHUNKS]
+    (
+        received_ref,
+        left_grad_ref,
+        right_grad_ref,
+        left_ref,
+        right_ref,
+        sems,
+        *sums,
+    ) = refs[owners + 2 * TABLE_CHUNKS :]
     rows = sums[0].shape[0] - 16
-    core = core_ref[0]
+    core, batch = index_ref[0], index_ref[1]
     sources = received_ref.shape[0] // packed
     chunks = packed // 16
     lines, _ = masks()
@@ -659,41 +718,55 @@
         wanted = group * EMB + (to_lane & (EMB - 1))
         spread_grads.append(jnp.where(from_lane == wanted, 1.0, 0.0).astype(BF16))
 
+    def place(source):
+        distance = lax.div(source, PARTS)
+        return (distance ^ batch) * PARTS + source - distance * PARTS
+
     def spread(source, grad_ref):
-        asked = asked_ref[pl.ds(source * chunks, chunks), :]
-        names = (own_group - lax.shift_right_logical(asked, table_lanes)) & (GROUPS - 1)
-        names = names.astype(F32)
-        for first in range(0, chunks, 8):
-            count = min(8, chunks - first)
-            held = slot_lines(names[first : first + count])
+        def step(first, count, pair):
+            asked = asked_ref[pl.ds(place(source) * chunks + first, count), :]
+            names = (own_group - lax.shift_right_logical(asked, table_lanes)) & (GROUPS - 1)
             start = aligned(source * packed + first * 16, 16)
             grads = received_ref[pl.ds(start, count * 16), :]
             lane_group = lax.shift_right_logical(iota((count * 16, LANES), 1), 4).astype(F32)
-            for pair in range(GROUPS // 2):
-                wide_names = matmul(held, spread_names[pair])
-                wide_grads = matmul(grads, spread_grads[pair])
-                for side in range(2):
-                    half = slice(side * LANES, (side + 1) * LANES)
-                    masked = jnp.where(wide_names[:, half] == lane_group, wide_grads[:, half], 0.0)
-                    for chunk in range(count):
-                        start = (first + chunk) * LANES + (pair * 2 + side) * 16
-                        grad_ref[start : start + 16, :] = masked[chunk * 16 : (chunk + 1) * 16]
+            wide_names = matmul(slot_lines(names.astype(F32)), spread_names[pair])
+            wide_grads = matmul(grads, spread_grads[pair])
+            for side in range(2):
+                half = slice(side * LANES, (side + 1) * LANES)
+                masked = jnp.where(wide_names[:, half] == lane_group, wide_grads[:, half], 0.0)
+                for chunk in range(count):
+                    start = (first + chunk) * LANES + (pair * 2 + side) * 16
+                    grad_ref[start : start + 16, :] = masked[chunk * 16 : (chunk + 1) * 16]
+
+        return [
+            functools.partial(step, first, min(4, chunks - first), pair)
+            for first in range(0, chunks, 4)
+            for pair in range(GROUPS // 2)
+        ]
 
     def clear(step, carry):
-        start = aligned(step * 16, 16)
         for total in sums:
-            total[pl.ds(start, 16), :] = jnp.zeros((16, LANES), F32)
+            total[pl.ds(aligned(8 + step * LANES, 8), LANES), :] = jnp.zeros((LANES, LANES), F32)
         return carry
 
-    lax.fori_loop(0, (rows + 16) // 16, clear, 0)
-    spread(0, left_grad_ref)
+    def before():
+        for total in sums:
+            total[0:8, :] = jnp.zeros((8, LANES), F32)
+            total[8 + rows : 16 + rows, :] = jnp.zeros((8, LANES), F32)
+        lax.fori_loop(0, rows // LANES, clear, 0)
+        gather_blocks(received_refs, received_ref)
+        for one in spread(0, left_grad_ref):
+            one()
 
     def process(source, words):
         now, later = left_grad_ref, right_grad_ref
         if words is right_ref:
             now, later = later, now
-        spread(jnp.minimum(source + 1, sources - 1), later)
-        for row in range(GROUPS * packed // 8):
+        steps = spread(jnp.minimum(source + 1, sources - 1), later)
+        rows = GROUPS * packed // 8
+        for row in range(rows):
+            if row * len(steps) // rows != (row - 1) * len(steps) // rows:
+                steps[row * len(steps) // rows]()
             grads = now[row * 8 : (row + 1) * 8, :]
             for k in range(8):
                 place = pl.ds(words[row * 8 + k], 8)
@@ -701,24 +774,37 @@
                 pltpu.store(total.at[place, :], total[place, :] + grads, mask=lines[k])
 
     size = GROUPS * packed
-    word_stream(request_ref, (left_ref, right_ref), sems, 0, size, sources, process)
-
-    def finish(block, carry):
+    word_stream(
+        request_ref,
+        (left_ref, right_ref),
+        sems,
+        lambda at: place(at) * size,
+        sources,
+        process,
+        before,
+    )
+
+    def finish(kept, block, carry):
         start = aligned(8 + block * LANES, 8)
         total = functools.reduce(jnp.add, [one[pl.ds(start, LANES), :] for one in sums])
         turned = matmul_nt(eye, total.astype(BF16)).astype(BF16)
+        each = GROUPS // (2 * TABLE_CHUNKS)
         for group in range(GROUPS):
             half, column = divmod(group, GROUPS // 2)
+            chunk, column = divmod(column, each)
+            table_ref = table_refs[chunk + (0 if half == kept else TABLE_CHUNKS)]
             column = aligned(column * rows + block * LANES, LANES)
-            total_ref[half ^ core, :, pl.ds(column, LANES)] = turned[
-                group * EMB : (group + 1) * EMB
-            ]
+            table_ref[:, pl.ds(column, LANES)] = turned[group * EMB : (group + 1) * EMB]
         return carry
 
-    lax.fori_loop(0, rows // LANES, finish, 0, unroll=8)
-
-
-def unpack_kernel(weight_piece, shared_piece, pairs, piece_ref, *refs):
+    for kept in range(2):
+
+        @pl.when(core == kept)
+        def _():
+            lax.fori_loop(0, rows // LANES, functools.partial(finish, kept), 0, unroll=8)
+
+
+def unpack_kernel(weight_piece, extra_piece, pairs, piece_ref, *refs):
     (
         dense_w_ref,
         gate_ref,
@@ -731,33 +817,36 @@
         head_w_ref,
         head_b_ref,
         weight_ref,
-        shared_ref,
+        extra_ref,
     ) = refs
     for owner in range(piece_ref.shape[0]):
         weight_ref[owner * weight_piece : (owner + 1) * weight_piece, :] = piece_ref[
             owner, :weight_piece, :
         ].astype(F32)
-        high = piece_ref[owner, weight_piece : weight_piece + shared_piece, :].astype(F32)
-        low = piece_ref[owner, weight_piece + shared_piece :, :].astype(F32)
-        shared_ref[owner * shared_piece : (owner + 1) * shared_piece, :] = high + low
-    bias = 2 * D_IN + H1
+        high = piece_ref[owner, weight_piece : weight_piece + extra_piece, :].astype(F32)
+        low = piece_ref[owner, weight_piece + extra_piece :, :].astype(F32)
+        extra_ref[owner * extra_piece : (owner + 1) * extra_piece, :] = high + low
+    gate_rows = D_IN // LANES * pairs
+    small = H2 + gate_rows + 16
+
+    def small_line(row):
+        return extra_ref[small + row : small + row + 1, :] + extra_ref[small + 6 + row : small + 7 + row, :]
+
     for half in range(H1 // LANES):
         span = slice(half * LANES, (half + 1) * LANES)
         hidden_w_ref[0, :, span] = weight_ref[half * D_IN : (half + 1) * D_IN, :]
-        hidden_b_ref[:, span] = weight_ref[bias + half : bias + half + 1, :]
-    output_w_ref[0] = weight_ref[2 * D_IN : bias, :]
-    output_b_ref[...] = weight_ref[bias + 2 : bias + 3, :]
-    tower_w_ref[...] = shared_ref[:H2, :]
-    head_w_ref[...] = shared_ref[H2 : H2 + 1, :]
-    tower_b_ref[...] = shared_ref[H2 + 8 : H2 + 9, :]
-    head_b_ref[...] = shared_ref[H2 + 16 : H2 + 17, :TASKS]
-    gate_base = H2 + 24
+        hidden_b_ref[:, span] = small_line(3 + half)
+    output_w_ref[0] = weight_ref[2 * D_IN : GRAD_ROWS, :]
+    output_b_ref[...] = small_line(5)
+    tower_w_ref[...] = extra_ref[:H2, :]
+    head_w_ref[...] = small_line(0)
+    tower_b_ref[...] = small_line(1)
+    head_b_ref[...] = small_line(2)[:, :TASKS]
     for block in range(D_IN // LANES):
-        gate_ref[:, block * LANES : (block + 1) * LANES] = shared_ref[
-            gate_base + block * pairs : gate_base + (block + 1) * pairs, :
+        gate_ref[:, block * LANES : (block + 1) * LANES] = extra_ref[
+            H2 + block * pairs : H2 + (block + 1) * pairs, :
         ]
-    dense_base = gate_base + D_IN // LANES * pairs
-    dense_w_ref[...] = shared_ref[dense_base : dense_base + DENSE, :BOTTOM]
+    dense_w_ref[...] = extra_ref[H2 + gate_rows : H2 + gate_rows + DENSE, :BOTTOM]
 
 
 SMEM = pl.BlockSpec(memory_space=pltpu.SMEM)
@@ -765,7 +854,7 @@
 ANY = pl.BlockSpec(memory_space=pl.ANY)
 
 
-def call(kernel, outs, ins, scratch, name, micros):
+def call(kernel, outs, ins, scratch, name, micros, vmem=16):
     return pl.pallas_call(
         kernel,
         out_shape=outs,
@@ -776,7 +865,7 @@
         cost_estimate=pl.CostEstimate(
             flops=int(micros * 1.15e9), bytes_accessed=int(micros * 3e6), transcendentals=0
         ),
-        compiler_params=pltpu.CompilerParams(vmem_limit_bytes=VMEM_BYTES),
+        compiler_params=pltpu.CompilerParams(vmem_limit_bytes=vmem << 20),
     )
 
 
@@ -814,26 +903,37 @@
     slots = owners * PARTS * GROUPS * packed
     part_slots = owners * packed
     lookup_rows = lookups // LANES
-    list_rows = -(-lookup_rows // 16) * 16
+    list_part = -(-lookup_rows // (PARTS * 24)) * 24
+    list_rows = list_part * PARTS
 
     def tie(*values):
         return lax.optimization_barrier(values)
 
     def exchange(values, axis):
         return lax.all_to_all(values, axis, split_axis=0, concat_axis=0, tiled=True)
+
+    def swap(values, axis, bits):
+        size = lax.axis_size(axis)
+        return lax.ppermute(values, axis, [(one, one ^ bits) for one in range(size)])
+
+    def swap_all(blocks):
+        order = sorted(range(1, owners), key=lambda bits: (-bits.bit_length(), bits))
+        moved = {bits: swap(blocks[bits], "batch", bits) for bits in order}
+        return [blocks[0]] + [moved[bits] for bits in range(1, owners)]
 
     owner_list = row_owner.reshape(lookup_rows, LANES)
     local_list = local_row.reshape(lookup_rows, LANES)
     slot_rows = slots // LANES
     list_shape = jax.ShapeDtypeStruct((list_rows, LANES), I32)
+    batch_index = lax.axis_index("batch").reshape(1)
     requests, back, out = call(
         functools.partial(route_kernel, owners, part_lookups, packed, table_lanes),
         (jax.ShapeDtypeStruct((slot_rows, LANES), I32), list_shape, list_shape),
-        [VMEM, VMEM],
-        [pltpu.VMEM((list_rows, LANES), I32)] * 3 + [pltpu.VMEM((slot_rows, 2 * LANES), F32)],
+        [SMEM, VMEM, VMEM],
+        [pltpu.VMEM((list_rows, LANES), I32)] * 3 + [pltpu.VMEM((PARTS, slot_rows // PARTS, 2 * LANES), F32)],
         "route",
         9,
-    )(owner_list, local_list)
+    )(batch_index, owner_list, local_list)
     asked = exchange(requests.reshape(owners, slots // owners), "batch")
     asked = asked.reshape(slot_rows, LANES)
     offset = 8 - (jnp.arange(LANES, dtype=I32) & 7)
@@ -841,10 +941,11 @@
     back = back.reshape(-1)
     out = out.reshape(-1)
 
+    hidden_b, out = tie(hidden_b, out)
     table, weights = call(
         pack_kernel,
         (
-            jax.ShapeDtypeStruct((table_packed + 16, LANES), F32),
+            pltpu.VMEM((table_packed + 16, LANES), F32),
             jax.ShapeDtypeStruct((WEIGHT_ROWS, LANES), BF16),
         ),
         [VMEM] * 5,
@@ -852,6 +953,7 @@
         "pack",
         5,
     )(emb_table.T, hidden_w, output_w, hidden_b, output_b)
+    table = pltpu.with_memory_space_constraint(table, pltpu.VMEM)
     weights = lax.all_gather(weights, "expert", axis=0, tiled=False)
 
     slot_words = [pltpu.SMEM((GROUPS * packed,), I32)] * 2 + [pltpu.SemaphoreType.DMA((2,))]
@@ -862,7 +964,11 @@
             functools.partial(fetch_kernel, owners, part, packed, table_lanes),
             jax.ShapeDtypeStruct((part_slots, LANES), BF16),
             [ANY, VMEM, VMEM],
-            [pltpu.VMEM((part_slots, LANES), F32)] + slot_words,
+            [
+                pltpu.VMEM((part_slots, LANES), F32),
+                pltpu.VMEM((GROUPS * packed, LANES), F32),
+            ]
+            + slot_words,
             "fetch",
             24 // PARTS,
         )(words, asked, table)
@@ -884,15 +990,16 @@
     pairs = TASKS * experts
     shared_rows = H2 + 24 + D_IN // LANES * pairs + 16
     vectors = jnp.stack([tower_b, head_w])
-    sent, grad_dense, grad_weight, grad_shared = call(
-        functools.partial(dense_kernel, part_rows, experts, scale),
+    *sent, grad_dense, grad_weight, grad_bias, grad_shared = call(
+        functools.partial(dense_kernel, owners, part_rows, experts, scale),
         (
-            jax.ShapeDtypeStruct((PARTS * part_slots, LANES), BF16),
+            *[jax.ShapeDtypeStruct((PARTS * packed, LANES), BF16)] * owners,
             jax.ShapeDtypeStruct((DENSE, row_total), F32),
-            jax.ShapeDtypeStruct((experts, WEIGHT_ROWS, LANES), BF16),
+            jax.ShapeDtypeStruct((experts, GRAD_ROWS, LANES), BF16),
+            jax.ShapeDtypeStruct((experts, 8, LANES), F32),
             jax.ShapeDtypeStruct((shared_rows, LANES), F32),
         ),
-        [ANY, ANY] + [VMEM] * 7 + [SMEM, VMEM] + [VMEM] * (PARTS - 1),
+        [ANY, ANY] + [VMEM] * 7 + [SMEM] + [VMEM] * PARTS,
         [
             pltpu.VMEM((slots + 16, LANES), F32),
             pltpu.VMEM((row_total, D_IN), BF16),
@@ -910,9 +1017,11 @@
             pltpu.VMEM((D_IN, row_total), BF16),
             pltpu.VMEM((FIELDS, LANES, LANES), F32),
             *row_words,
+            pltpu.VMEM((PARTS * part_slots, LANES), BF16),
         ],
         "dense",
         45,
+        56,
     )(
         back,
         out,
@@ -927,70 +1036,72 @@
         labels,
         *early,
     )
-    received = exchange(sent.reshape(owners, PARTS * packed, LANES), "batch")
-    received = received.reshape(PARTS * part_slots, LANES)
+    received = swap_all(sent)
 
     def split(values):
         high = lax.reduce_precision(values, exponent_bits=8, mantissa_bits=7)
         return high.astype(BF16), (values - high).astype(BF16)
 
-    weight_piece = -(-WEIGHT_ROWS // (16 * owners)) * 16
-    shared_piece = -(-shared_rows // (16 * owners)) * 16
-    piece_rows = weight_piece + 2 * shared_piece
-    weight = jnp.pad(
-        grad_weight, ((0, 0), (0, weight_piece * owners - WEIGHT_ROWS), (0, 0))
-    ).reshape(experts, owners, weight_piece, LANES)
-    shared = jnp.pad(grad_shared, ((0, shared_piece * owners - shared_rows), (0, 0)))
+    received[1], grad_weight, grad_bias, grad_shared = tie(
+        received[1], grad_weight, grad_bias, grad_shared
+    )
+
+    def spread_rows(values, piece):
+        rows = values.shape[1]
+        values = jnp.pad(values, ((0, 0), (0, piece * owners - rows), (0, 0)))
+        return values.reshape(experts, owners, piece, LANES).transpose(1, 0, 2, 3)
+
+    large = jnp.concatenate([grad_shared[:H2], grad_shared[H2 + 24 :]], axis=0).astype(BF16)
+    small = jnp.concatenate([grad_shared[H2 + 8 * row : H2 + 8 * row + 1] for row in range(3)])
+    small = jnp.concatenate(
+        [jnp.broadcast_to(small[None], (experts, 3, LANES)), grad_bias[:, :3]], axis=1
+    )
+    extra = jnp.concatenate(
+        [jnp.broadcast_to(large[None], (experts, *large.shape)), *split(small)], axis=1
+    )
+    weight_piece = -(-GRAD_ROWS // (16 * owners)) * 16
+    extra_piece = -(-extra.shape[1] // (16 * owners)) * 16
+    piece_rows = weight_piece + extra_piece
     pieces = jnp.concatenate(
-        [weight.transpose(1, 0, 2, 3)]
-        + [
-            jnp.broadcast_to(
-                one.reshape(owners, 1, shared_piece, LANES), (owners, experts, shared_piece, LANES)
-            )
-            for one in split(shared)
-        ],
-        axis=2,
-    )
-    received, pieces = tie(received, pieces)
+        [spread_rows(grad_weight, weight_piece), spread_rows(extra, extra_piece)], axis=2
+    )
+    late = owners - 2
+    *received[:late], pieces = tie(*received[:late], pieces)
     pieces = exchange(pieces.reshape(owners * experts, piece_rows, LANES), ("batch", "expert"))
 
+    columns = table_rows // 2 // TABLE_CHUNKS
     table_part = call(
-        functools.partial(add_kernel, packed, table_lanes),
-        jax.ShapeDtypeStruct((2, EMB, table_rows // 2), BF16),
-        [SMEM, ANY, VMEM, VMEM],
-        [pltpu.VMEM((GROUPS * packed, LANES), F32)] * 2
+        functools.partial(add_kernel, owners, packed, table_lanes),
+        (jax.ShapeDtypeStruct((EMB, columns), BF16),) * (2 * TABLE_CHUNKS),
+        [SMEM, ANY, VMEM] + [VMEM] * owners,
+        [pltpu.VMEM((PARTS * part_slots, LANES), BF16)]
+        + [pltpu.VMEM((GROUPS * packed, LANES), F32)] * 2
         + slot_words
         + [pltpu.VMEM((table_packed + 16, LANES), F32)] * STREAMS,
         "add",
         60,
-    )(core.reshape(1), words, asked, received)
-
-    table_part, pieces = tie(table_part, pieces)
-    def swap(values, axis, bits):
-        size = lax.axis_size(axis)
-        return lax.ppermute(values, axis, [(one, one ^ bits) for one in range(size)])
+        48,
+    )(jnp.concatenate([core.reshape(1), batch_index]), words, asked, *received)
 
     def add_low(left, right):
         return (left.astype(F32) + right.astype(F32)).astype(BF16)
 
-    chunks = 2
-    columns = table_rows // 2 // chunks
-    kept = []
-    for chunk in range(chunks):
-        cut = slice(chunk * columns, (chunk + 1) * columns)
-        kept.append(add_low(table_part[0, :, cut], swap(table_part[1, :, cut], "expert", 1)))
+    *table_part, pieces = tie(*table_part, pieces)
+    kept = [
+        add_low(one, swap(other, "expert", 1))
+        for one, other in zip(table_part[:TABLE_CHUNKS], table_part[TABLE_CHUNKS:])
+    ]
     sums = jnp.sum(pieces.astype(F32), axis=0)
-    shared = sums[weight_piece : weight_piece + shared_piece] + sums[weight_piece + shared_piece :]
-    piece = jnp.concatenate([sums[:weight_piece].astype(BF16), *split(shared)], axis=0)
+    piece = jnp.concatenate([sums[:weight_piece].astype(BF16), *split(sums[weight_piece:])], axis=0)
     *kept, piece = tie(*kept, piece)
-    pieces = exchange(jnp.broadcast_to(piece[None], (owners, piece_rows, LANES)), "batch")
+    pieces = exchange(jnp.broadcast_to(piece[None], (owners, *piece.shape)), "batch")
 
     bit = 2
     while bit < experts:
         kept = [add_low(one, swap(one, "expert", bit)) for one in kept]
         bit *= 2
     small = call(
-        functools.partial(unpack_kernel, weight_piece, shared_piece, pairs),
+        functools.partial(unpack_kernel, weight_piece, extra_piece, pairs),
         tuple(
             jax.ShapeDtypeStruct(shape, F32)
             for shape in (
@@ -1009,13 +1120,13 @@
         [VMEM],
         [
             pltpu.VMEM((owners * weight_piece, LANES), F32),
-            pltpu.VMEM((owners * shared_piece, LANES), F32),
+            pltpu.VMEM((owners * extra_piece, LANES), F32),
         ],
         "unpack",
         3,
     )(pieces)
-    *kept, small = tie(*kept, small)
     others = [swap(one, "expert", 1) for one in kept]
+    *others, small = tie(*others, small)
     lower = [jnp.where(core == 0, one, other) for one, other in zip(kept, others)]
     upper = [jnp.where(core == 0, other, one) for one, other in zip(kept, others)]
     table_total = jnp.concatenate(lower + upper, axis=1).astype(F32).T

time: 261 us -> 235 us (0.900)
  Pallas kernels: 145 us -> 121 us
  waiting for transfers between devices: 55.1 us -> 37.4 us
  local copies, waits for them, and re-layouts: 4.94 us -> 12.5 us
  starting transfers between devices: 32.8 us -> 39.6 us
    all_to_all x6 -> x5, waiting for transfers between devices: 32.6 us -> 7.3 us  [exchange(): return lax.all_to_all(values, axis, split_axis=0, concat_axis=0, tiled=True)]
    ppermute x6 -> x13, starting transfers between devices: 2.8 us -> 14.3 us  [swap(): lax.ppermute(values, axis, [(one, one ^ bits) for one in range(size)])]
    pallas_call x2, Pallas kernels: 37 us -> 26.7 us  [shards(): call(functools.partial(fetch_kernel, owners, part, packed, table_lanes),...]
    pallas_call x4, Pallas kernels: 88 us -> 79.8 us  [the longest x1 39.4 us: shards(): call(functools.partial(add_kernel, owners, packed, table_lanes), (jax.Sha...]
    ppermute x6 -> x13, waiting for transfers between devices: 22.5 us -> 30.1 us  [swap(): lax.ppermute(values, axis, [(one, one ^ bits) for one in range(size)])]
    unnamed x20 -> x34, local copies, waits for them, and re-layouts: 2.38 us -> 8.81 us
    all_to_all x6 -> x5, starting transfers between devices: 30 us -> 25.3 us  [exchange(): return lax.all_to_all(values, axis, split_axis=0, concat_axis=0, tiled=True)]
  transfers between devices with their start and end apart: 13 -> 19, of which waited for: 10 -> 8; matrix products, arithmetic and copies ran while one was open for 2% -> 4% of each run, Pallas kernels for 37% -> 33%
where the time goes in v2:
time: 235 us; the launch traced here: 234 us
  Pallas kernels  121 us (51%)
  starting transfers between devices  39.6 us (17%)
  waiting for transfers between devices  37.4 us (16%)
  between operations  14.4 us (6%)
  local copies, waits for them, and re-layouts  12.5 us (5%)
  other arithmetic  8.71 us (4%)
    pallas_call x1, Pallas kernels, shards(): call(functools.partial(add_kernel, owners, packed, table_lanes), (jax.Sha...  39.4 us
    pallas_call x1, Pallas kernels, shards(): call(functools.partial(dense_kernel, owners, part_rows, experts, scale),...  36.5 us
    ppermute x13, waiting for transfers between devices, swap(): lax.ppermute(values, axis, [(one, one ^ bits) for one in range(size)])  30.1 us
    pallas_call x2, Pallas kernels, shards(): call(functools.partial(fetch_kernel, owners, part, packed, table_lanes),...  26.7 us
    all_to_all x5, starting transfers between devices, exchange(): return lax.all_to_all(values, axis, split_axis=0, concat_axis=0, tiled=True)  25.3 us
    ppermute x13, starting transfers between devices, swap(): lax.ppermute(values, axis, [(one, one ^ bits) for one in range(size)])  14.3 us
    unnamed x34, local copies, waits for them, and re-layouts  8.81 us
    pallas_call x1, Pallas kernels, shards(): call(functools.partial(unpermute_kernel, part, part_rows), jax.ShapeDtype...  7.58 us
  transfers between devices with their start and end apart: 19, of which 8 were waited for; matrix products, arithmetic and copies ran while one was open for 4% of the time, Pallas kernels for 33%

profile of v2, /device:TPU:0, one launch (start us, length us, event | category | flops | bytes accessed | tf_op | source)
XLA Modules:
  0.0 234.1 jit_solution(6230510538322867091)
XLA Ops:
  9.1 7.4 %route.1 = (s32[272,128]{1,0:T(8,128)}, s32[144,128]{1,0:T(8,128)S(1)}, s32[144,128]{1,0:T(8,128)S(1)}) custom-call(s32[1]{0:T(128)} %bitcast.1.batch_ref, s32[130,128]{1,0:T(8,128)S(1)} %bitcast.38, s32[130,128]{1,0:T(8,128)S(1)} %bitcast.40), custom_call_target="tpu_custom_call" | custom-call | flops 10350000128 | bytes 27000000 | tf_op jit(solution)/shard_map/route/pallas_call | solution.py:929
  16.6 7.3 %all-to-all-start = ((s32[8,1,4352]{2,1,0:T(1,128)}), s32[8,1,4352]{2,1,0:T(1,128)S(1)}, u32[]{:S(2)}, u32[]{:S(2)}) async-start(s32[8,1,4352]{2,1,0:T(1,128)} %bitcast.3), calls=%async_computation | async-start | bytes 278528 | tf_op jit(solution)/shard_map/all_to_all | solution.py:913
  23.9 3.1 %pack.1 = (f32[8208,128]{1,0:T(8,128)S(1)}, bf16[1296,128]{1,0:T(8,128)(2,1)}) custom-call(bf16[16,65536]{1,0:T(8,128)(2,1)S(1)} %bitcast.39, bf16[1,512,256]{2,1,0:T(8,128)(2,1)S(1)} %copy-done.1, bf16[1,256,128]{2,1,0:T(8,128)(2,1)S(1)} %copy-done.3, f32[1,256]{1,0:T(1,128)S(1)} %copy-done.4, f32[1,128]{1,0:T(1,128)S(1)} %copy-done.5), custom_call_target="tpu_custom_call" | custom-call | flops 5750000128 | bytes 15000000 | tf_op jit(solution)/shard_map/pack/pallas_call | solution.py:945
  27.0 2.0 copy-done.8
  31.4 2.2 copy-done.9
  33.6 13.3 %fetch.3 = bf16[2176,128]{1,0:T(8,128)(2,1)} custom-call(s32[34816]{0:T(1024)S(1)} %bitcast_add_fusion.request_ref, s32[272,128]{1,0:T(8,128)S(1)} %bitcast.35, f32[8208,128]{1,0:T(8,128)S(1)} %copy-done.9), custom_call_target="tpu_custom_call" | custom-call | flops 13799999488 | bytes 36000000 | tf_op jit(solution)/shard_map/fetch/pallas_call | solution.py:963
  46.9 4.4 %all-to-all-start.2 = ((bf16[8,272,128]{2,1,0:T(8,128)(2,1)}), bf16[8,272,128]{2,1,0:T(8,128)(2,1)S(1)}, u32[]{:S(2)}, u32[]{:S(2)}) async-start(bf16[8,272,128]{2,1,0:T(8,128)(2,1)} %bitcast.16), calls=%async_computation.2 | async-start | bytes 1114112 | tf_op jit(solution)/shard_map/all_to_all | solution.py:913
  51.3 2.2 copy-done.10
  53.4 13.3 %fetch.2 = bf16[2176,128]{1,0:T(8,128)(2,1)} custom-call(s32[34816]{0:T(1024)S(1)} %bitcast_add_fusion.request_ref, s32[272,128]{1,0:T(8,128)S(1)} %bitcast.36, f32[8208,128]{1,0:T(8,128)S(1)} %copy-done.10), custom_call_target="tpu_custom_call" | custom-call | flops 13799999488 | bytes 36000000 | tf_op jit(solution)/shard_map/fetch/pallas_call | solution.py:963
  66.8 6.0 %all-to-all-start.1 = ((bf16[8,272,128]{2,1,0:T(8,128)(2,1)}), bf16[8,272,128]{2,1,0:T(8,128)(2,1)S(1)}, u32[]{:S(2)}, u32[]{:S(2)}) async-start(bf16[8,272,128]{2,1,0:T(8,128)(2,1)} %bitcast.10), calls=%async_computation.1 | async-start | bytes 1114112 | tf_op jit(solution)/shard_map/all_to_all | solution.py:913
  72.8 7.6 %unpermute.1.refs_0_ = bf16[320,512]{1,0:T(8,128)(2,1)S(1)} custom-call(s32[18432]{0:T(1024)S(1)} %bitcast.41, bf16[2176,128]{1,0:T(8,128)(2,1)S(1)} %bitcast.34), custom_call_target="tpu_custom_call" | custom-call | flops 17250000896 | bytes 45000000 | tf_op jit(solution)/shard_map/unpermute/pallas_call | solution.py:980
  81.1 5.7 %all-to-all-done.1 = bf16[8,272,128]{2,1,0:T(8,128)(2,1)S(1)} async-done(((bf16[8,272,128]{2,1,0:T(8,128)(2,1)}), bf16[8,272,128]{2,1,0:T(8,128)(2,1)S(1)}, u32[]{:S(2)}, u32[]{:S(2)}) %all-to-all-start.1) | async-done | bytes 557088 | tf_op jit(solution)/shard_map/all_to_all | solution.py:913
  87.6 36.5 %dense.1 = (bf16[544,128]{1,0:T(8,128)(2,1)}, bf16[544,128]{1,0:T(8,128)(2,1)}, bf16[544,128]{1,0:T(8,128)(2,1)}, bf16[544,128]{1,0:T(8,128)(2,1)}, bf16[544,128...) custom-call(s32[18432]{0:T(1024)} %bitcast.42, ...), custom_call_target="tpu_custom_call" | custom-call | flops 51749998592 | bytes 135000000 | tf_op jit(solution)/shard_map/dense/pallas_call | solution.py:993
  125.7 2.0 collective-permute-start.2
  128.5 3.1 %collective-permute-start.4 = (bf16[544,128]{1,0:T(8,128)(2,1)}, bf16[544,128]{1,0:T(8,128)(2,1)S(1)}, u32[]{:S(2)}, u32[]{:S(2)}) collective-permute-start(bf16[544,128]{1,0:T(8,128)(2,1)} %get-tuple-element.92), channel_id=1, source_target_pairs={{0,20},{4,16},{8,28},{12,24},{16,4},{20,0},{24,12},{28,8},{1,21},{... | collective-permute-start | bytes 417800 | tf_op jit(solution)/shard_map/ppermute | solution.py:917
  137.0 2.4 %collective-permute-start.6 = (bf16[544,128]{1,0:T(8,128)(2,1)S(1)}, bf16[544,128]{1,0:T(8,128)(2,1)S(1)}, u32[]{:S(2)}, u32[]{:S(2)}) collective-permute-start(bf16[544,128]{1,0:T(8,128)(2,1)S(1)} %copy-done.16), channel_id=1, source_target_pairs={{0,28},{4,24},{8,20},{12,16},{16,12},{20,8},{24,4},{28,0},{1,29},{... | collective-permute-start | bytes 417800 | tf_op jit(solution)/shard_map/ppermute | solution.py:917
  140.7 6.0 %collective-permute-done.3.refs_4_ = bf16[544,128]{1,0:T(8,128)(2,1)S(1)} collective-permute-done((bf16[544,128]{1,0:T(8,128)(2,1)}, bf16[544,128]{1,0:T(8,128)(2,1)S(1)}, u32[]{:S(2)}, u32[]{:S(2)}) %collective-permute-start.3) | collective-permute-done | bytes 139296 | tf_op jit(solution)/shard_map/ppermute | solution.py:917
  146.7 3.7 %collective-permute-done.4.refs_5_ = bf16[544,128]{1,0:T(8,128)(2,1)S(1)} collective-permute-done((bf16[544,128]{1,0:T(8,128)(2,1)}, bf16[544,128]{1,0:T(8,128)(2,1)S(1)}, u32[]{:S(2)}, u32[]{:S(2)}) %collective-permute-start.4) | collective-permute-done | bytes 139296 | tf_op jit(solution)/shard_map/ppermute | solution.py:917
  150.4 3.4 %all-to-all-start.3 = ((bf16[32,192,128]{2,1,0:T(8,128)(2,1)}), bf16[32,192,128]{2,1,0:T(8,128)(2,1)}, u32[]{:S(2)}, u32[]{:S(2)}) async-start(bf16[32,192,128]{2,1,0:T(8,128)(2,1)} %bitcast.22), calls=%async_computation.3 | async-start | bytes 3145728 | tf_op jit(solution)/shard_map/all_to_all | solution.py:913
  153.9 39.4 %add.42 = (bf16[16,16384]{1,0:T(8,128)(2,1)S(1)}, bf16[16,16384]{1,0:T(8,128)(2,1)S(1)}, bf16[16,16384]{1,0:T(8,128)(2,1)S(1)}, bf16[16,16384]{1,0:T(8,128)(2,1)S(1)}) custom-call(s32[2]{0:T(128)S(1)} %pad_add_fusion.index_ref, s32[34816]{0:T(1024)S(1)} %bitcast_add_fusion.request_ref, s32[272,128]{1,0:T(8,128)S(1)} %bitcast.37, ...), custom_call_target="tpu_custom_call" | custom-call | flops 69000003584 | bytes 180000000 | tf_op jit(solution)/shard_map/add/pallas_call | solution.py:1073
  199.8 4.3 %all-to-all-start.4 = ((bf16[8,224,128]{2,1,0:T(8,128)(2,1)}), bf16[8,224,128]{2,1,0:T(8,128)(2,1)S(1)}, u32[]{:S(2)}, u32[]{:S(2)}) async-start(bf16[8,224,128]{2,1,0:T(8,128)(2,1)} %broadcast_in_dim.8), calls=%async_computation.4 | async-start | bytes 917504 | tf_op jit(solution)/shard_map/all_to_all | solution.py:913
  204.5 7.5 %collective-permute-done.9 = bf16[16,16384]{1,0:T(8,128)(2,1)S(1)} collective-permute-done((bf16[16,16384]{1,0:T(8,128)(2,1)S(1)}, bf16[16,16384]{1,0:T(8,128)(2,1)S(1)}, u32[]{:S(2)}, u32[]{:S(2)}) %collective-permute-start.9) | collective-permute-done | bytes 524320 | tf_op jit(solution)/shard_map/ppermute | solution.py:917
  212.2 10.5 %collective-permute-done.11 = bf16[16,16384]{1,0:T(8,128)(2,1)S(1)} collective-permute-done((bf16[16,16384]{1,0:T(8,128)(2,1)S(1)}, bf16[16,16384]{1,0:T(8,128)(2,1)S(1)}, u32[]{:S(2)}, u32[]{:S(2)}) %collective-permute-start.11) | collective-permute-done | bytes 524320 | tf_op jit(solution)/shard_map/ppermute | solution.py:917
  225.0 2.3 convert_bitcast_fusion
  (87 shorter events, 24.4 us)
Async XLA Ops:
  9.1 14.8 %copy-start.1 = (bf16[1,512,256]{2,1,0:T(8,128)(2,1)S(1)}, bf16[1,512,256]{2,1,0:T(8,128)(2,1)}, u32[]{:S(2)}) copy-start(bf16[1,512,256]{2,1,0:T(8,128)(2,1)} %hidden_w_ref.1) | copy-start | bytes 786436
  9.1 14.8 %copy-start.3 = (bf16[1,256,128]{2,1,0:T(8,128)(2,1)S(1)}, bf16[1,256,128]{2,1,0:T(8,128)(2,1)}, u32[]{:S(2)}) copy-start(bf16[1,256,128]{2,1,0:T(8,128)(2,1)} %output_w_ref.1) | copy-start | bytes 196612
  9.1 14.8 %copy-start.4 = (f32[1,256]{1,0:T(1,128)S(1)}, f32[1,256]{1,0:T(1,128)}, u32[]{:S(2)}) copy-start(f32[1,256]{1,0:T(1,128)} %hidden_b_ref) | copy-start | bytes 3076
  9.1 14.8 %copy-start.5 = (f32[1,128]{1,0:T(1,128)S(1)}, f32[1,128]{1,0:T(1,128)}, u32[]{:S(2)}) copy-start(f32[1,128]{1,0:T(1,128)} %output_b_ref.1) | copy-start | bytes 1540
  16.6 56.2 %copy-start.6 = (s32[144,128]{1,0:T(8,128)}, s32[144,128]{1,0:T(8,128)S(1)}, u32[]{:S(2)}) copy-start(s32[144,128]{1,0:T(8,128)S(1)} %get-tuple-element.77) | copy-start | bytes 221188
  16.6 14.7 %all-to-all-start = ((s32[8,1,4352]{2,1,0:T(1,128)}), s32[8,1,4352]{2,1,0:T(1,128)S(1)}, u32[]{:S(2)}, u32[]{:S(2)}) async-start(s32[8,1,4352]{2,1,0:T(1,128)} %bitcast.3), calls=%async_computation | async-start | bytes 278528 | tf_op jit(solution)/shard_map/all_to_all | solution.py:913
  23.8 63.0 %all-gather.3.cloned.1.call-start = ((), (), s32[]{:S(2)}) async-start(), calls=%async_computation.5 | async-start | bytes 1658880 | tf_op jit(solution)/shard_map/all_gather | solution.py:957
  46.9 19.9 %all-to-all-start.2 = ((bf16[8,272,128]{2,1,0:T(8,128)(2,1)}), bf16[8,272,128]{2,1,0:T(8,128)(2,1)S(1)}, u32[]{:S(2)}, u32[]{:S(2)}) async-start(bf16[8,272,128]{2,1,0:T(8,128)(2,1)} %bitcast.16), calls=%async_computation.2 | async-start | bytes 1114112 | tf_op jit(solution)/shard_map/all_to_all | solution.py:913
  66.8 20.0 %all-to-all-start.1 = ((bf16[8,272,128]{2,1,0:T(8,128)(2,1)}), bf16[8,272,128]{2,1,0:T(8,128)(2,1)S(1)}, u32[]{:S(2)}, u32[]{:S(2)}) async-start(bf16[8,272,128]{2,1,0:T(8,128)(2,1)} %bitcast.10), calls=%async_computation.1 | async-start | bytes 1114112 | tf_op jit(solution)/shard_map/all_to_all | solution.py:913
  124.1 7.5 %collective-permute-start = (bf16[544,128]{1,0:T(8,128)(2,1)}, bf16[544,128]{1,0:T(8,128)(2,1)S(1)}, u32[]{:S(2)}, u32[]{:S(2)}) collective-permute-start(bf16[544,128]{1,0:T(8,128)(2,1)} %get-tuple-element.84), channel_id=1, source_target_pairs={{0,4},{4,0},{8,12},{12,8},{16,20},{20,16},{24,28},{28,24},{1,5},{5... | collective-permute-start | bytes 417800 | tf_op jit(solution)/shard_map/ppermute | solution.py:917
  125.7 11.2 %collective-permute-start.1 = (bf16[544,128]{1,0:T(8,128)(2,1)}, bf16[544,128]{1,0:T(8,128)(2,1)S(1)}, u32[]{:S(2)}, u32[]{:S(2)}) collective-permute-start(bf16[544,128]{1,0:T(8,128)(2,1)} %get-tuple-element.89), channel_id=1, source_target_pairs={{0,8},{4,12},{8,0},{12,4},{16,24},{20,28},{24,16},{28,20},{1,9},{5... | collective-permute-start | bytes 417800 | tf_op jit(solution)/shard_map/ppermute | solution.py:917
  125.7 15.0 %collective-permute-start.2 = (bf16[544,128]{1,0:T(8,128)(2,1)}, bf16[544,128]{1,0:T(8,128)(2,1)S(1)}, u32[]{:S(2)}, u32[]{:S(2)}) collective-permute-start(bf16[544,128]{1,0:T(8,128)(2,1)} %get-tuple-element.90), channel_id=1, source_target_pairs={{0,12},{4,8},{8,4},{12,0},{16,28},{20,24},{24,20},{28,16},{1,13},{... | collective-permute-start | bytes 417800 | tf_op jit(solution)/shard_map/ppermute | solution.py:917
  127.7 18.9 %collective-permute-start.3 = (bf16[544,128]{1,0:T(8,128)(2,1)}, bf16[544,128]{1,0:T(8,128)(2,1)S(1)}, u32[]{:S(2)}, u32[]{:S(2)}) collective-permute-start(bf16[544,128]{1,0:T(8,128)(2,1)} %get-tuple-element.91), channel_id=1, source_target_pairs={{0,16},{4,20},{8,24},{12,28},{16,0},{20,4},{24,8},{28,12},{1,17},{... | collective-permute-start | bytes 417800 | tf_op jit(solution)/shard_map/ppermute | solution.py:917
  128.5 21.9 %collective-permute-start.4 = (bf16[544,128]{1,0:T(8,128)(2,1)}, bf16[544,128]{1,0:T(8,128)(2,1)S(1)}, u32[]{:S(2)}, u32[]{:S(2)}) collective-permute-start(bf16[544,128]{1,0:T(8,128)(2,1)} %get-tuple-element.92), channel_id=1, source_target_pairs={{0,20},{4,16},{8,28},{12,24},{16,4},{20,0},{24,12},{28,8},{1,21},{... | collective-permute-start | bytes 417800 | tf_op jit(solution)/shard_map/ppermute | solution.py:917
  131.6 22.3 %collective-permute-start.5 = (bf16[544,128]{1,0:T(8,128)(2,1)}, bf16[544,128]{1,0:T(8,128)(2,1)S(1)}, u32[]{:S(2)}, u32[]{:S(2)}) collective-permute-start(bf16[544,128]{1,0:T(8,128)(2,1)} %get-tuple-element.102), channel_id=1, source_target_pairs={{0,24},{4,28},{8,16},{12,20},{16,8},{20,12},{24,0},{28,4},{1,25},{... | collective-permute-start | bytes 417800 | tf_op jit(solution)/shard_map/ppermute | solution.py:917
  137.0 16.9 %collective-permute-start.6 = (bf16[544,128]{1,0:T(8,128)(2,1)S(1)}, bf16[544,128]{1,0:T(8,128)(2,1)S(1)}, u32[]{:S(2)}, u32[]{:S(2)}) collective-permute-start(bf16[544,128]{1,0:T(8,128)(2,1)S(1)} %copy-done.16), channel_id=1, source_target_pairs={{0,28},{4,24},{8,20},{12,16},{16,12},{20,8},{24,4},{28,0},{1,29},{... | collective-permute-start | bytes 417800 | tf_op jit(solution)/shard_map/ppermute | solution.py:917
  150.4 42.8 %all-to-all-start.3 = ((bf16[32,192,128]{2,1,0:T(8,128)(2,1)}), bf16[32,192,128]{2,1,0:T(8,128)(2,1)}, u32[]{:S(2)}, u32[]{:S(2)}) async-start(bf16[32,192,128]{2,1,0:T(8,128)(2,1)} %bitcast.22), calls=%async_computation.3 | async-start | bytes 3145728 | tf_op jit(solution)/shard_map/all_to_all | solution.py:913
  193.2 2.3 collective-permute-start.7
  195.0 2.1 collective-permute-start.8
  197.2 14.8 %collective-permute-start.9 = (bf16[16,16384]{1,0:T(8,128)(2,1)S(1)}, bf16[16,16384]{1,0:T(8,128)(2,1)S(1)}, u32[]{:S(2)}, u32[]{:S(2)}) collective-permute-start(bf16[16,16384]{1,0:T(8,128)(2,1)S(1)} %add_convert_fusion.3), channel_id=1, source_target_pairs={{0,2},{1,3},{2,0},{3,1},{4,6},{5,7},{6,4},{7,5},{8,10},{9,11},{10,... | collective-permute-start | bytes 1572872 | tf_op jit(solution)/shard_map/ppermute | solution.py:917
  199.8 23.1 %all-to-all-start.4 = ((bf16[8,224,128]{2,1,0:T(8,128)(2,1)}), bf16[8,224,128]{2,1,0:T(8,128)(2,1)S(1)}, u32[]{:S(2)}, u32[]{:S(2)}) async-start(bf16[8,224,128]{2,1,0:T(8,128)(2,1)} %broadcast_in_dim.8), calls=%async_computation.4 | async-start | bytes 917504 | tf_op jit(solution)/shard_map/all_to_all | solution.py:913
  204.1 18.6 %collective-permute-start.11 = (bf16[16,16384]{1,0:T(8,128)(2,1)S(1)}, bf16[16,16384]{1,0:T(8,128)(2,1)S(1)}, u32[]{:S(2)}, u32[]{:S(2)}) collective-permute-start(bf16[16,16384]{1,0:T(8,128)(2,1)S(1)} %add_convert_fusion.2), channel_id=1, source_target_pairs={{0,2},{1,3},{2,0},{3,1},{4,6},{5,7},{6,4},{7,5},{8,10},{9,11},{10,... | collective-permute-start | bytes 1572872 | tf_op jit(solution)/shard_map/ppermute | solution.py:917
  212.1 11.7 %collective-permute-start.10 = (bf16[16,16384]{1,0:T(8,128)(2,1)S(1)}, bf16[16,16384]{1,0:T(8,128)(2,1)S(1)}, u32[]{:S(2)}, u32[]{:S(2)}) collective-permute-start(bf16[16,16384]{1,0:T(8,128)(2,1)S(1)} %add_convert_fusion.1), channel_id=1, source_target_pairs={{0,1},{1,0},{2,3},{3,2},{4,5},{5,4},{6,7},{7,6},{8,9},{9,8},{10,11... | collective-permute-start | bytes 1572872 | tf_op jit(solution)/shard_map/ppermute | solution.py:917
  222.8 2.0 collective-permute-start.12
  (12 other events, 70.3 us)
Sparse Core Ops, SparseCore 0:
  29.1 19.6 all-gather.2

commit v3 on v2

--- a/solution.py
+++ b/solution.py
@@ -76,7 +76,11 @@
     for part in range(PARTS):
         lines = slice(part * part_rows, part * part_rows + filled)
         taken = slice(part * filled, (part + 1) * filled)
-        high_ref[lines, :] = owner_ref[taken, :]
+        for line in range(filled):
+            start = (part * filled + line) * LANES
+            high_ref[part * part_rows + line : part * part_rows + line + 1, :] = owner_ref[
+                :, start : start + LANES
+            ]
         low_ref[lines, :] = local_ref[taken, :]
     owner = high_ref[...]
     local = low_ref[...]
@@ -407,7 +411,7 @@
 
 
 def dense_kernel(
-    owners,
+    order,
     part_rows,
     experts,
     scale,
@@ -426,6 +430,7 @@
 ):
     early = refs[: PARTS - 1]
     refs = refs[PARTS - 1 :]
+    owners = len(order)
     sent_refs = refs[:owners]
     (
         grad_dense_ref,
@@ -507,18 +512,23 @@
         tall = jnp.transpose(jnp.broadcast_to(line, (LANES, LANES)))
         return jnp.concatenate([tall] * blocks, axis=1)
 
+    def hidden_weights(expert):
+        return jnp.concatenate(
+            [weight_ref[expert, half * D_IN : (half + 1) * D_IN, :] for half in range(2)], axis=1
+        )
+
     def bias_line(expert, rows):
         lines = [weight_ref[expert, 2 * D_IN + H1 :, :].astype(F32)[row : row + 1] for row in rows]
         return functools.reduce(jnp.add, lines)
 
     def forward(expert, carry):
         turned = turned_ref[...]
-        for half in range(H1 // LANES):
-            weights = weight_ref[expert, half * D_IN : (half + 1) * D_IN, :]
-            bias = column(bias_line(expert, range(half * 3, half * 3 + 3)))
-            value, slope = silu_parts(matmul_tn(weights, turned) + bias)
-            hidden_ref[expert, half * LANES : (half + 1) * LANES, :] = value.astype(BF16)
-            hidden_slope_ref[expert, half * LANES : (half + 1) * LANES, :] = slope
+        bias = jnp.concatenate(
+            [column(bias_line(expert, range(half * 3, half * 3 + 3))) for half in range(2)], axis=0
+        )
+        value, slope = silu_parts(matmul_tn(hidden_weights(expert), turned) + bias)
+        hidden_ref[expert] = value.astype(BF16)
+        hidden_slope_ref[expert] = slope
         weights = weight_ref[expert, 2 * D_IN : 2 * D_IN + H1, :]
         bias = column(bias_line(expert, (6, 7, 8)))
         value, slope = silu_parts(matmul_tn(weights, hidden_ref[expert]) + bias)
@@ -589,16 +599,16 @@
         put_weight(expert, slice(2 * D_IN, 2 * D_IN + H1), matmul_nt(hidden, output_grad))
         weights = weight_ref[expert, 2 * D_IN : 2 * D_IN + H1, :]
         hidden_grad = (matmul(weights, output_grad) * hidden_slope_ref[expert]).astype(BF16)
-        turned = turned_ref[...]
-        sums = []
-        for half in range(H1 // LANES):
-            half_grad = hidden_grad[half * LANES : (half + 1) * LANES]
+        weight_grad = matmul_nt(turned_ref[...], hidden_grad)
+        for half in range(2):
             put_weight(
-                expert, slice(half * D_IN, (half + 1) * D_IN), matmul_nt(turned, half_grad)
+                expert,
+                slice(half * D_IN, (half + 1) * D_IN),
+                weight_grad[:, half * LANES : (half + 1) * LANES],
             )
-            weights = weight_ref[expert, half * D_IN : (half + 1) * D_IN, :]
-            input_ref[...] += matmul(weights, half_grad)
-            sums.append(matmul_nt(ones, half_grad)[0:1])
+        input_ref[...] += matmul(hidden_weights(expert), hidden_grad)
+        hidden_sum = matmul_nt(ones, hidden_grad)[0:1]
+        sums = [hidden_sum[:, half * LANES : (half + 1) * LANES] for half in range(2)]
         sums.append(matmul_nt(ones, output_grad)[0:1])
         sums.append(jnp.zeros((8 - 3, LANES), F32))
         grad_bias_ref[expert] = jnp.concatenate(sums, axis=0)
@@ -635,24 +645,33 @@
 
     chunk_rows = left_ref.shape[0] // FIELDS
 
+    def make_tile(block, field):
+        span = pl.ds(aligned(block * LANES, LANES), LANES)
+        piece = low_ref[field * EMB : (field + 1) * EMB, span]
+        tiled_ref[block & 1, field] = matmul_nt(eye, jnp.concatenate([piece] * GROUPS, axis=0))
+
     def permute(chunk, words):
         block = lax.div(chunk * chunk_rows, LANES)
-        first = chunk * chunk_rows - block * LANES
-        span = pl.ds(aligned(block * LANES, LANES), LANES)
-
-        @pl.when(first == 0)
-        def _():
+        first = 0 if words is left_ref else chunk_rows
+        ahead = list(range(FIELDS))[first * FIELDS // LANES : (first + chunk_rows) * FIELDS // LANES]
+        later = jnp.minimum(block + 1, blocks - 1)
+        for step in range(chunk_rows // 8):
+            start_row = first + step * 8
             for field in range(FIELDS):
-                piece = low_ref[field * EMB : (field + 1) * EMB, span]
-                tiled_ref[field] = matmul_nt(eye, jnp.concatenate([piece] * GROUPS, axis=0))
-
-        for step in range(chunk_rows // 8):
-            start_row = aligned(first + step * 8, 8)
-            for field in range(FIELDS):
-                tile = tiled_ref[field, pl.ds(start_row, 8), :]
+                place = step * FIELDS + field
+                total = chunk_rows // 8 * FIELDS
+                if place * len(ahead) // total != (place - 1) * len(ahead) // total:
+                    made = ahead[place * len(ahead) // total]
+                    make_tile(later, made)
+                tile = tiled_ref[block & 1, field, start_row : start_row + 8, :]
                 for k in range(8):
                     start = words[(step * 8 + k) * FIELDS + field]
                     pltpu.store(wide_ref.at[pl.ds(start, 8), :], tile, mask=lines[k])
+
+    def permute_before():
+        lax.fori_loop(0, slot_blocks, clear, 0, unroll=2)
+        for field in range(FIELDS):
+            make_tile(0, field)
 
     def permute_place(at):
         each = part_rows // chunk_rows
@@ -666,7 +685,7 @@
         permute_place,
         width // chunk_rows,
         permute,
-        lambda: lax.fori_loop(0, slot_blocks, clear, 0, unroll=2),
+        permute_before,
     )
 
     def merge(block, carry):
@@ -683,8 +702,8 @@
 
     lax.fori_loop(0, slot_blocks, merge, 0, unroll=4 if slot_blocks % 4 == 0 else 1)
     each = sent_ref.shape[0] // owners
-    for one in range(owners):
-        sent_refs[one][...] = sent_ref[one * each : (one + 1) * each, :]
+    for one, held in enumerate(order):
+        sent_refs[one][...] = sent_ref[held * each : (held + 1) * each, :]
 
 
 def add_kernel(owners, packed, table_lanes, index_ref, request_ref, asked_ref, *refs):
@@ -916,12 +935,9 @@
         size = lax.axis_size(axis)
         return lax.ppermute(values, axis, [(one, one ^ bits) for one in range(size)])
 
-    def swap_all(blocks):
-        order = sorted(range(1, owners), key=lambda bits: (-bits.bit_length(), bits))
-        moved = {bits: swap(blocks[bits], "batch", bits) for bits in order}
-        return [blocks[0]] + [moved[bits] for bits in range(1, owners)]
-
-    owner_list = row_owner.reshape(lookup_rows, LANES)
+    order = sorted(range(owners), key=lambda bits: (-bits.bit_length(), bits))
+
+    owner_list = row_owner.T
     local_list = local_row.reshape(lookup_rows, LANES)
     slot_rows = slots // LANES
     list_shape = jax.ShapeDtypeStruct((list_rows, LANES), I32)
@@ -991,7 +1007,7 @@
     shared_rows = H2 + 24 + D_IN // LANES * pairs + 16
     vectors = jnp.stack([tower_b, head_w])
     *sent, grad_dense, grad_weight, grad_bias, grad_shared = call(
-        functools.partial(dense_kernel, owners, part_rows, experts, scale),
+        functools.partial(dense_kernel, order, part_rows, experts, scale),
         (
             *[jax.ShapeDtypeStruct((PARTS * packed, LANES), BF16)] * owners,
             jax.ShapeDtypeStruct((DENSE, row_total), F32),
@@ -1015,13 +1031,13 @@
             pltpu.VMEM((pairs, row_total), F32),
             pltpu.VMEM((D_IN, row_total), F32),
             pltpu.VMEM((D_IN, row_total), BF16),
-            pltpu.VMEM((FIELDS, LANES, LANES), F32),
+            pltpu.VMEM((2, FIELDS, LANES, LANES), F32),
             *row_words,
             pltpu.VMEM((PARTS * part_slots, LANES), BF16),
         ],
         "dense",
         45,
-        56,
+        min(60, 30 + 4 * experts),
     )(
         back,
         out,
@@ -1036,7 +1052,8 @@
         labels,
         *early,
     )
-    received = swap_all(sent)
+    moved = {bits: swap(one, "batch", bits) if bits else one for bits, one in zip(order, sent)}
+    received = [moved[bits] for bits in range(owners)]
 
     def split(values):
         high = lax.reduce_precision(values, exponent_bits=8, mantissa_bits=7)
@@ -1094,12 +1111,14 @@
     sums = jnp.sum(pieces.astype(F32), axis=0)
     piece = jnp.concatenate([sums[:weight_piece].astype(BF16), *split(sums[weight_piece:])], axis=0)
     *kept, piece = tie(*kept, piece)
+    bit = 2
+    over = [swap(one, "expert", bit) for one in kept]
     pieces = exchange(jnp.broadcast_to(piece[None], (owners, *piece.shape)), "batch")
-
-    bit = 2
     while bit < experts:
-        kept = [add_low(one, swap(one, "expert", bit)) for one in kept]
+        kept = [add_low(one, other) for one, other in zip(kept, over)]
         bit *= 2
+        if bit < experts:
+            over = [swap(one, "expert", bit) for one in kept]
     small = call(
         functools.partial(unpack_kernel, weight_piece, extra_piece, pairs),
         tuple(

time: 235 us -> 242 us (1.030)
  local copies, waits for them, and re-layouts: 12.5 us -> 16.9 us
  other arithmetic: 8.71 us -> 6.18 us
    unnamed x34 -> x50, local copies, waits for them, and re-layouts: 8.81 us -> 15.9 us
    all_to_all x5, starting transfers between devices: 25.3 us -> 28.1 us  [exchange(): return lax.all_to_all(values, axis, split_axis=0, concat_axis=0, tiled=True)]
  transfers between devices with their start and end apart: 19 -> 19, of which waited for: 8 -> 9; matrix products, arithmetic and copies ran while one was open for 4% -> 2% of each run, Pallas kernels for 33% -> 32%
where the time goes in v3:
time: 242 us; the launch traced here: 241 us
  Pallas kernels  123 us (51%)
  starting transfers between devices  41.9 us (17%)
  waiting for transfers between devices  38.6 us (16%)
  local copies, waits for them, and re-layouts  16.9 us (7%)
  between operations  14.5 us (6%)
  other arithmetic  6.18 us (3%)
    pallas_call x1, Pallas kernels, shards(): call(functools.partial(add_kernel, owners, packed, table_lanes), (jax.Sha...  39.3 us
    pallas_call x1, Pallas kernels, shards(): call(functools.partial(dense_kernel, order, part_rows, experts, scale), (...  38.1 us
    ppermute x13, waiting for transfers between devices, swap(): lax.ppermute(values, axis, [(one, one ^ bits) for one in range(size)])  32.3 us
    all_to_all x5, starting transfers between devices, exchange(): return lax.all_to_all(values, axis, split_axis=0, concat_axis=0, tiled=True)  28.1 us
    pallas_call x2, Pallas kernels, shards(): call(functools.partial(fetch_kernel, owners, part, packed, table_lanes),...  26.8 us
    unnamed x50, local copies, waits for them, and re-layouts  15.9 us
    ppermute x13, starting transfers between devices, swap(): lax.ppermute(values, axis, [(one, one ^ bits) for one in range(size)])  13.8 us
    pallas_call x1, Pallas kernels, shards(): call(functools.partial(unpermute_kernel, part, part_rows), jax.ShapeDtype...  7.57 us
  transfers between devices with their start and end apart: 19, of which 9 were waited for; matrix products, arithmetic and copies ran while one was open for 2% of the time, Pallas kernels for 32%

profile of v3, /device:TPU:0, one launch (start us, length us, event | category | flops | bytes accessed | tf_op | source)
XLA Modules:
  0.0 241.2 jit_solution(17441183306388835507)
XLA Ops:
  9.0 7.5 %route.1 = (s32[272,128]{1,0:T(8,128)}, s32[144,128]{1,0:T(8,128)S(1)}, s32[144,128]{1,0:T(8,128)S(1)}) custom-call(s32[1]{0:T(128)} %bitcast.1.batch_ref, s32[1,16640]{1,0:T(1,128)S(1)} %bitcast.43, s32[130,128]{1,0:T(8,128)S(1)} %bitcast.42), custom_call_target="tpu_custom_call" | custom-call | flops 10350000128 | bytes 27000000 | tf_op jit(solution)/shard_map/route/pallas_call | solution.py:945
  16.4 7.3 %all-to-all-start = ((s32[8,1,4352]{2,1,0:T(1,128)}), s32[8,1,4352]{2,1,0:T(1,128)S(1)}, u32[]{:S(2)}, u32[]{:S(2)}) async-start(s32[8,1,4352]{2,1,0:T(1,128)} %bitcast.4), calls=%async_computation | async-start | bytes 278528 | tf_op jit(solution)/shard_map/all_to_all | solution.py:932
  25.4 3.1 %pack.1 = (f32[8208,128]{1,0:T(8,128)S(1)}, bf16[1296,128]{1,0:T(8,128)(2,1)}) custom-call(bf16[16,65536]{1,0:T(8,128)(2,1)S(1)} %bitcast.40, bf16[1,512,256]{2,1,0:T(8,128)(2,1)S(1)} %copy-done.2, bf16[1,256,128]{2,1,0:T(8,128)(2,1)S(1)} %copy-done.7, f32[1,256]{1,0:T(1,128)S(1)} %copy-done.13, f32[1,128]{1,0:T(1,128)S(1)} %copy-done.14), custom_call_target="tpu_custom_call" | custom-call | flops 5750000128 | bytes 15000000 | tf_op jit(solution)/shard_map/pack/pallas_call | solution.py:961
  28.4 2.0 copy-done.16
  31.2 2.2 copy-done.17
  33.4 13.4 %fetch.3 = bf16[2176,128]{1,0:T(8,128)(2,1)} custom-call(s32[34816]{0:T(1024)S(1)} %bitcast_add_fusion.request_ref, s32[272,128]{1,0:T(8,128)S(1)} %bitcast.37, f32[8208,128]{1,0:T(8,128)S(1)} %copy-done.17), custom_call_target="tpu_custom_call" | custom-call | flops 13799999488 | bytes 36000000 | tf_op jit(solution)/shard_map/fetch/pallas_call | solution.py:979
  46.9 5.4 %all-to-all-start.2 = ((bf16[8,272,128]{2,1,0:T(8,128)(2,1)}), bf16[8,272,128]{2,1,0:T(8,128)(2,1)S(1)}, u32[]{:S(2)}, u32[]{:S(2)}) async-start(bf16[8,272,128]{2,1,0:T(8,128)(2,1)} %bitcast.17), calls=%async_computation.2 | async-start | bytes 1114112 | tf_op jit(solution)/shard_map/all_to_all | solution.py:932
  52.3 2.2 copy-done.18
  54.5 13.4 %fetch.2 = bf16[2176,128]{1,0:T(8,128)(2,1)} custom-call(s32[34816]{0:T(1024)S(1)} %bitcast_add_fusion.request_ref, s32[272,128]{1,0:T(8,128)S(1)} %bitcast.38, f32[8208,128]{1,0:T(8,128)S(1)} %copy-done.18), custom_call_target="tpu_custom_call" | custom-call | flops 13799999488 | bytes 36000000 | tf_op jit(solution)/shard_map/fetch/pallas_call | solution.py:979
  67.9 6.1 %all-to-all-start.1 = ((bf16[8,272,128]{2,1,0:T(8,128)(2,1)}), bf16[8,272,128]{2,1,0:T(8,128)(2,1)S(1)}, u32[]{:S(2)}, u32[]{:S(2)}) async-start(bf16[8,272,128]{2,1,0:T(8,128)(2,1)} %bitcast.11), calls=%async_computation.1 | async-start | bytes 1114112 | tf_op jit(solution)/shard_map/all_to_all | solution.py:932
  74.1 7.6 %unpermute.1.refs_0_ = bf16[320,512]{1,0:T(8,128)(2,1)S(1)} custom-call(s32[18432]{0:T(1024)S(1)} %bitcast.45, bf16[2176,128]{1,0:T(8,128)(2,1)S(1)} %bitcast.36), custom_call_target="tpu_custom_call" | custom-call | flops 17250000896 | bytes 45000000 | tf_op jit(solution)/shard_map/unpermute/pallas_call | solution.py:996
  82.4 5.6 %all-to-all-done.1 = bf16[8,272,128]{2,1,0:T(8,128)(2,1)S(1)} async-done(((bf16[8,272,128]{2,1,0:T(8,128)(2,1)}), bf16[8,272,128]{2,1,0:T(8,128)(2,1)S(1)}, u32[]{:S(2)}, u32[]{:S(2)}) %all-to-all-start.1) | async-done | bytes 557088 | tf_op jit(solution)/shard_map/all_to_all | solution.py:932
  90.3 38.1 %dense.1 = (bf16[544,128]{1,0:T(8,128)(2,1)S(1)}, bf16[544,128]{1,0:T(8,128)(2,1)S(1)}, bf16[544,128]{1,0:T(8,128)(2,1)S(1)}, bf16[544,128]{1,0:T(8,128)(2,1)S(1...) custom-call(s32[18432]{0:T(1024)S(1)} %bitcast.46, ...), custom_call_target="tpu_custom_call" | custom-call | flops 51749998592 | bytes 135000000 | tf_op jit(solution)/shard_map/dense/pallas_call | solution.py:1009
  130.6 2.0 collective-permute-start.2
  133.4 3.0 %collective-permute-start.4 = (bf16[544,128]{1,0:T(8,128)(2,1)S(1)}, bf16[544,128]{1,0:T(8,128)(2,1)S(1)}, u32[]{:S(2)}, u32[]{:S(2)}) collective-permute-start(bf16[544,128]{1,0:T(8,128)(2,1)S(1)} %get-tuple-element.92), channel_id=1, source_target_pairs={{0,20},{4,16},{8,28},{12,24},{16,4},{20,0},{24,12},{28,8},{1,21},{... | collective-permute-start | bytes 417800 | tf_op jit(solution)/shard_map/ppermute | solution.py:936
  138.8 1.8 collective-permute-start.6
  142.0 9.4 %collective-permute-done.3.refs_4_ = bf16[544,128]{1,0:T(8,128)(2,1)S(1)} collective-permute-done((bf16[544,128]{1,0:T(8,128)(2,1)S(1)}, bf16[544,128]{1,0:T(8,128)(2,1)S(1)}, u32[]{:S(2)}, u32[]{:S(2)}) %collective-permute-start.3) | collective-permute-done | bytes 139296 | tf_op jit(solution)/shard_map/ppermute | solution.py:936
  151.4 3.8 %collective-permute-done.4.refs_5_ = bf16[544,128]{1,0:T(8,128)(2,1)S(1)} collective-permute-done((bf16[544,128]{1,0:T(8,128)(2,1)S(1)}, bf16[544,128]{1,0:T(8,128)(2,1)S(1)}, u32[]{:S(2)}, u32[]{:S(2)}) %collective-permute-start.4) | collective-permute-done | bytes 139296 | tf_op jit(solution)/shard_map/ppermute | solution.py:936
  155.2 3.4 %all-to-all-start.3 = ((bf16[32,192,128]{2,1,0:T(8,128)(2,1)}), bf16[32,192,128]{2,1,0:T(8,128)(2,1)}, u32[]{:S(2)}, u32[]{:S(2)}) async-start(bf16[32,192,128]{2,1,0:T(8,128)(2,1)} %bitcast.48), calls=%async_computation.3 | async-start | bytes 3145728 | tf_op jit(solution)/shard_map/all_to_all | solution.py:932
  161.1 39.3 %add.41 = (bf16[16,16384]{1,0:T(8,128)(2,1)S(1)}, bf16[16,16384]{1,0:T(8,128)(2,1)S(1)}, bf16[16,16384]{1,0:T(8,128)(2,1)S(1)}, bf16[16,16384]{1,0:T(8,128)(2,1)S(1)}) custom-call(s32[2]{0:T(128)S(1)} %pad_add_fusion.index_ref, s32[34816]{0:T(1024)S(1)} %bitcast_add_fusion.request_ref, s32[272,128]{1,0:T(8,128)S(1)} %bitcast.39, ...), custom_call_target="tpu_custom_call" | custom-call | flops 69000003584 | bytes 180000000 | tf_op jit(solution)/shard_map/add/pallas_call | solution.py:1090
  207.0 5.9 %all-to-all-start.4 = ((bf16[8,224,128]{2,1,0:T(8,128)(2,1)}), bf16[8,224,128]{2,1,0:T(8,128)(2,1)S(1)}, u32[]{:S(2)}, u32[]{:S(2)}) async-start(bf16[8,224,128]{2,1,0:T(8,128)(2,1)} %broadcast_in_dim.8), calls=%async_computation.4 | async-start | bytes 917504 | tf_op jit(solution)/shard_map/all_to_all | solution.py:932
  213.4 5.8 %collective-permute-done.9 = bf16[16,16384]{1,0:T(8,128)(2,1)S(1)} collective-permute-done((bf16[16,16384]{1,0:T(8,128)(2,1)S(1)}, bf16[16,16384]{1,0:T(8,128)(2,1)S(1)}, u32[]{:S(2)}, u32[]{:S(2)}) %collective-permute-start.9) | collective-permute-done | bytes 524320 | tf_op jit(solution)/shard_map/ppermute | solution.py:936
  219.4 10.5 %collective-permute-done.11 = bf16[16,16384]{1,0:T(8,128)(2,1)S(1)} collective-permute-done((bf16[16,16384]{1,0:T(8,128)(2,1)S(1)}, bf16[16,16384]{1,0:T(8,128)(2,1)S(1)}, u32[]{:S(2)}, u32[]{:S(2)}) %collective-permute-start.11) | collective-permute-done | bytes 524320 | tf_op jit(solution)/shard_map/ppermute | solution.py:936
  232.1 2.3 convert_bitcast_fusion
  (102 shorter events, 25.7 us)
Async XLA Ops:
  9.0 14.8 %copy-start.2 = (bf16[1,512,256]{2,1,0:T(8,128)(2,1)S(1)}, bf16[1,512,256]{2,1,0:T(8,128)(2,1)}, u32[]{:S(2)}) copy-start(bf16[1,512,256]{2,1,0:T(8,128)(2,1)} %hidden_w_ref.1) | copy-start | bytes 786436
  9.0 14.8 %copy-start.7 = (bf16[1,256,128]{2,1,0:T(8,128)(2,1)S(1)}, bf16[1,256,128]{2,1,0:T(8,128)(2,1)}, u32[]{:S(2)}) copy-start(bf16[1,256,128]{2,1,0:T(8,128)(2,1)} %output_w_ref.1) | copy-start | bytes 196612
  9.0 14.8 %copy-start.13 = (f32[1,256]{1,0:T(1,128)S(1)}, f32[1,256]{1,0:T(1,128)}, u32[]{:S(2)}) copy-start(f32[1,256]{1,0:T(1,128)} %hidden_b_ref) | copy-start | bytes 3076
  9.0 14.8 %copy-start.14 = (f32[1,128]{1,0:T(1,128)S(1)}, f32[1,128]{1,0:T(1,128)}, u32[]{:S(2)}) copy-start(f32[1,128]{1,0:T(1,128)} %output_b_ref.1) | copy-start | bytes 1540
  16.4 14.7 %all-to-all-start = ((s32[8,1,4352]{2,1,0:T(1,128)}), s32[8,1,4352]{2,1,0:T(1,128)S(1)}, u32[]{:S(2)}, u32[]{:S(2)}) async-start(s32[8,1,4352]{2,1,0:T(1,128)} %bitcast.4), calls=%async_computation | async-start | bytes 278528 | tf_op jit(solution)/shard_map/all_to_all | solution.py:932
  23.7 64.3 %all-gather.3.cloned.1.call-start = ((), (), s32[]{:S(2)}) async-start(), calls=%async_computation.5 | async-start | bytes 1658880 | tf_op jit(solution)/shard_map/all_gather | solution.py:973
  46.9 21.0 %all-to-all-start.2 = ((bf16[8,272,128]{2,1,0:T(8,128)(2,1)}), bf16[8,272,128]{2,1,0:T(8,128)(2,1)S(1)}, u32[]{:S(2)}, u32[]{:S(2)}) async-start(bf16[8,272,128]{2,1,0:T(8,128)(2,1)} %bitcast.17), calls=%async_computation.2 | async-start | bytes 1114112 | tf_op jit(solution)/shard_map/all_to_all | solution.py:932
  67.9 20.1 %all-to-all-start.1 = ((bf16[8,272,128]{2,1,0:T(8,128)(2,1)}), bf16[8,272,128]{2,1,0:T(8,128)(2,1)S(1)}, u32[]{:S(2)}, u32[]{:S(2)}) async-start(bf16[8,272,128]{2,1,0:T(8,128)(2,1)} %bitcast.11), calls=%async_computation.1 | async-start | bytes 1114112 | tf_op jit(solution)/shard_map/all_to_all | solution.py:932
  74.0 14.0 %copy-start.8 = (bf16[128,128]{1,0:T(8,128)(2,1)S(1)}, bf16[128,128]{1,0:T(8,128)(2,1)}, u32[]{:S(2)}) copy-start(bf16[128,128]{1,0:T(8,128)(2,1)} %tower_ref.1) | copy-start | bytes 98308
  129.1 7.4 %collective-permute-start = (bf16[544,128]{1,0:T(8,128)(2,1)}, bf16[544,128]{1,0:T(8,128)(2,1)S(1)}, u32[]{:S(2)}, u32[]{:S(2)}) collective-permute-start(bf16[544,128]{1,0:T(8,128)(2,1)} %get-tuple-element.84), channel_id=1, source_target_pairs={{0,4},{4,0},{8,12},{12,8},{16,20},{20,16},{24,28},{28,24},{1,5},{5... | collective-permute-start | bytes 417800 | tf_op jit(solution)/shard_map/ppermute | solution.py:936
  130.6 8.2 %collective-permute-start.1 = (bf16[544,128]{1,0:T(8,128)(2,1)S(1)}, bf16[544,128]{1,0:T(8,128)(2,1)S(1)}, u32[]{:S(2)}, u32[]{:S(2)}) collective-permute-start(bf16[544,128]{1,0:T(8,128)(2,1)S(1)} %get-tuple-element.89), channel_id=1, source_target_pairs={{0,8},{4,12},{8,0},{12,4},{16,24},{20,28},{24,16},{28,20},{1,9},{5... | collective-permute-start | bytes 417800 | tf_op jit(solution)/shard_map/ppermute | solution.py:936
  130.6 11.4 %collective-permute-start.2 = (bf16[544,128]{1,0:T(8,128)(2,1)S(1)}, bf16[544,128]{1,0:T(8,128)(2,1)S(1)}, u32[]{:S(2)}, u32[]{:S(2)}) collective-permute-start(bf16[544,128]{1,0:T(8,128)(2,1)S(1)} %get-tuple-element.90), channel_id=1, source_target_pairs={{0,12},{4,8},{8,4},{12,0},{16,28},{20,24},{24,20},{28,16},{1,13},{... | collective-permute-start | bytes 417800 | tf_op jit(solution)/shard_map/ppermute | solution.py:936
  132.6 18.7 %collective-permute-start.3 = (bf16[544,128]{1,0:T(8,128)(2,1)S(1)}, bf16[544,128]{1,0:T(8,128)(2,1)S(1)}, u32[]{:S(2)}, u32[]{:S(2)}) collective-permute-start(bf16[544,128]{1,0:T(8,128)(2,1)S(1)} %get-tuple-element.91), channel_id=1, source_target_pairs={{0,16},{4,20},{8,24},{12,28},{16,0},{20,4},{24,8},{28,12},{1,17},{... | collective-permute-start | bytes 417800 | tf_op jit(solution)/shard_map/ppermute | solution.py:936
  133.4 21.7 %collective-permute-start.4 = (bf16[544,128]{1,0:T(8,128)(2,1)S(1)}, bf16[544,128]{1,0:T(8,128)(2,1)S(1)}, u32[]{:S(2)}, u32[]{:S(2)}) collective-permute-start(bf16[544,128]{1,0:T(8,128)(2,1)S(1)} %get-tuple-element.92), channel_id=1, source_target_pairs={{0,20},{4,16},{8,28},{12,24},{16,4},{20,0},{24,12},{28,8},{1,21},{... | collective-permute-start | bytes 417800 | tf_op jit(solution)/shard_map/ppermute | solution.py:936
  136.5 22.1 %collective-permute-start.5 = (bf16[544,128]{1,0:T(8,128)(2,1)S(1)}, bf16[544,128]{1,0:T(8,128)(2,1)S(1)}, u32[]{:S(2)}, u32[]{:S(2)}) collective-permute-start(bf16[544,128]{1,0:T(8,128)(2,1)S(1)} %get-tuple-element.102), channel_id=1, source_target_pairs={{0,24},{4,28},{8,16},{12,20},{16,8},{20,12},{24,0},{28,4},{1,25},{... | collective-permute-start | bytes 417800 | tf_op jit(solution)/shard_map/ppermute | solution.py:936
  138.8 20.4 %collective-permute-start.6 = (bf16[544,128]{1,0:T(8,128)(2,1)S(1)}, bf16[544,128]{1,0:T(8,128)(2,1)S(1)}, u32[]{:S(2)}, u32[]{:S(2)}) collective-permute-start(bf16[544,128]{1,0:T(8,128)(2,1)S(1)} %get-tuple-element.103), channel_id=1, source_target_pairs={{0,28},{4,24},{8,20},{12,16},{16,12},{20,8},{24,4},{28,0},{1,29},{... | collective-permute-start | bytes 417800 | tf_op jit(solution)/shard_map/ppermute | solution.py:936
  155.2 45.2 %all-to-all-start.3 = ((bf16[32,192,128]{2,1,0:T(8,128)(2,1)}), bf16[32,192,128]{2,1,0:T(8,128)(2,1)}, u32[]{:S(2)}, u32[]{:S(2)}) async-start(bf16[32,192,128]{2,1,0:T(8,128)(2,1)} %bitcast.48), calls=%async_computation.3 | async-start | bytes 3145728 | tf_op jit(solution)/shard_map/all_to_all | solution.py:932
  200.4 2.3 collective-permute-start.7
  202.1 2.1 collective-permute-start.8
  204.4 14.8 %collective-permute-start.9 = (bf16[16,16384]{1,0:T(8,128)(2,1)S(1)}, bf16[16,16384]{1,0:T(8,128)(2,1)S(1)}, u32[]{:S(2)}, u32[]{:S(2)}) collective-permute-start(bf16[16,16384]{1,0:T(8,128)(2,1)S(1)} %add_convert_fusion.3), channel_id=1, source_target_pairs={{0,2},{1,3},{2,0},{3,1},{4,6},{5,7},{6,4},{7,5},{8,10},{9,11},{10,... | collective-permute-start | bytes 1572872 | tf_op jit(solution)/shard_map/ppermute | solution.py:936
  207.0 23.1 %all-to-all-start.4 = ((bf16[8,224,128]{2,1,0:T(8,128)(2,1)}), bf16[8,224,128]{2,1,0:T(8,128)(2,1)S(1)}, u32[]{:S(2)}, u32[]{:S(2)}) async-start(bf16[8,224,128]{2,1,0:T(8,128)(2,1)} %broadcast_in_dim.8), calls=%async_computation.4 | async-start | bytes 917504 | tf_op jit(solution)/shard_map/all_to_all | solution.py:932
  212.8 17.0 %collective-permute-start.11 = (bf16[16,16384]{1,0:T(8,128)(2,1)S(1)}, bf16[16,16384]{1,0:T(8,128)(2,1)S(1)}, u32[]{:S(2)}, u32[]{:S(2)}) collective-permute-start(bf16[16,16384]{1,0:T(8,128)(2,1)S(1)} %add_convert_fusion.2), channel_id=1, source_target_pairs={{0,2},{1,3},{2,0},{3,1},{4,6},{5,7},{6,4},{7,5},{8,10},{9,11},{10,... | collective-permute-start | bytes 1572872 | tf_op jit(solution)/shard_map/ppermute | solution.py:936
  219.3 11.7 %collective-permute-start.10 = (bf16[16,16384]{1,0:T(8,128)(2,1)S(1)}, bf16[16,16384]{1,0:T(8,128)(2,1)S(1)}, u32[]{:S(2)}, u32[]{:S(2)}) collective-permute-start(bf16[16,16384]{1,0:T(8,128)(2,1)S(1)} %add_convert_fusion.1), channel_id=1, source_target_pairs={{0,1},{1,0},{2,3},{3,2},{4,5},{5,4},{6,7},{7,6},{8,9},{9,8},{10,11... | collective-permute-start | bytes 1572872 | tf_op jit(solution)/shard_map/ppermute | solution.py:936
  230.0 2.0 collective-permute-start.12
  (20 other events, 96.1 us)
Sparse Core Ops, SparseCore 0:
  30.6 19.6 all-gather.2

commit v4 on v2

--- a/solution.py
+++ b/solution.py
@@ -26,7 +26,7 @@
 STREAMS = 8
 PARTS = 2
 CHUNK_ROWS = 64
-TABLE_CHUNKS = 2
+TABLE_CHUNKS = 1
 
 F32 = jnp.float32
 BF16 = jnp.bfloat16
@@ -282,9 +282,11 @@
 
 
 def fetch_kernel(
-    owners, part, packed, table_lanes, request_ref, asked_ref, table_ref, found_ref, turn_ref,
-    piece_ref, left_ref, right_ref, sems
+    owners, part, packed, table_lanes, request_ref, asked_ref, far_table_ref, found_ref, table_ref,
+    turn_ref, piece_ref, left_ref, right_ref, sems, table_sem
 ):
+    table_copy = pltpu.make_async_copy(far_table_ref, table_ref, table_sem)
+    table_copy.start()
     lines, _ = masks()
     chunks = packed // 16
     within = same_group()
@@ -301,6 +303,7 @@
 
     def before():
         lax.fori_loop(0, owners, turn_step, 0, unroll=4)
+        table_copy.wait()
 
     def process(source, words):
         for chunk in range(chunks):
@@ -384,10 +387,10 @@
     )
 
 
-def gather_blocks(block_refs, whole_ref):
+def gather_blocks(order, block_refs, whole_ref):
     rows = block_refs[0].shape[0]
-    for one, block_ref in enumerate(block_refs):
-        whole_ref[one * rows : (one + 1) * rows, :] = block_ref[...]
+    for held, block_ref in zip(order, block_refs):
+        whole_ref[held * rows : (held + 1) * rows, :] = block_ref[...]
 
 
 def unpermute_kernel(
@@ -407,7 +410,7 @@
 
 
 def dense_kernel(
-    owners,
+    order,
     part_rows,
     experts,
     scale,
@@ -426,6 +429,7 @@
 ):
     early = refs[: PARTS - 1]
     refs = refs[PARTS - 1 :]
+    owners = len(order)
     sent_refs = refs[:owners]
     (
         grad_dense_ref,
@@ -683,11 +687,12 @@
 
     lax.fori_loop(0, slot_blocks, merge, 0, unroll=4 if slot_blocks % 4 == 0 else 1)
     each = sent_ref.shape[0] // owners
-    for one in range(owners):
-        sent_refs[one][...] = sent_ref[one * each : (one + 1) * each, :]
-
-
-def add_kernel(owners, packed, table_lanes, index_ref, request_ref, asked_ref, *refs):
+    for one, held in enumerate(order):
+        sent_refs[one][...] = sent_ref[held * each : (held + 1) * each, :]
+
+
+def add_kernel(order, packed, table_lanes, index_ref, request_ref, asked_ref, *refs):
+    owners = len(order)
     received_refs = refs[:owners]
     table_refs = refs[owners : owners + 2 * TABLE_CHUNKS]
     (
@@ -754,7 +759,7 @@
             total[0:8, :] = jnp.zeros((8, LANES), F32)
             total[8 + rows : 16 + rows, :] = jnp.zeros((8, LANES), F32)
         lax.fori_loop(0, rows // LANES, clear, 0)
-        gather_blocks(received_refs, received_ref)
+        gather_blocks(order, received_refs, received_ref)
         for one in spread(0, left_grad_ref):
             one()
 
@@ -916,10 +921,7 @@
         size = lax.axis_size(axis)
         return lax.ppermute(values, axis, [(one, one ^ bits) for one in range(size)])
 
-    def swap_all(blocks):
-        order = sorted(range(1, owners), key=lambda bits: (-bits.bit_length(), bits))
-        moved = {bits: swap(blocks[bits], "batch", bits) for bits in order}
-        return [blocks[0]] + [moved[bits] for bits in range(1, owners)]
+    order = sorted(range(owners), key=lambda bits: (-bits.bit_length(), bits))
 
     owner_list = row_owner.reshape(lookup_rows, LANES)
     local_list = local_row.reshape(lookup_rows, LANES)
@@ -945,7 +947,7 @@
     table, weights = call(
         pack_kernel,
         (
-            pltpu.VMEM((table_packed + 16, LANES), F32),
+            jax.ShapeDtypeStruct((table_packed + 16, LANES), F32),
             jax.ShapeDtypeStruct((WEIGHT_ROWS, LANES), BF16),
         ),
         [VMEM] * 5,
@@ -953,7 +955,6 @@
         "pack",
         5,
     )(emb_table.T, hidden_w, output_w, hidden_b, output_b)
-    table = pltpu.with_memory_space_constraint(table, pltpu.VMEM)
     weights = lax.all_gather(weights, "expert", axis=0, tiled=False)
 
     slot_words = [pltpu.SMEM((GROUPS * packed,), I32)] * 2 + [pltpu.SemaphoreType.DMA((2,))]
@@ -963,12 +964,14 @@
         found = call(
             functools.partial(fetch_kernel, owners, part, packed, table_lanes),
             jax.ShapeDtypeStruct((part_slots, LANES), BF16),
-            [ANY, VMEM, VMEM],
+            [ANY, VMEM, ANY],
             [
+                pltpu.VMEM((table_packed + 16, LANES), F32),
                 pltpu.VMEM((part_slots, LANES), F32),
                 pltpu.VMEM((GROUPS * packed, LANES), F32),
             ]
-            + slot_words,
+            + slot_words
+            + [pltpu.SemaphoreType.DMA],
             "fetch",
             24 // PARTS,
         )(words, asked, table)
@@ -991,7 +994,7 @@
     shared_rows = H2 + 24 + D_IN // LANES * pairs + 16
     vectors = jnp.stack([tower_b, head_w])
     *sent, grad_dense, grad_weight, grad_bias, grad_shared = call(
-        functools.partial(dense_kernel, owners, part_rows, experts, scale),
+        functools.partial(dense_kernel, order, part_rows, experts, scale),
         (
             *[jax.ShapeDtypeStruct((PARTS * packed, LANES), BF16)] * owners,
             jax.ShapeDtypeStruct((DENSE, row_total), F32),
@@ -1036,14 +1039,15 @@
         labels,
         *early,
     )
-    received = swap_all(sent)
+    received = [swap(one, "batch", bits) if bits else one for bits, one in zip(order, sent)]
 
     def split(values):
         high = lax.reduce_precision(values, exponent_bits=8, mantissa_bits=7)
         return high.astype(BF16), (values - high).astype(BF16)
 
-    received[1], grad_weight, grad_bias, grad_shared = tie(
-        received[1], grad_weight, grad_bias, grad_shared
+    near = owners - 2
+    received[near], grad_weight, grad_bias, grad_shared = tie(
+        received[near], grad_weight, grad_bias, grad_shared
     )
 
     def spread_rows(values, piece):
@@ -1065,13 +1069,12 @@
     pieces = jnp.concatenate(
         [spread_rows(grad_weight, weight_piece), spread_rows(extra, extra_piece)], axis=2
     )
-    late = owners - 2
-    *received[:late], pieces = tie(*received[:late], pieces)
+    *received[2:], pieces = tie(*received[2:], pieces)
     pieces = exchange(pieces.reshape(owners * experts, piece_rows, LANES), ("batch", "expert"))
 
     columns = table_rows // 2 // TABLE_CHUNKS
     table_part = call(
-        functools.partial(add_kernel, owners, packed, table_lanes),
+        functools.partial(add_kernel, order, packed, table_lanes),
         (jax.ShapeDtypeStruct((EMB, columns), BF16),) * (2 * TABLE_CHUNKS),
         [SMEM, ANY, VMEM] + [VMEM] * owners,
         [pltpu.VMEM((PARTS * part_slots, LANES), BF16)]
@@ -1091,15 +1094,17 @@
         add_low(one, swap(other, "expert", 1))
         for one, other in zip(table_part[:TABLE_CHUNKS], table_part[TABLE_CHUNKS:])
     ]
+    *kept, pieces = tie(*kept, pieces)
+    over = [swap(one, "expert", 2) for one in kept]
     sums = jnp.sum(pieces.astype(F32), axis=0)
     piece = jnp.concatenate([sums[:weight_piece].astype(BF16), *split(sums[weight_piece:])], axis=0)
-    *kept, piece = tie(*kept, piece)
     pieces = exchange(jnp.broadcast_to(piece[None], (owners, *piece.shape)), "batch")
-
     bit = 2
     while bit < experts:
-        kept = [add_low(one, swap(one, "expert", bit)) for one in kept]
+        kept = [add_low(one, other) for one, other in zip(kept, over)]
         bit *= 2
+        if bit < experts:
+            over = [swap(one, "expert", bit) for one in kept]
     small = call(
         functools.partial(unpack_kernel, weight_piece, extra_piece, pairs),
         tuple(

time: 235 us -> 241 us (1.026)
  starting transfers between devices: 39.6 us -> 49.9 us
  waiting for transfers between devices: 37.4 us -> 30.5 us
    ppermute x13 -> x10, starting transfers between devices: 14.3 us -> 22.5 us  [swap(): lax.ppermute(values, axis, [(one, one ^ bits) for one in range(size)])]
    ppermute x13 -> x10, waiting for transfers between devices: 30.1 us -> 23.1 us  [swap(): lax.ppermute(values, axis, [(one, one ^ bits) for one in range(size)])]
  transfers between devices with their start and end apart: 19 -> 16, of which waited for: 8 -> 7; matrix products, arithmetic and copies ran while one was open for 4% -> 4% of each run, Pallas kernels for 33% -> 33%
where the time goes in v4:
time: 241 us; the launch traced here: 239 us
  Pallas kernels  122 us (51%)
  starting transfers between devices  49.9 us (21%)
  waiting for transfers between devices  30.5 us (13%)
  between operations  14.4 us (6%)
  local copies, waits for them, and re-layouts  12.5 us (5%)
  other arithmetic  9.9 us (4%)
    pallas_call x1, Pallas kernels, shards(): call(functools.partial(add_kernel, order, packed, table_lanes), (jax.Shap...  38.7 us
    pallas_call x1, Pallas kernels, shards(): call(functools.partial(dense_kernel, order, part_rows, experts, scale), (...  36.4 us
    pallas_call x2, Pallas kernels, shards(): call(functools.partial(fetch_kernel, owners, part, packed, table_lanes),...  28 us
    all_to_all x5, starting transfers between devices, exchange(): return lax.all_to_all(values, axis, split_axis=0, concat_axis=0, tiled=True)  27.4 us
    ppermute x10, waiting for transfers between devices, swap(): lax.ppermute(values, axis, [(one, one ^ bits) for one in range(size)])  23.1 us
    ppermute x10, starting transfers between devices, swap(): lax.ppermute(values, axis, [(one, one ^ bits) for one in range(size)])  22.5 us
    unnamed x34, local copies, waits for them, and re-layouts  8.81 us
    pallas_call x1, Pallas kernels, shards(): call(functools.partial(unpermute_kernel, part, part_rows), jax.ShapeDtype...  7.59 us
  transfers between devices with their start and end apart: 16, of which 7 were waited for; matrix products, arithmetic and copies ran while one was open for 4% of the time, Pallas kernels for 33%

profile of v4, /device:TPU:0, one launch (start us, length us, event | category | flops | bytes accessed | tf_op | source)
XLA Modules:
  0.0 239.2 jit_solution(13338773503340267372)
XLA Ops:
  9.1 7.4 %route.1 = (s32[272,128]{1,0:T(8,128)}, s32[144,128]{1,0:T(8,128)S(1)}, s32[144,128]{1,0:T(8,128)S(1)}) custom-call(s32[1]{0:T(128)} %bitcast.1.batch_ref, s32[130,128]{1,0:T(8,128)S(1)} %bitcast.38, s32[130,128]{1,0:T(8,128)S(1)} %bitcast.40), custom_call_target="tpu_custom_call" | custom-call | flops 10350000128 | bytes 27000000 | tf_op jit(solution)/shard_map/route/pallas_call | solution.py:931
  16.6 7.3 %all-to-all-start = ((s32[8,1,4352]{2,1,0:T(1,128)}), s32[8,1,4352]{2,1,0:T(1,128)S(1)}, u32[]{:S(2)}, u32[]{:S(2)}) async-start(s32[8,1,4352]{2,1,0:T(1,128)} %bitcast.3), calls=%async_computation | async-start | bytes 278528 | tf_op jit(solution)/shard_map/all_to_all | solution.py:918
  23.9 3.1 %pack.1 = (f32[8208,128]{1,0:T(8,128)S(1)}, bf16[1296,128]{1,0:T(8,128)(2,1)}) custom-call(bf16[16,65536]{1,0:T(8,128)(2,1)S(1)} %bitcast.39, bf16[1,512,256]{2,1,0:T(8,128)(2,1)S(1)} %copy-done.1, bf16[1,256,128]{2,1,0:T(8,128)(2,1)S(1)} %copy-done.3, f32[1,256]{1,0:T(1,128)S(1)} %copy-done.4, f32[1,128]{1,0:T(1,128)S(1)} %copy-done.5), custom_call_target="tpu_custom_call" | custom-call | flops 5750000128 | bytes 15000000 | tf_op jit(solution)/shard_map/pack/pallas_call | solution.py:947
  27.0 2.0 copy-done.8
  31.4 2.2 copy-done.9
  33.6 14.0 %fetch.3 = bf16[2176,128]{1,0:T(8,128)(2,1)} custom-call(s32[34816]{0:T(1024)S(1)} %bitcast_add_fusion.request_ref, s32[272,128]{1,0:T(8,128)S(1)} %bitcast.35, f32[8208,128]{1,0:T(8,128)S(1)} %copy-done.9), custom_call_target="tpu_custom_call" | custom-call | flops 13799999488 | bytes 36000000 | tf_op jit(solution)/shard_map/fetch/pallas_call | solution.py:964
  47.6 4.3 %all-to-all-start.2 = ((bf16[8,272,128]{2,1,0:T(8,128)(2,1)}), bf16[8,272,128]{2,1,0:T(8,128)(2,1)S(1)}, u32[]{:S(2)}, u32[]{:S(2)}) async-start(bf16[8,272,128]{2,1,0:T(8,128)(2,1)} %bitcast.16), calls=%async_computation.2 | async-start | bytes 1114112 | tf_op jit(solution)/shard_map/all_to_all | solution.py:918
  51.9 2.2 copy-done.10
  54.1 14.0 %fetch.2 = bf16[2176,128]{1,0:T(8,128)(2,1)} custom-call(s32[34816]{0:T(1024)S(1)} %bitcast_add_fusion.request_ref, s32[272,128]{1,0:T(8,128)S(1)} %bitcast.36, f32[8208,128]{1,0:T(8,128)S(1)} %copy-done.10), custom_call_target="tpu_custom_call" | custom-call | flops 13799999488 | bytes 36000000 | tf_op jit(solution)/shard_map/fetch/pallas_call | solution.py:964
  68.1 6.0 %all-to-all-start.1 = ((bf16[8,272,128]{2,1,0:T(8,128)(2,1)}), bf16[8,272,128]{2,1,0:T(8,128)(2,1)S(1)}, u32[]{:S(2)}, u32[]{:S(2)}) async-start(bf16[8,272,128]{2,1,0:T(8,128)(2,1)} %bitcast.10), calls=%async_computation.1 | async-start | bytes 1114112 | tf_op jit(solution)/shard_map/all_to_all | solution.py:918
  74.1 7.6 %unpermute.1.refs_0_ = bf16[320,512]{1,0:T(8,128)(2,1)S(1)} custom-call(s32[18432]{0:T(1024)S(1)} %bitcast.41, bf16[2176,128]{1,0:T(8,128)(2,1)S(1)} %bitcast.34), custom_call_target="tpu_custom_call" | custom-call | flops 17250000896 | bytes 45000000 | tf_op jit(solution)/shard_map/unpermute/pallas_call | solution.py:983
  82.4 5.7 %all-to-all-done.1 = bf16[8,272,128]{2,1,0:T(8,128)(2,1)S(1)} async-done(((bf16[8,272,128]{2,1,0:T(8,128)(2,1)}), bf16[8,272,128]{2,1,0:T(8,128)(2,1)S(1)}, u32[]{:S(2)}, u32[]{:S(2)}) %all-to-all-start.1) | async-done | bytes 557088 | tf_op jit(solution)/shard_map/all_to_all | solution.py:918
  88.9 36.4 %dense.1 = (bf16[544,128]{1,0:T(8,128)(2,1)}, bf16[544,128]{1,0:T(8,128)(2,1)}, bf16[544,128]{1,0:T(8,128)(2,1)}, bf16[544,128]{1,0:T(8,128)(2,1)}, bf16[544,128...) custom-call(s32[18432]{0:T(1024)} %bitcast.42, ...), custom_call_target="tpu_custom_call" | custom-call | flops 51749998592 | bytes 135000000 | tf_op jit(solution)/shard_map/dense/pallas_call | solution.py:996
  126.9 2.9 %collective-permute-start.1 = (bf16[544,128]{1,0:T(8,128)(2,1)}, bf16[544,128]{1,0:T(8,128)(2,1)S(1)}, u32[]{:S(2)}, u32[]{:S(2)}) collective-permute-start(bf16[544,128]{1,0:T(8,128)(2,1)} %get-tuple-element.78), channel_id=1, source_target_pairs={{0,20},{4,16},{8,28},{12,24},{16,4},{20,0},{24,12},{28,8},{1,21},{... | collective-permute-start | bytes 417800 | tf_op jit(solution)/shard_map/ppermute | solution.py:922
  131.0 3.5 %collective-permute-start.3 = (bf16[544,128]{1,0:T(8,128)(2,1)}, bf16[544,128]{1,0:T(8,128)(2,1)S(1)}, u32[]{:S(2)}, u32[]{:S(2)}) collective-permute-start(bf16[544,128]{1,0:T(8,128)(2,1)} %get-tuple-element.80), channel_id=1, source_target_pairs={{0,28},{4,24},{8,20},{12,16},{16,12},{20,8},{24,4},{28,0},{1,29},{... | collective-permute-start | bytes 417800 | tf_op jit(solution)/shard_map/ppermute | solution.py:922
  139.4 11.6 %collective-permute-start.5 = (bf16[544,128]{1,0:T(8,128)(2,1)S(1)}, bf16[544,128]{1,0:T(8,128)(2,1)S(1)}, u32[]{:S(2)}, u32[]{:S(2)}) collective-permute-start(bf16[544,128]{1,0:T(8,128)(2,1)S(1)} %copy-done.16), channel_id=1, source_target_pairs={{0,12},{4,8},{8,4},{12,0},{16,28},{20,24},{24,20},{28,16},{1,13},{... | collective-permute-start | bytes 417800 | tf_op jit(solution)/shard_map/ppermute | solution.py:922
  152.4 1.7 collective-permute-done.5.refs_5_
  154.0 4.6 %all-to-all-start.3 = ((bf16[32,192,128]{2,1,0:T(8,128)(2,1)}), bf16[32,192,128]{2,1,0:T(8,128)(2,1)}, u32[]{:S(2)}, u32[]{:S(2)}) async-start(bf16[32,192,128]{2,1,0:T(8,128)(2,1)} %bitcast.22), calls=%async_computation.3 | async-start | bytes 3145728 | tf_op jit(solution)/shard_map/all_to_all | solution.py:918
  158.7 38.7 %add.32 = (bf16[16,32768]{1,0:T(8,128)(2,1)S(1)}, bf16[16,32768]{1,0:T(8,128)(2,1)S(1)}) custom-call(s32[2]{0:T(128)S(1)} %pad_add_fusion.index_ref, s32[34816]{0:T(1024)S(1)} %bitcast_add_fusion.request_ref, s32[272,128]{1,0:T(8,128)S(1)} %bitcast.37, bf16[544,128]{1,0:T(8,128)(2,1)S(1)} %collective-permute-done.refs_0_, ...), custom_call_target="tpu_custom_call" | custom-call | flops 69000003584 | bytes 180000000 | tf_op jit(solution)/shard_map/add/pallas_call | solution.py:1076
  197.5 2.6 %collective-permute-done.7 = bf16[16,32768]{1,0:T(8,128)(2,1)S(1)} collective-permute-done((bf16[16,32768]{1,0:T(8,128)(2,1)S(1)}, bf16[16,32768]{1,0:T(8,128)(2,1)S(1)}, u32[]{:S(2)}, u32[]{:S(2)}) %collective-permute-start.7) | collective-permute-done | bytes 1048608 | tf_op jit(solution)/shard_map/ppermute | solution.py:922
  204.5 5.2 %all-to-all-start.4 = ((bf16[8,224,128]{2,1,0:T(8,128)(2,1)}), bf16[8,224,128]{2,1,0:T(8,128)(2,1)S(1)}, u32[]{:S(2)}, u32[]{:S(2)}) async-start(bf16[8,224,128]{2,1,0:T(8,128)(2,1)} %broadcast_in_dim.8), calls=%async_computation.4 | async-start | bytes 917504 | tf_op jit(solution)/shard_map/all_to_all | solution.py:918
  209.6 16.1 %collective-permute-done.8 = bf16[16,32768]{1,0:T(8,128)(2,1)} collective-permute-done((bf16[16,32768]{1,0:T(8,128)(2,1)S(1)}, bf16[16,32768]{1,0:T(8,128)(2,1)}, u32[]{:S(2)}, u32[]{:S(2)}) %collective-permute-start.8) | collective-permute-done | bytes 1048608 | tf_op jit(solution)/shard_map/ppermute | solution.py:922
  228.2 1.7 collective-permute-done.9
  230.1 2.3 convert_bitcast_fusion
  (79 shorter events, 21.7 us)
Async XLA Ops:
  9.1 14.8 %copy-start = (bf16[65536,16]{0,1:T(8,128)(2,1)S(1)}, bf16[65536,16]{0,1:T(8,128)(2,1)}, u32[]{:S(2)}) copy-start(bf16[65536,16]{0,1:T(8,128)(2,1)} %param.15) | copy-start | bytes 6291460
  9.1 14.8 %copy-start.1 = (bf16[1,512,256]{2,1,0:T(8,128)(2,1)S(1)}, bf16[1,512,256]{2,1,0:T(8,128)(2,1)}, u32[]{:S(2)}) copy-start(bf16[1,512,256]{2,1,0:T(8,128)(2,1)} %hidden_w_ref.1) | copy-start | bytes 786436
  9.1 14.8 %copy-start.3 = (bf16[1,256,128]{2,1,0:T(8,128)(2,1)S(1)}, bf16[1,256,128]{2,1,0:T(8,128)(2,1)}, u32[]{:S(2)}) copy-start(bf16[1,256,128]{2,1,0:T(8,128)(2,1)} %output_w_ref.1) | copy-start | bytes 196612
  9.1 14.8 %copy-start.4 = (f32[1,256]{1,0:T(1,128)S(1)}, f32[1,256]{1,0:T(1,128)}, u32[]{:S(2)}) copy-start(f32[1,256]{1,0:T(1,128)} %hidden_b_ref) | copy-start | bytes 3076
  9.1 14.8 %copy-start.5 = (f32[1,128]{1,0:T(1,128)S(1)}, f32[1,128]{1,0:T(1,128)}, u32[]{:S(2)}) copy-start(f32[1,128]{1,0:T(1,128)} %output_b_ref.1) | copy-start | bytes 1540
  16.6 10.5 %copy-start.7 = (s32[144,128]{1,0:T(8,128)}, s32[144,128]{1,0:T(8,128)S(1)}, u32[]{:S(2)}) copy-start(s32[144,128]{1,0:T(8,128)S(1)} %get-tuple-element.72) | copy-start | bytes 221188
  16.6 57.5 %copy-start.6 = (s32[144,128]{1,0:T(8,128)}, s32[144,128]{1,0:T(8,128)S(1)}, u32[]{:S(2)}) copy-start(s32[144,128]{1,0:T(8,128)S(1)} %get-tuple-element.71) | copy-start | bytes 221188
  16.6 14.7 %all-to-all-start = ((s32[8,1,4352]{2,1,0:T(1,128)}), s32[8,1,4352]{2,1,0:T(1,128)S(1)}, u32[]{:S(2)}, u32[]{:S(2)}) async-start(s32[8,1,4352]{2,1,0:T(1,128)} %bitcast.3), calls=%async_computation | async-start | bytes 278528 | tf_op jit(solution)/shard_map/all_to_all | solution.py:918
  23.8 64.3 %all-gather.3.cloned.1.call-start = ((), (), s32[]{:S(2)}) async-start(), calls=%async_computation.5 | async-start | bytes 1658880 | tf_op jit(solution)/shard_map/all_gather | solution.py:958
  47.6 20.5 %all-to-all-start.2 = ((bf16[8,272,128]{2,1,0:T(8,128)(2,1)}), bf16[8,272,128]{2,1,0:T(8,128)(2,1)S(1)}, u32[]{:S(2)}, u32[]{:S(2)}) async-start(bf16[8,272,128]{2,1,0:T(8,128)(2,1)} %bitcast.16), calls=%async_computation.2 | async-start | bytes 1114112 | tf_op jit(solution)/shard_map/all_to_all | solution.py:918
  68.1 20.0 %all-to-all-start.1 = ((bf16[8,272,128]{2,1,0:T(8,128)(2,1)}), bf16[8,272,128]{2,1,0:T(8,128)(2,1)S(1)}, u32[]{:S(2)}, u32[]{:S(2)}) async-start(bf16[8,272,128]{2,1,0:T(8,128)(2,1)} %bitcast.10), calls=%async_computation.1 | async-start | bytes 1114112 | tf_op jit(solution)/shard_map/all_to_all | solution.py:918
  125.3 14.1 %copy-start.16 = (bf16[544,128]{1,0:T(8,128)(2,1)S(1)}, bf16[544,128]{1,0:T(8,128)(2,1)}, u32[]{:S(2)}) copy-start(bf16[544,128]{1,0:T(8,128)(2,1)} %get-tuple-element.82) | copy-start | bytes 417796
  125.3 9.3 %collective-permute-start.6 = (bf16[544,128]{1,0:T(8,128)(2,1)}, bf16[544,128]{1,0:T(8,128)(2,1)S(1)}, u32[]{:S(2)}, u32[]{:S(2)}) collective-permute-start(bf16[544,128]{1,0:T(8,128)(2,1)} %get-tuple-element.83), channel_id=1, source_target_pairs={{0,4},{4,0},{8,12},{12,8},{16,20},{20,16},{24,28},{28,24},{1,5},{5... | collective-permute-start | bytes 417800 | tf_op jit(solution)/shard_map/ppermute | solution.py:922
  126.9 31.8 %collective-permute-start = (bf16[544,128]{1,0:T(8,128)(2,1)}, bf16[544,128]{1,0:T(8,128)(2,1)S(1)}, u32[]{:S(2)}, u32[]{:S(2)}) collective-permute-start(bf16[544,128]{1,0:T(8,128)(2,1)} %get-tuple-element.77), channel_id=1, source_target_pairs={{0,16},{4,20},{8,24},{12,28},{16,0},{20,4},{24,8},{28,12},{1,17},{... | collective-permute-start | bytes 417800 | tf_op jit(solution)/shard_map/ppermute | solution.py:922
  126.9 31.8 %collective-permute-start.1 = (bf16[544,128]{1,0:T(8,128)(2,1)}, bf16[544,128]{1,0:T(8,128)(2,1)S(1)}, u32[]{:S(2)}, u32[]{:S(2)}) collective-permute-start(bf16[544,128]{1,0:T(8,128)(2,1)} %get-tuple-element.78), channel_id=1, source_target_pairs={{0,20},{4,16},{8,28},{12,24},{16,4},{20,0},{24,12},{28,8},{1,21},{... | collective-permute-start | bytes 417800 | tf_op jit(solution)/shard_map/ppermute | solution.py:922
  129.8 9.6 %collective-permute-start.2 = (bf16[544,128]{1,0:T(8,128)(2,1)}, bf16[544,128]{1,0:T(8,128)(2,1)S(1)}, u32[]{:S(2)}, u32[]{:S(2)}) collective-permute-start(bf16[544,128]{1,0:T(8,128)(2,1)} %get-tuple-element.79), channel_id=1, source_target_pairs={{0,24},{4,28},{8,16},{12,20},{16,8},{20,12},{24,0},{28,4},{1,25},{... | collective-permute-start | bytes 417800 | tf_op jit(solution)/shard_map/ppermute | solution.py:922
  131.0 21.3 %collective-permute-start.3 = (bf16[544,128]{1,0:T(8,128)(2,1)}, bf16[544,128]{1,0:T(8,128)(2,1)S(1)}, u32[]{:S(2)}, u32[]{:S(2)}) collective-permute-start(bf16[544,128]{1,0:T(8,128)(2,1)} %get-tuple-element.80), channel_id=1, source_target_pairs={{0,28},{4,24},{8,20},{12,16},{16,12},{20,8},{24,4},{28,0},{1,29},{... | collective-permute-start | bytes 417800 | tf_op jit(solution)/shard_map/ppermute | solution.py:922
  134.6 17.8 %collective-permute-start.4 = (bf16[544,128]{1,0:T(8,128)(2,1)}, bf16[544,128]{1,0:T(8,128)(2,1)S(1)}, u32[]{:S(2)}, u32[]{:S(2)}) collective-permute-start(bf16[544,128]{1,0:T(8,128)(2,1)} %get-tuple-element.81), channel_id=1, source_target_pairs={{0,8},{4,12},{8,0},{12,4},{16,24},{20,28},{24,16},{28,20},{1,9},{5... | collective-permute-start | bytes 417800 | tf_op jit(solution)/shard_map/ppermute | solution.py:922
  139.4 14.6 %collective-permute-start.5 = (bf16[544,128]{1,0:T(8,128)(2,1)S(1)}, bf16[544,128]{1,0:T(8,128)(2,1)S(1)}, u32[]{:S(2)}, u32[]{:S(2)}) collective-permute-start(bf16[544,128]{1,0:T(8,128)(2,1)S(1)} %copy-done.16), channel_id=1, source_target_pairs={{0,12},{4,8},{8,4},{12,0},{16,28},{20,24},{24,20},{28,16},{1,13},{... | collective-permute-start | bytes 417800 | tf_op jit(solution)/shard_map/ppermute | solution.py:922
  154.0 43.4 %all-to-all-start.3 = ((bf16[32,192,128]{2,1,0:T(8,128)(2,1)}), bf16[32,192,128]{2,1,0:T(8,128)(2,1)}, u32[]{:S(2)}, u32[]{:S(2)}) async-start(bf16[32,192,128]{2,1,0:T(8,128)(2,1)} %bitcast.22), calls=%async_computation.3 | async-start | bytes 3145728 | tf_op jit(solution)/shard_map/all_to_all | solution.py:918
  197.4 2.7 %collective-permute-start.7 = (bf16[16,32768]{1,0:T(8,128)(2,1)S(1)}, bf16[16,32768]{1,0:T(8,128)(2,1)S(1)}, u32[]{:S(2)}, u32[]{:S(2)}) collective-permute-start(bf16[16,32768]{1,0:T(8,128)(2,1)S(1)} %get-tuple-element.102), channel_id=1, source_target_pairs={{0,1},{1,0},{2,3},{3,2},{4,5},{5,4},{6,7},{7,6},{8,9},{9,8},{10,11... | collective-permute-start | bytes 3145736 | tf_op jit(solution)/shard_map/ppermute | solution.py:922
  200.4 25.4 %collective-permute-start.8 = (bf16[16,32768]{1,0:T(8,128)(2,1)S(1)}, bf16[16,32768]{1,0:T(8,128)(2,1)}, u32[]{:S(2)}, u32[]{:S(2)}) collective-permute-start(bf16[16,32768]{1,0:T(8,128)(2,1)S(1)} %add_convert_fusion.1), channel_id=1, source_target_pairs={{0,2},{1,3},{2,0},{3,1},{4,6},{5,7},{6,4},{7,5},{8,10},{9,11},{10,... | collective-permute-start | bytes 3145736 | tf_op jit(solution)/shard_map/ppermute | solution.py:922
  204.5 22.9 %all-to-all-start.4 = ((bf16[8,224,128]{2,1,0:T(8,128)(2,1)}), bf16[8,224,128]{2,1,0:T(8,128)(2,1)S(1)}, u32[]{:S(2)}, u32[]{:S(2)}) async-start(bf16[8,224,128]{2,1,0:T(8,128)(2,1)} %broadcast_in_dim.8), calls=%async_computation.4 | async-start | bytes 917504 | tf_op jit(solution)/shard_map/all_to_all | solution.py:918
  227.2 2.7 %collective-permute-start.9 = (bf16[16,32768]{1,0:T(8,128)(2,1)S(1)}, bf16[16,32768]{1,0:T(8,128)(2,1)S(1)}, u32[]{:S(2)}, u32[]{:S(2)}) collective-permute-start(bf16[16,32768]{1,0:T(8,128)(2,1)S(1)} %add_convert_fusion), channel_id=1, source_target_pairs={{0,1},{1,0},{2,3},{3,2},{4,5},{5,4},{6,7},{7,6},{8,9},{9,8},{10,11... | collective-permute-start | bytes 3145736 | tf_op jit(solution)/shard_map/ppermute | solution.py:922
  (9 other events, 25.4 us)
Sparse Core Ops, SparseCore 0:
  29.1 19.6 all-gather.2

commit v5 on v2

--- a/solution.py
+++ b/solution.py
@@ -282,9 +282,11 @@
 
 
 def fetch_kernel(
-    owners, part, packed, table_lanes, request_ref, asked_ref, table_ref, found_ref, turn_ref,
-    piece_ref, left_ref, right_ref, sems
+    owners, part, packed, table_lanes, request_ref, asked_ref, far_table_ref, found_ref, table_ref,
+    turn_ref, piece_ref, left_ref, right_ref, sems, table_sem
 ):
+    table_copy = pltpu.make_async_copy(far_table_ref, table_ref, table_sem)
+    table_copy.start()
     lines, _ = masks()
     chunks = packed // 16
     within = same_group()
@@ -301,6 +303,7 @@
 
     def before():
         lax.fori_loop(0, owners, turn_step, 0, unroll=4)
+        table_copy.wait()
 
     def process(source, words):
         for chunk in range(chunks):
@@ -917,9 +920,7 @@
         return lax.ppermute(values, axis, [(one, one ^ bits) for one in range(size)])
 
     def swap_all(blocks):
-        order = sorted(range(1, owners), key=lambda bits: (-bits.bit_length(), bits))
-        moved = {bits: swap(blocks[bits], "batch", bits) for bits in order}
-        return [blocks[0]] + [moved[bits] for bits in range(1, owners)]
+        return [blocks[0]] + [swap(blocks[bits], "batch", bits) for bits in range(1, owners)]
 
     owner_list = row_owner.reshape(lookup_rows, LANES)
     local_list = local_row.reshape(lookup_rows, LANES)
@@ -945,15 +946,15 @@
     table, weights = call(
         pack_kernel,
         (
-            pltpu.VMEM((table_packed + 16, LANES), F32),
+            jax.ShapeDtypeStruct((table_packed + 16, LANES), F32),
             jax.ShapeDtypeStruct((WEIGHT_ROWS, LANES), BF16),
         ),
         [VMEM] * 5,
         [],
         "pack",
         5,
+        56,
     )(emb_table.T, hidden_w, output_w, hidden_b, output_b)
-    table = pltpu.with_memory_space_constraint(table, pltpu.VMEM)
     weights = lax.all_gather(weights, "expert", axis=0, tiled=False)
 
     slot_words = [pltpu.SMEM((GROUPS * packed,), I32)] * 2 + [pltpu.SemaphoreType.DMA((2,))]
@@ -963,14 +964,17 @@
         found = call(
             functools.partial(fetch_kernel, owners, part, packed, table_lanes),
             jax.ShapeDtypeStruct((part_slots, LANES), BF16),
-            [ANY, VMEM, VMEM],
+            [ANY, VMEM, ANY],
             [
+                pltpu.VMEM((table_packed + 16, LANES), F32),
                 pltpu.VMEM((part_slots, LANES), F32),
                 pltpu.VMEM((GROUPS * packed, LANES), F32),
             ]
-            + slot_words,
+            + slot_words
+            + [pltpu.SemaphoreType.DMA],
             "fetch",
             24 // PARTS,
+            56,
         )(words, asked, table)
         found = exchange(found.reshape(owners, packed, LANES), "batch")
         returned.append(found.reshape(part_slots, LANES))
@@ -984,6 +988,7 @@
                 [pltpu.VMEM((GROUPS * part_slots + 16, LANES), F32), *row_words],
                 "unpermute",
                 15,
+                56,
             )(back, returned[part])
         )
 
@@ -1042,8 +1047,9 @@
         high = lax.reduce_precision(values, exponent_bits=8, mantissa_bits=7)
         return high.astype(BF16), (values - high).astype(BF16)
 
-    received[1], grad_weight, grad_bias, grad_shared = tie(
-        received[1], grad_weight, grad_bias, grad_shared
+    far = owners // 2
+    received[far], grad_weight, grad_bias, grad_shared = tie(
+        received[far], grad_weight, grad_bias, grad_shared
     )
 
     def spread_rows(values, piece):
@@ -1091,15 +1097,17 @@
         add_low(one, swap(other, "expert", 1))
         for one, other in zip(table_part[:TABLE_CHUNKS], table_part[TABLE_CHUNKS:])
     ]
+    *kept, pieces = tie(*kept, pieces)
+    over = [swap(one, "expert", 2) for one in kept]
     sums = jnp.sum(pieces.astype(F32), axis=0)
     piece = jnp.concatenate([sums[:weight_piece].astype(BF16), *split(sums[weight_piece:])], axis=0)
-    *kept, piece = tie(*kept, piece)
     pieces = exchange(jnp.broadcast_to(piece[None], (owners, *piece.shape)), "batch")
-
     bit = 2
     while bit < experts:
-        kept = [add_low(one, swap(one, "expert", bit)) for one in kept]
+        kept = [add_low(one, other) for one, other in zip(kept, over)]
         bit *= 2
+        if bit < experts:
+            over = [swap(one, "expert", bit) for one in kept]
     small = call(
         functools.partial(unpack_kernel, weight_piece, extra_piece, pairs),
         tuple(

time: 235 us -> 233 us (level)
  waiting for transfers between devices: 37.4 us -> 27.9 us
  starting transfers between devices: 39.6 us -> 46.3 us
  local copies, waits for them, and re-layouts: 12.5 us -> 6.7 us
  Pallas kernels: 121 us -> 126 us
    ppermute x13, waiting for transfers between devices: 30.1 us -> 19.2 us  [swap(): lax.ppermute(values, axis, [(one, one ^ bits) for one in range(size)])]
    all_to_all x5, starting transfers between devices: 25.3 us -> 31.2 us  [exchange(): return lax.all_to_all(values, axis, split_axis=0, concat_axis=0, tiled=True)]
    unnamed x34 -> x24, local copies, waits for them, and re-layouts: 8.81 us -> 2.96 us
    pallas_call x1, Pallas kernels: 39.4 us -> 34.1 us  [shards(): call(functools.partial(add_kernel, owners, packed, table_lanes), (jax.Sha...]
    pallas_call x2, Pallas kernels: 26.7 us -> 31.2 us  [shards(): call(functools.partial(fetch_kernel, owners, part, packed, table_lanes),...]
    pallas_call x1, Pallas kernels: 3.07 us -> 6.25 us  [shards(): call(pack_kernel, (jax.ShapeDtypeStruct((table_packed + 16, LANES), F32),...]
  transfers between devices with their start and end apart: 19 -> 19, of which waited for: 8 -> 10; matrix products, arithmetic and copies ran while one was open for 4% -> 4% of each run, Pallas kernels for 33% -> 35%
where the time goes in v5:
time: 233 us; the launch traced here: 231 us
  Pallas kernels  126 us (54%)
  starting transfers between devices  46.3 us (20%)
  waiting for transfers between devices  27.9 us (12%)
  between operations  14.4 us (6%)
  other arithmetic  10.5 us (5%)
  local copies, waits for them, and re-layouts  6.7 us (3%)
    pallas_call x1, Pallas kernels, shards(): call(functools.partial(dense_kernel, owners, part_rows, experts, scale),...  36.4 us
    pallas_call x1, Pallas kernels, shards(): call(functools.partial(add_kernel, owners, packed, table_lanes), (jax.Sha...  34.1 us
    all_to_all x5, starting transfers between devices, exchange(): return lax.all_to_all(values, axis, split_axis=0, concat_axis=0, tiled=True)  31.2 us
    pallas_call x2, Pallas kernels, shards(): call(functools.partial(fetch_kernel, owners, part, packed, table_lanes),...  31.2 us
    ppermute x13, waiting for transfers between devices, swap(): lax.ppermute(values, axis, [(one, one ^ bits) for one in range(size)])  19.2 us
    ppermute x13, starting transfers between devices, swap(): lax.ppermute(values, axis, [(one, one ^ bits) for one in range(size)])  15 us
    pallas_call x1, Pallas kernels, shards(): call(functools.partial(unpermute_kernel, part, part_rows), jax.ShapeDtype...  9.37 us
    all_to_all x5, waiting for transfers between devices, exchange(): return lax.all_to_all(values, axis, split_axis=0, concat_axis=0, tiled=True)  8.66 us
  transfers between devices with their start and end apart: 19, of which 10 were waited for; matrix products, arithmetic and copies ran while one was open for 4% of the time, Pallas kernels for 35%

profile of v5, /device:TPU:0, one launch (start us, length us, event | category | flops | bytes accessed | tf_op | source)
XLA Modules:
  0.0 231.5 jit_solution(17567831224224549968)
XLA Ops:
  9.1 7.4 %route.1 = (s32[272,128]{1,0:T(8,128)}, s32[144,128]{1,0:T(8,128)S(1)}, s32[144,128]{1,0:T(8,128)S(1)}) custom-call(s32[1]{0:T(128)} %bitcast.1.batch_ref, s32[130,128]{1,0:T(8,128)S(1)} %bitcast.37, s32[130,128]{1,0:T(8,128)S(1)} %bitcast.38), custom_call_target="tpu_custom_call" | custom-call | flops 10350000128 | bytes 27000000 | tf_op jit(solution)/shard_map/route/pallas_call | solution.py:930
  17.8 7.3 %all-to-all-start = ((s32[8,1,4352]{2,1,0:T(1,128)}), s32[8,1,4352]{2,1,0:T(1,128)S(1)}, u32[]{:S(2)}, u32[]{:S(2)}) async-start(s32[8,1,4352]{2,1,0:T(1,128)} %bitcast.3), calls=%async_computation | async-start | bytes 278528 | tf_op jit(solution)/shard_map/all_to_all | solution.py:916
  25.1 6.2 %pack.1 = (f32[8208,128]{1,0:T(8,128)}, bf16[1296,128]{1,0:T(8,128)(2,1)}) custom-call(bf16[16,65536]{1,0:T(8,128)(2,1)} %bitcast.53, bf16[1,512,256]{2,1,0:T(8,128)(2,1)} %hidden_w_ref.1, bf16[1,256,128]{2,1,0:T(8,128)(2,1)} %output_w_ref.1, f32[1,256]{1,0:T(1,128)} %hidden_b_ref, f32[1,128]{1,0:T(1,128)} %output_b_ref.1), custom_call_target="tpu_custom_call" | custom-call | flops 5750000128 | bytes 15000000 | tf_op jit(solution)/shard_map/pack/pallas_call | solution.py:946
  33.2 15.6 %fetch.3 = bf16[2176,128]{1,0:T(8,128)(2,1)} custom-call(s32[34816]{0:T(1024)} %bitcast_add_fusion.request_ref, s32[272,128]{1,0:T(8,128)} %bitcast.34, f32[8208,128]{1,0:T(8,128)} %get-tuple-element.81.far_table_ref), custom_call_target="tpu_custom_call" | custom-call | flops 13799999488 | bytes 36000000 | tf_op jit(solution)/shard_map/fetch/pallas_call | solution.py:964
  48.9 5.8 %all-to-all-start.2 = ((bf16[8,272,128]{2,1,0:T(8,128)(2,1)}), bf16[8,272,128]{2,1,0:T(8,128)(2,1)S(1)}, u32[]{:S(2)}, u32[]{:S(2)}) async-start(bf16[8,272,128]{2,1,0:T(8,128)(2,1)} %bitcast.49), calls=%async_computation.2 | async-start | bytes 1114112 | tf_op jit(solution)/shard_map/all_to_all | solution.py:916
  54.6 15.6 %fetch.2 = bf16[2176,128]{1,0:T(8,128)(2,1)} custom-call(s32[34816]{0:T(1024)} %bitcast_add_fusion.request_ref, s32[272,128]{1,0:T(8,128)} %bitcast.35, f32[8208,128]{1,0:T(8,128)} %get-tuple-element.81.far_table_ref), custom_call_target="tpu_custom_call" | custom-call | flops 13799999488 | bytes 36000000 | tf_op jit(solution)/shard_map/fetch/pallas_call | solution.py:964
  70.3 6.3 %all-to-all-start.1 = ((bf16[8,272,128]{2,1,0:T(8,128)(2,1)}), bf16[8,272,128]{2,1,0:T(8,128)(2,1)S(1)}, u32[]{:S(2)}, u32[]{:S(2)}) async-start(bf16[8,272,128]{2,1,0:T(8,128)(2,1)} %bitcast.48), calls=%async_computation.1 | async-start | bytes 1114112 | tf_op jit(solution)/shard_map/all_to_all | solution.py:916
  76.6 9.4 %unpermute.1.refs_0_ = bf16[320,512]{1,0:T(8,128)(2,1)} custom-call(s32[18432]{0:T(1024)} %bitcast.39, bf16[2176,128]{1,0:T(8,128)(2,1)} %bitcast.47), custom_call_target="tpu_custom_call" | custom-call | flops 17250000896 | bytes 45000000 | tf_op jit(solution)/shard_map/unpermute/pallas_call | solution.py:984
  86.0 4.8 %all-to-all-done.1 = bf16[8,272,128]{2,1,0:T(8,128)(2,1)S(1)} async-done(((bf16[8,272,128]{2,1,0:T(8,128)(2,1)}), bf16[8,272,128]{2,1,0:T(8,128)(2,1)S(1)}, u32[]{:S(2)}, u32[]{:S(2)}) %all-to-all-start.1) | async-done | bytes 557088 | tf_op jit(solution)/shard_map/all_to_all | solution.py:916
  91.6 36.4 %dense.1 = (bf16[544,128]{1,0:T(8,128)(2,1)}, bf16[544,128]{1,0:T(8,128)(2,1)}, bf16[544,128]{1,0:T(8,128)(2,1)}, bf16[544,128]{1,0:T(8,128)(2,1)}, bf16[544,128...) custom-call(s32[18432]{0:T(1024)} %bitcast.40, ...), custom_call_target="tpu_custom_call" | custom-call | flops 51749998592 | bytes 135000000 | tf_op jit(solution)/shard_map/dense/pallas_call | solution.py:998
  129.7 2.1 collective-permute-start.1
  132.5 3.0 %collective-permute-start.4 = (bf16[544,128]{1,0:T(8,128)(2,1)}, bf16[544,128]{1,0:T(8,128)(2,1)S(1)}, u32[]{:S(2)}, u32[]{:S(2)}) collective-permute-start(bf16[544,128]{1,0:T(8,128)(2,1)} %get-tuple-element.92), channel_id=1, source_target_pairs={{0,20},{4,16},{8,28},{12,24},{16,4},{20,0},{24,12},{28,8},{1,21},{... | collective-permute-start | bytes 417800 | tf_op jit(solution)/shard_map/ppermute | solution.py:920
  136.3 2.3 collective-permute-start.5
  142.5 2.8 %collective-permute-start.6 = (bf16[544,128]{1,0:T(8,128)(2,1)S(1)}, bf16[544,128]{1,0:T(8,128)(2,1)S(1)}, u32[]{:S(2)}, u32[]{:S(2)}) collective-permute-start(bf16[544,128]{1,0:T(8,128)(2,1)S(1)} %copy-done.11), channel_id=1, source_target_pairs={{0,28},{4,24},{8,20},{12,16},{16,12},{20,8},{24,4},{28,0},{1,29},{... | collective-permute-start | bytes 417800 | tf_op jit(solution)/shard_map/ppermute | solution.py:920
  146.7 1.7 collective-permute-done.4.refs_5_
  148.4 4.8 %all-to-all-start.3 = ((bf16[32,192,128]{2,1,0:T(8,128)(2,1)}), bf16[32,192,128]{2,1,0:T(8,128)(2,1)}, u32[]{:S(2)}, u32[]{:S(2)}) async-start(bf16[32,192,128]{2,1,0:T(8,128)(2,1)} %bitcast.42), calls=%async_computation.3 | async-start | bytes 3145728 | tf_op jit(solution)/shard_map/all_to_all | solution.py:916
  153.3 34.1 %add.42 = (bf16[16,16384]{1,0:T(8,128)(2,1)S(1)}, bf16[16,16384]{1,0:T(8,128)(2,1)S(1)}, bf16[16,16384]{1,0:T(8,128)(2,1)S(1)}, bf16[16,16384]{1,0:T(8,128)(2,1)S(1)}) custom-call(s32[2]{0:T(128)S(1)} %pad_add_fusion.index_ref, s32[34816]{0:T(1024)S(1)} %copy-done.2, s32[272,128]{1,0:T(8,128)S(1)} %bitcast.36, bf16[544,128]{1,0:T(8,128)(2,1)S(1)} %copy-done.6, ...), custom_call_target="tpu_custom_call" | custom-call | flops 69000003584 | bytes 180000000 | tf_op jit(solution)/shard_map/add/pallas_call | solution.py:1079
  187.4 3.4 %all-to-all-done.3 = bf16[32,192,128]{2,1,0:T(8,128)(2,1)} async-done(((bf16[32,192,128]{2,1,0:T(8,128)(2,1)}), bf16[32,192,128]{2,1,0:T(8,128)(2,1)}, u32[]{:S(2)}, u32[]{:S(2)}) %all-to-all-start.3) | async-done | bytes 1572896 | tf_op jit(solution)/shard_map/all_to_all | solution.py:916
  193.5 1.5 collective-permute-start.9
  195.0 1.6 convert_reduce_fusion
  197.5 7.1 %all-to-all-start.4 = ((bf16[8,224,128]{2,1,0:T(8,128)(2,1)}), bf16[8,224,128]{2,1,0:T(8,128)(2,1)S(1)}, u32[]{:S(2)}, u32[]{:S(2)}) async-start(bf16[8,224,128]{2,1,0:T(8,128)(2,1)} %broadcast_in_dim.8), calls=%async_computation.4 | async-start | bytes 917504 | tf_op jit(solution)/shard_map/all_to_all | solution.py:916
  205.0 3.1 %collective-permute-done.9 = bf16[16,16384]{1,0:T(8,128)(2,1)S(1)} collective-permute-done((bf16[16,16384]{1,0:T(8,128)(2,1)S(1)}, bf16[16,16384]{1,0:T(8,128)(2,1)S(1)}, u32[]{:S(2)}, u32[]{:S(2)}) %collective-permute-start.9) | collective-permute-done | bytes 524320 | tf_op jit(solution)/shard_map/ppermute | solution.py:920
  208.3 10.4 %collective-permute-done.11 = bf16[16,16384]{1,0:T(8,128)(2,1)S(1)} collective-permute-done((bf16[16,16384]{1,0:T(8,128)(2,1)S(1)}, bf16[16,16384]{1,0:T(8,128)(2,1)S(1)}, u32[]{:S(2)}, u32[]{:S(2)}) %collective-permute-start.11) | collective-permute-done | bytes 524320 | tf_op jit(solution)/shard_map/ppermute | solution.py:920
  222.3 2.3 convert_bitcast_fusion
  (77 shorter events, 21.9 us)
Async XLA Ops:
  17.8 14.7 %all-to-all-start = ((s32[8,1,4352]{2,1,0:T(1,128)}), s32[8,1,4352]{2,1,0:T(1,128)S(1)}, u32[]{:S(2)}, u32[]{:S(2)}) async-start(s32[8,1,4352]{2,1,0:T(1,128)} %bitcast.3), calls=%async_computation | async-start | bytes 278528 | tf_op jit(solution)/shard_map/all_to_all | solution.py:916
  25.0 65.8 %all-gather.3.cloned.1.call-start = ((), (), s32[]{:S(2)}) async-start(), calls=%async_computation.5 | async-start | bytes 1658880 | tf_op jit(solution)/shard_map/all_gather | solution.py:958
  48.9 21.4 %all-to-all-start.2 = ((bf16[8,272,128]{2,1,0:T(8,128)(2,1)}), bf16[8,272,128]{2,1,0:T(8,128)(2,1)S(1)}, u32[]{:S(2)}, u32[]{:S(2)}) async-start(bf16[8,272,128]{2,1,0:T(8,128)(2,1)} %bitcast.49), calls=%async_computation.2 | async-start | bytes 1114112 | tf_op jit(solution)/shard_map/all_to_all | solution.py:916
  70.3 6.4 %copy-start.8 = (bf16[8,272,128]{2,1,0:T(8,128)(2,1)}, bf16[8,272,128]{2,1,0:T(8,128)(2,1)S(1)}, u32[]{:S(2)}) copy-start(bf16[8,272,128]{2,1,0:T(8,128)(2,1)S(1)} %all-to-all-done.2) | copy-start | bytes 1671172
  70.3 20.6 %all-to-all-start.1 = ((bf16[8,272,128]{2,1,0:T(8,128)(2,1)}), bf16[8,272,128]{2,1,0:T(8,128)(2,1)S(1)}, u32[]{:S(2)}, u32[]{:S(2)}) async-start(bf16[8,272,128]{2,1,0:T(8,128)(2,1)} %bitcast.48), calls=%async_computation.1 | async-start | bytes 1114112 | tf_op jit(solution)/shard_map/all_to_all | solution.py:916
  128.1 14.4 %copy-start.11 = (bf16[544,128]{1,0:T(8,128)(2,1)S(1)}, bf16[544,128]{1,0:T(8,128)(2,1)}, u32[]{:S(2)}) copy-start(bf16[544,128]{1,0:T(8,128)(2,1)} %get-tuple-element.103) | copy-start | bytes 417796
  128.1 8.2 %collective-permute-start.3 = (bf16[544,128]{1,0:T(8,128)(2,1)}, bf16[544,128]{1,0:T(8,128)(2,1)S(1)}, u32[]{:S(2)}, u32[]{:S(2)}) collective-permute-start(bf16[544,128]{1,0:T(8,128)(2,1)} %get-tuple-element.87), channel_id=1, source_target_pairs={{0,16},{4,20},{8,24},{12,28},{16,0},{20,4},{24,8},{28,12},{1,17},{... | collective-permute-start | bytes 417800 | tf_op jit(solution)/shard_map/ppermute | solution.py:920
  129.0 13.5 %collective-permute-start = (bf16[544,128]{1,0:T(8,128)(2,1)}, bf16[544,128]{1,0:T(8,128)(2,1)S(1)}, u32[]{:S(2)}, u32[]{:S(2)}) collective-permute-start(bf16[544,128]{1,0:T(8,128)(2,1)} %get-tuple-element.84), channel_id=1, source_target_pairs={{0,4},{4,0},{8,12},{12,8},{16,20},{20,16},{24,28},{28,24},{1,5},{5... | collective-permute-start | bytes 417800 | tf_op jit(solution)/shard_map/ppermute | solution.py:920
  129.7 17.0 %collective-permute-start.1 = (bf16[544,128]{1,0:T(8,128)(2,1)}, bf16[544,128]{1,0:T(8,128)(2,1)S(1)}, u32[]{:S(2)}, u32[]{:S(2)}) collective-permute-start(bf16[544,128]{1,0:T(8,128)(2,1)} %get-tuple-element.85), channel_id=1, source_target_pairs={{0,8},{4,12},{8,0},{12,4},{16,24},{20,28},{24,16},{28,20},{1,9},{5... | collective-permute-start | bytes 417800 | tf_op jit(solution)/shard_map/ppermute | solution.py:920
  131.8 14.9 %collective-permute-start.2 = (bf16[544,128]{1,0:T(8,128)(2,1)}, bf16[544,128]{1,0:T(8,128)(2,1)S(1)}, u32[]{:S(2)}, u32[]{:S(2)}) collective-permute-start(bf16[544,128]{1,0:T(8,128)(2,1)} %get-tuple-element.86), channel_id=1, source_target_pairs={{0,12},{4,8},{8,4},{12,0},{16,28},{20,24},{24,20},{28,16},{1,13},{... | collective-permute-start | bytes 417800 | tf_op jit(solution)/shard_map/ppermute | solution.py:920
  132.5 15.9 %collective-permute-start.4 = (bf16[544,128]{1,0:T(8,128)(2,1)}, bf16[544,128]{1,0:T(8,128)(2,1)S(1)}, u32[]{:S(2)}, u32[]{:S(2)}) collective-permute-start(bf16[544,128]{1,0:T(8,128)(2,1)} %get-tuple-element.92), channel_id=1, source_target_pairs={{0,20},{4,16},{8,28},{12,24},{16,4},{20,0},{24,12},{28,8},{1,21},{... | collective-permute-start | bytes 417800 | tf_op jit(solution)/shard_map/ppermute | solution.py:920
  136.3 16.9 %collective-permute-start.5 = (bf16[544,128]{1,0:T(8,128)(2,1)}, bf16[544,128]{1,0:T(8,128)(2,1)S(1)}, u32[]{:S(2)}, u32[]{:S(2)}) collective-permute-start(bf16[544,128]{1,0:T(8,128)(2,1)} %get-tuple-element.102), channel_id=1, source_target_pairs={{0,24},{4,28},{8,16},{12,20},{16,8},{20,12},{24,0},{28,4},{1,25},{... | collective-permute-start | bytes 417800 | tf_op jit(solution)/shard_map/ppermute | solution.py:920
  142.5 10.7 %collective-permute-start.6 = (bf16[544,128]{1,0:T(8,128)(2,1)S(1)}, bf16[544,128]{1,0:T(8,128)(2,1)S(1)}, u32[]{:S(2)}, u32[]{:S(2)}) collective-permute-start(bf16[544,128]{1,0:T(8,128)(2,1)S(1)} %copy-done.11), channel_id=1, source_target_pairs={{0,28},{4,24},{8,20},{12,16},{16,12},{20,8},{24,4},{28,0},{1,29},{... | collective-permute-start | bytes 417800 | tf_op jit(solution)/shard_map/ppermute | solution.py:920
  146.7 6.6 %copy-start.1 = (s32[8,1,4352]{2,1,0:T(1,128)S(1)}, s32[8,1,4352]{2,1,0:T(1,128)}, u32[]{:S(2)}) copy-start(s32[8,1,4352]{2,1,0:T(1,128)} %copy-done) | copy-start | bytes 417796
  146.7 6.6 %copy-start.2 = (s32[34816]{0:T(1024)S(1)}, s32[34816]{0:T(1024)}, u32[]{:S(2)}) copy-start(s32[34816]{0:T(1024)} %bitcast_add_fusion.request_ref) | copy-start | bytes 417796
  146.7 6.6 %copy-start.6 = (bf16[544,128]{1,0:T(8,128)(2,1)S(1)}, bf16[544,128]{1,0:T(8,128)(2,1)}, u32[]{:S(2)}) copy-start(bf16[544,128]{1,0:T(8,128)(2,1)} %get-tuple-element.96.refs_0_) | copy-start | bytes 417796
  148.4 42.3 %all-to-all-start.3 = ((bf16[32,192,128]{2,1,0:T(8,128)(2,1)}), bf16[32,192,128]{2,1,0:T(8,128)(2,1)}, u32[]{:S(2)}, u32[]{:S(2)}) async-start(bf16[32,192,128]{2,1,0:T(8,128)(2,1)} %bitcast.42), calls=%async_computation.3 | async-start | bytes 3145728 | tf_op jit(solution)/shard_map/all_to_all | solution.py:916
  190.7 1.9 collective-permute-start.7
  190.7 2.7 %collective-permute-start.8 = (bf16[16,16384]{1,0:T(8,128)(2,1)S(1)}, bf16[16,16384]{1,0:T(8,128)(2,1)S(1)}, u32[]{:S(2)}, u32[]{:S(2)}) collective-permute-start(bf16[16,16384]{1,0:T(8,128)(2,1)S(1)} %get-tuple-element.112), channel_id=1, source_target_pairs={{0,1},{1,0},{2,3},{3,2},{4,5},{5,4},{6,7},{7,6},{8,9},{9,8},{10,11... | collective-permute-start | bytes 1572872 | tf_op jit(solution)/shard_map/ppermute | solution.py:920
  193.5 14.6 %collective-permute-start.9 = (bf16[16,16384]{1,0:T(8,128)(2,1)S(1)}, bf16[16,16384]{1,0:T(8,128)(2,1)S(1)}, u32[]{:S(2)}, u32[]{:S(2)}) collective-permute-start(bf16[16,16384]{1,0:T(8,128)(2,1)S(1)} %add_convert_fusion.3), channel_id=1, source_target_pairs={{0,2},{1,3},{2,0},{3,1},{4,6},{5,7},{6,4},{7,5},{8,10},{9,11},{10,... | collective-permute-start | bytes 1572872 | tf_op jit(solution)/shard_map/ppermute | solution.py:920
  197.5 21.5 %all-to-all-start.4 = ((bf16[8,224,128]{2,1,0:T(8,128)(2,1)}), bf16[8,224,128]{2,1,0:T(8,128)(2,1)S(1)}, u32[]{:S(2)}, u32[]{:S(2)}) async-start(bf16[8,224,128]{2,1,0:T(8,128)(2,1)} %broadcast_in_dim.8), calls=%async_computation.4 | async-start | bytes 917504 | tf_op jit(solution)/shard_map/all_to_all | solution.py:916
  204.6 14.2 %collective-permute-start.11 = (bf16[16,16384]{1,0:T(8,128)(2,1)S(1)}, bf16[16,16384]{1,0:T(8,128)(2,1)S(1)}, u32[]{:S(2)}, u32[]{:S(2)}) collective-permute-start(bf16[16,16384]{1,0:T(8,128)(2,1)S(1)} %add_convert_fusion.2), channel_id=1, source_target_pairs={{0,2},{1,3},{2,0},{3,1},{4,6},{5,7},{6,4},{7,5},{8,10},{9,11},{10,... | collective-permute-start | bytes 1572872 | tf_op jit(solution)/shard_map/ppermute | solution.py:920
  208.3 11.7 %collective-permute-start.10 = (bf16[16,16384]{1,0:T(8,128)(2,1)S(1)}, bf16[16,16384]{1,0:T(8,128)(2,1)S(1)}, u32[]{:S(2)}, u32[]{:S(2)}) collective-permute-start(bf16[16,16384]{1,0:T(8,128)(2,1)S(1)} %add_convert_fusion.1), channel_id=1, source_target_pairs={{0,1},{1,0},{2,3},{3,2},{4,5},{5,4},{6,7},{7,6},{8,9},{9,8},{10,11... | collective-permute-start | bytes 1572872 | tf_op jit(solution)/shard_map/ppermute | solution.py:920
  218.9 2.1 collective-permute-start.12
  (7 other events, 16.4 us)
Sparse Core Ops, SparseCore 0:
  31.5 19.6 all-gather.2

commit v6 on v2

--- a/solution.py
+++ b/solution.py
@@ -291,19 +291,20 @@
     group = lax.shift_right_logical(iota((8, LANES), 1), 4)
     bits = [(group & (1 << bit)) != 0 for bit in range(3)]
 
-    def turn_step(source, carry):
-        at = (source * PARTS + part) * chunks
-        numbers = lax.shift_right_logical(asked_ref[pl.ds(at, chunks), :], table_lanes)
-        turn_ref[pl.ds(aligned(source * packed, 16), packed), :] = matmul(
-            slot_lines(numbers.astype(F32)), within
-        )
-        return carry
+    def make_turns(source, first, count):
+        at = (source * PARTS + part) * chunks + first
+        numbers = lax.shift_right_logical(asked_ref[pl.ds(at, count), :], table_lanes)
+        start = aligned(source * packed + first * 16, 16)
+        turn_ref[pl.ds(start, count * 16), :] = matmul(slot_lines(numbers.astype(F32)), within)
 
     def before():
-        lax.fori_loop(0, owners, turn_step, 0, unroll=4)
+        make_turns(0, 0, chunks)
 
     def process(source, words):
+        later = jnp.minimum(source + 1, owners - 1)
         for chunk in range(chunks):
+            if chunk % 4 == 0:
+                make_turns(later, chunk, min(4, chunks - chunk))
             for line in range(LANES):
                 base = chunk * LANES + line // 8 * 8
                 pltpu.store(
@@ -917,9 +918,7 @@
         return lax.ppermute(values, axis, [(one, one ^ bits) for one in range(size)])
 
     def swap_all(blocks):
-        order = sorted(range(1, owners), key=lambda bits: (-bits.bit_length(), bits))
-        moved = {bits: swap(blocks[bits], "batch", bits) for bits in order}
-        return [blocks[0]] + [moved[bits] for bits in range(1, owners)]
+        return [blocks[0]] + [swap(blocks[bits], "batch", bits) for bits in range(1, owners)]
 
     owner_list = row_owner.reshape(lookup_rows, LANES)
     local_list = local_row.reshape(lookup_rows, LANES)
@@ -1042,8 +1041,9 @@
         high = lax.reduce_precision(values, exponent_bits=8, mantissa_bits=7)
         return high.astype(BF16), (values - high).astype(BF16)
 
-    received[1], grad_weight, grad_bias, grad_shared = tie(
-        received[1], grad_weight, grad_bias, grad_shared
+    far = owners // 2
+    received[far], grad_weight, grad_bias, grad_shared = tie(
+        received[far], grad_weight, grad_bias, grad_shared
     )
 
     def spread_rows(values, piece):
@@ -1091,15 +1091,17 @@
         add_low(one, swap(other, "expert", 1))
         for one, other in zip(table_part[:TABLE_CHUNKS], table_part[TABLE_CHUNKS:])
     ]
+    *kept, pieces = tie(*kept, pieces)
+    over = [swap(one, "expert", 2) for one in kept]
     sums = jnp.sum(pieces.astype(F32), axis=0)
     piece = jnp.concatenate([sums[:weight_piece].astype(BF16), *split(sums[weight_piece:])], axis=0)
-    *kept, piece = tie(*kept, piece)
     pieces = exchange(jnp.broadcast_to(piece[None], (owners, *piece.shape)), "batch")
-
     bit = 2
     while bit < experts:
-        kept = [add_low(one, swap(one, "expert", bit)) for one in kept]
+        kept = [add_low(one, other) for one, other in zip(kept, over)]
         bit *= 2
+        if bit < experts:
+            over = [swap(one, "expert", bit) for one in kept]
     small = call(
         functools.partial(unpack_kernel, weight_piece, extra_piece, pairs),
         tuple(

time: 235 us -> 230 us (0.979); the launches traced: 234 us -> 227 us
  waiting for transfers between devices: 37.4 us -> 26 us
  starting transfers between devices: 39.6 us -> 45.1 us
    ppermute x13, waiting for transfers between devices: 30.1 us -> 18.5 us  [swap(): lax.ppermute(values, axis, [(one, one ^ bits) for one in range(size)])]
    all_to_all x5, starting transfers between devices: 25.3 us -> 29.5 us  [exchange(): return lax.all_to_all(values, axis, split_axis=0, concat_axis=0, tiled=True)]
  transfers between devices with their start and end apart: 19 -> 19, of which waited for: 8 -> 10; matrix products, arithmetic and copies ran while one was open for 4% -> 4% of each run, Pallas kernels for 33% -> 33%
where the time goes in v6:
time: 230 us; the launch traced here: 227 us
  Pallas kernels  120 us (52%)
  starting transfers between devices  45.1 us (20%)
  waiting for transfers between devices  26 us (11%)
  between operations  14.4 us (6%)
  local copies, waits for them, and re-layouts  12.6 us (5%)
  other arithmetic  8.74 us (4%)
    pallas_call x1, Pallas kernels, shards(): call(functools.partial(add_kernel, owners, packed, table_lanes), (jax.Sha...  37.3 us
    pallas_call x1, Pallas kernels, shards(): call(functools.partial(dense_kernel, owners, part_rows, experts, scale),...  36.4 us
    all_to_all x5, starting transfers between devices, exchange(): return lax.all_to_all(values, axis, split_axis=0, concat_axis=0, tiled=True)  29.5 us
    pallas_call x2, Pallas kernels, shards(): call(functools.partial(fetch_kernel, owners, part, packed, table_lanes),...  27.1 us
    ppermute x13, waiting for transfers between devices, swap(): lax.ppermute(values, axis, [(one, one ^ bits) for one in range(size)])  18.5 us
    ppermute x13, starting transfers between devices, swap(): lax.ppermute(values, axis, [(one, one ^ bits) for one in range(size)])  15.5 us
    unnamed x34, local copies, waits for them, and re-layouts  8.81 us
    pallas_call x1, Pallas kernels, shards(): call(functools.partial(unpermute_kernel, part, part_rows), jax.ShapeDtype...  7.58 us
  transfers between devices with their start and end apart: 19, of which 10 were waited for; matrix products, arithmetic and copies ran while one was open for 4% of the time, Pallas kernels for 33%

profile of v6, /device:TPU:0, one launch (start us, length us, event | category | flops | bytes accessed | tf_op | source)
XLA Modules:
  0.0 226.6 jit_solution(1217335570859889251)
XLA Ops:
  9.1 7.4 %route.1 = (s32[272,128]{1,0:T(8,128)}, s32[144,128]{1,0:T(8,128)S(1)}, s32[144,128]{1,0:T(8,128)S(1)}) custom-call(s32[1]{0:T(128)} %bitcast.1.batch_ref, s32[130,128]{1,0:T(8,128)S(1)} %bitcast.38, s32[130,128]{1,0:T(8,128)S(1)} %bitcast.40), custom_call_target="tpu_custom_call" | custom-call | flops 10350000128 | bytes 27000000 | tf_op jit(solution)/shard_map/route/pallas_call | solution.py:928
  16.6 7.3 %all-to-all-start = ((s32[8,1,4352]{2,1,0:T(1,128)}), s32[8,1,4352]{2,1,0:T(1,128)S(1)}, u32[]{:S(2)}, u32[]{:S(2)}) async-start(s32[8,1,4352]{2,1,0:T(1,128)} %bitcast.3), calls=%async_computation | async-start | bytes 278528 | tf_op jit(solution)/shard_map/all_to_all | solution.py:914
  23.9 3.1 %pack.1 = (f32[8208,128]{1,0:T(8,128)S(1)}, bf16[1296,128]{1,0:T(8,128)(2,1)}) custom-call(bf16[16,65536]{1,0:T(8,128)(2,1)S(1)} %bitcast.39, bf16[1,512,256]{2,1,0:T(8,128)(2,1)S(1)} %copy-done.1, bf16[1,256,128]{2,1,0:T(8,128)(2,1)S(1)} %copy-done.3, f32[1,256]{1,0:T(1,128)S(1)} %copy-done.4, f32[1,128]{1,0:T(1,128)S(1)} %copy-done.5), custom_call_target="tpu_custom_call" | custom-call | flops 5750000128 | bytes 15000000 | tf_op jit(solution)/shard_map/pack/pallas_call | solution.py:944
  27.0 2.0 copy-done.8
  31.4 2.2 copy-done.9
  33.6 13.5 %fetch.3 = bf16[2176,128]{1,0:T(8,128)(2,1)} custom-call(s32[34816]{0:T(1024)S(1)} %bitcast_add_fusion.request_ref, s32[272,128]{1,0:T(8,128)S(1)} %bitcast.35, f32[8208,128]{1,0:T(8,128)S(1)} %copy-done.9), custom_call_target="tpu_custom_call" | custom-call | flops 13799999488 | bytes 36000000 | tf_op jit(solution)/shard_map/fetch/pallas_call | solution.py:962
  47.1 4.5 %all-to-all-start.2 = ((bf16[8,272,128]{2,1,0:T(8,128)(2,1)}), bf16[8,272,128]{2,1,0:T(8,128)(2,1)S(1)}, u32[]{:S(2)}, u32[]{:S(2)}) async-start(bf16[8,272,128]{2,1,0:T(8,128)(2,1)} %bitcast.16), calls=%async_computation.2 | async-start | bytes 1114112 | tf_op jit(solution)/shard_map/all_to_all | solution.py:914
  51.6 2.2 copy-done.10
  53.8 13.5 %fetch.2 = bf16[2176,128]{1,0:T(8,128)(2,1)} custom-call(s32[34816]{0:T(1024)S(1)} %bitcast_add_fusion.request_ref, s32[272,128]{1,0:T(8,128)S(1)} %bitcast.36, f32[8208,128]{1,0:T(8,128)S(1)} %copy-done.10), custom_call_target="tpu_custom_call" | custom-call | flops 13799999488 | bytes 36000000 | tf_op jit(solution)/shard_map/fetch/pallas_call | solution.py:962
  67.4 6.1 %all-to-all-start.1 = ((bf16[8,272,128]{2,1,0:T(8,128)(2,1)}), bf16[8,272,128]{2,1,0:T(8,128)(2,1)S(1)}, u32[]{:S(2)}, u32[]{:S(2)}) async-start(bf16[8,272,128]{2,1,0:T(8,128)(2,1)} %bitcast.10), calls=%async_computation.1 | async-start | bytes 1114112 | tf_op jit(solution)/shard_map/all_to_all | solution.py:914
  73.5 7.6 %unpermute.1.refs_0_ = bf16[320,512]{1,0:T(8,128)(2,1)S(1)} custom-call(s32[18432]{0:T(1024)S(1)} %bitcast.41, bf16[2176,128]{1,0:T(8,128)(2,1)S(1)} %bitcast.34), custom_call_target="tpu_custom_call" | custom-call | flops 17250000896 | bytes 45000000 | tf_op jit(solution)/shard_map/unpermute/pallas_call | solution.py:979
  81.8 5.7 %all-to-all-done.1 = bf16[8,272,128]{2,1,0:T(8,128)(2,1)S(1)} async-done(((bf16[8,272,128]{2,1,0:T(8,128)(2,1)}), bf16[8,272,128]{2,1,0:T(8,128)(2,1)S(1)}, u32[]{:S(2)}, u32[]{:S(2)}) %all-to-all-start.1) | async-done | bytes 557088 | tf_op jit(solution)/shard_map/all_to_all | solution.py:914
  88.3 36.4 %dense.1 = (bf16[544,128]{1,0:T(8,128)(2,1)}, bf16[544,128]{1,0:T(8,128)(2,1)}, bf16[544,128]{1,0:T(8,128)(2,1)}, bf16[544,128]{1,0:T(8,128)(2,1)}, bf16[544,128...) custom-call(s32[18432]{0:T(1024)} %bitcast.42, ...), custom_call_target="tpu_custom_call" | custom-call | flops 51749998592 | bytes 135000000 | tf_op jit(solution)/shard_map/dense/pallas_call | solution.py:992
  126.4 2.1 collective-permute-start.1
  129.2 3.0 %collective-permute-start.4 = (bf16[544,128]{1,0:T(8,128)(2,1)}, bf16[544,128]{1,0:T(8,128)(2,1)S(1)}, u32[]{:S(2)}, u32[]{:S(2)}) collective-permute-start(bf16[544,128]{1,0:T(8,128)(2,1)} %get-tuple-element.92), channel_id=1, source_target_pairs={{0,20},{4,16},{8,28},{12,24},{16,4},{20,0},{24,12},{28,8},{1,21},{... | collective-permute-start | bytes 417800 | tf_op jit(solution)/shard_map/ppermute | solution.py:918
  132.9 2.3 %collective-permute-start.5 = (bf16[544,128]{1,0:T(8,128)(2,1)}, bf16[544,128]{1,0:T(8,128)(2,1)S(1)}, u32[]{:S(2)}, u32[]{:S(2)}) collective-permute-start(bf16[544,128]{1,0:T(8,128)(2,1)} %get-tuple-element.102), channel_id=1, source_target_pairs={{0,24},{4,28},{8,16},{12,20},{16,8},{20,12},{24,0},{28,4},{1,25},{... | collective-permute-start | bytes 417800 | tf_op jit(solution)/shard_map/ppermute | solution.py:918
  139.2 2.8 %collective-permute-start.6 = (bf16[544,128]{1,0:T(8,128)(2,1)S(1)}, bf16[544,128]{1,0:T(8,128)(2,1)S(1)}, u32[]{:S(2)}, u32[]{:S(2)}) collective-permute-start(bf16[544,128]{1,0:T(8,128)(2,1)S(1)} %copy-done.16), channel_id=1, source_target_pairs={{0,28},{4,24},{8,20},{12,16},{16,12},{20,8},{24,4},{28,0},{1,29},{... | collective-permute-start | bytes 417800 | tf_op jit(solution)/shard_map/ppermute | solution.py:918
  143.3 1.8 collective-permute-done.4.refs_5_
  145.1 4.0 %all-to-all-start.3 = ((bf16[32,192,128]{2,1,0:T(8,128)(2,1)}), bf16[32,192,128]{2,1,0:T(8,128)(2,1)}, u32[]{:S(2)}, u32[]{:S(2)}) async-start(bf16[32,192,128]{2,1,0:T(8,128)(2,1)} %bitcast.44), calls=%async_computation.3 | async-start | bytes 3145728 | tf_op jit(solution)/shard_map/all_to_all | solution.py:914
  149.2 37.3 %add.42 = (bf16[16,16384]{1,0:T(8,128)(2,1)S(1)}, bf16[16,16384]{1,0:T(8,128)(2,1)S(1)}, bf16[16,16384]{1,0:T(8,128)(2,1)S(1)}, bf16[16,16384]{1,0:T(8,128)(2,1)S(1)}) custom-call(s32[2]{0:T(128)S(1)} %pad_add_fusion.index_ref, s32[34816]{0:T(1024)S(1)} %bitcast_add_fusion.request_ref, s32[272,128]{1,0:T(8,128)S(1)} %bitcast.37, ...), custom_call_target="tpu_custom_call" | custom-call | flops 69000003584 | bytes 180000000 | tf_op jit(solution)/shard_map/add/pallas_call | solution.py:1073
  193.6 7.6 %all-to-all-start.4 = ((bf16[8,224,128]{2,1,0:T(8,128)(2,1)}), bf16[8,224,128]{2,1,0:T(8,128)(2,1)S(1)}, u32[]{:S(2)}, u32[]{:S(2)}) async-start(bf16[8,224,128]{2,1,0:T(8,128)(2,1)} %broadcast_in_dim.8), calls=%async_computation.4 | async-start | bytes 917504 | tf_op jit(solution)/shard_map/all_to_all | solution.py:914
  202.0 2.4 %collective-permute-done.9 = bf16[16,16384]{1,0:T(8,128)(2,1)S(1)} collective-permute-done((bf16[16,16384]{1,0:T(8,128)(2,1)S(1)}, bf16[16,16384]{1,0:T(8,128)(2,1)S(1)}, u32[]{:S(2)}, u32[]{:S(2)}) %collective-permute-start.9) | collective-permute-done | bytes 524320 | tf_op jit(solution)/shard_map/ppermute | solution.py:918
  204.5 10.6 %collective-permute-done.11 = bf16[16,16384]{1,0:T(8,128)(2,1)S(1)} collective-permute-done((bf16[16,16384]{1,0:T(8,128)(2,1)S(1)}, bf16[16,16384]{1,0:T(8,128)(2,1)S(1)}, u32[]{:S(2)}, u32[]{:S(2)}) %collective-permute-start.11) | collective-permute-done | bytes 524320 | tf_op jit(solution)/shard_map/ppermute | solution.py:918
  217.4 2.3 %convert_bitcast_fusion = f32[65536,16]{0,1:T(8,128)} fusion(bf16[16,16384]{1,0:T(8,128)(2,1)S(1)} %get-tuple-element.143, bf16[16,16384]{1,0:T(8,128)(2,1)S(1)} %get-tuple-element.151, bf16[16,16384]{1,0:T(8,128)(2,1)S(1)} %get-tuple-element.142, bf16[16,16384]{1,0:T(8,128)(2,1)S(1)} %get-tuple-element.152), kind=kLoop, calls=%fused_computation | loop fusion | flops 8388608 | bytes 6291456 | tf_op jit(solution)/shard_map/transpose | solution.py:1134
  (87 shorter events, 24.6 us)
Async XLA Ops:
  9.1 14.8 %copy-start.1 = (bf16[1,512,256]{2,1,0:T(8,128)(2,1)S(1)}, bf16[1,512,256]{2,1,0:T(8,128)(2,1)}, u32[]{:S(2)}) copy-start(bf16[1,512,256]{2,1,0:T(8,128)(2,1)} %hidden_w_ref.1) | copy-start | bytes 786436
  9.1 14.8 %copy-start.3 = (bf16[1,256,128]{2,1,0:T(8,128)(2,1)S(1)}, bf16[1,256,128]{2,1,0:T(8,128)(2,1)}, u32[]{:S(2)}) copy-start(bf16[1,256,128]{2,1,0:T(8,128)(2,1)} %output_w_ref.1) | copy-start | bytes 196612
  9.1 14.8 %copy-start.4 = (f32[1,256]{1,0:T(1,128)S(1)}, f32[1,256]{1,0:T(1,128)}, u32[]{:S(2)}) copy-start(f32[1,256]{1,0:T(1,128)} %hidden_b_ref) | copy-start | bytes 3076
  9.1 14.8 %copy-start.5 = (f32[1,128]{1,0:T(1,128)S(1)}, f32[1,128]{1,0:T(1,128)}, u32[]{:S(2)}) copy-start(f32[1,128]{1,0:T(1,128)} %output_b_ref.1) | copy-start | bytes 1540
  16.6 56.9 %copy-start.6 = (s32[144,128]{1,0:T(8,128)}, s32[144,128]{1,0:T(8,128)S(1)}, u32[]{:S(2)}) copy-start(s32[144,128]{1,0:T(8,128)S(1)} %get-tuple-element.77) | copy-start | bytes 221188
  16.6 14.7 %all-to-all-start = ((s32[8,1,4352]{2,1,0:T(1,128)}), s32[8,1,4352]{2,1,0:T(1,128)S(1)}, u32[]{:S(2)}, u32[]{:S(2)}) async-start(s32[8,1,4352]{2,1,0:T(1,128)} %bitcast.3), calls=%async_computation | async-start | bytes 278528 | tf_op jit(solution)/shard_map/all_to_all | solution.py:914
  23.8 63.6 %all-gather.3.cloned.1.call-start = ((), (), s32[]{:S(2)}) async-start(), calls=%async_computation.5 | async-start | bytes 1658880 | tf_op jit(solution)/shard_map/all_gather | solution.py:956
  47.1 20.2 %all-to-all-start.2 = ((bf16[8,272,128]{2,1,0:T(8,128)(2,1)}), bf16[8,272,128]{2,1,0:T(8,128)(2,1)S(1)}, u32[]{:S(2)}, u32[]{:S(2)}) async-start(bf16[8,272,128]{2,1,0:T(8,128)(2,1)} %bitcast.16), calls=%async_computation.2 | async-start | bytes 1114112 | tf_op jit(solution)/shard_map/all_to_all | solution.py:914
  67.4 20.1 %all-to-all-start.1 = ((bf16[8,272,128]{2,1,0:T(8,128)(2,1)}), bf16[8,272,128]{2,1,0:T(8,128)(2,1)S(1)}, u32[]{:S(2)}, u32[]{:S(2)}) async-start(bf16[8,272,128]{2,1,0:T(8,128)(2,1)} %bitcast.10), calls=%async_computation.1 | async-start | bytes 1114112 | tf_op jit(solution)/shard_map/all_to_all | solution.py:914
  124.7 8.2 %collective-permute-start.3 = (bf16[544,128]{1,0:T(8,128)(2,1)}, bf16[544,128]{1,0:T(8,128)(2,1)S(1)}, u32[]{:S(2)}, u32[]{:S(2)}) collective-permute-start(bf16[544,128]{1,0:T(8,128)(2,1)} %get-tuple-element.87), channel_id=1, source_target_pairs={{0,16},{4,20},{8,24},{12,28},{16,0},{20,4},{24,8},{28,12},{1,17},{... | collective-permute-start | bytes 417800 | tf_op jit(solution)/shard_map/ppermute | solution.py:918
  125.7 13.5 %collective-permute-start = (bf16[544,128]{1,0:T(8,128)(2,1)}, bf16[544,128]{1,0:T(8,128)(2,1)S(1)}, u32[]{:S(2)}, u32[]{:S(2)}) collective-permute-start(bf16[544,128]{1,0:T(8,128)(2,1)} %get-tuple-element.84), channel_id=1, source_target_pairs={{0,4},{4,0},{8,12},{12,8},{16,20},{20,16},{24,28},{28,24},{1,5},{5... | collective-permute-start | bytes 417800 | tf_op jit(solution)/shard_map/ppermute | solution.py:918
  126.4 16.9 %collective-permute-start.1 = (bf16[544,128]{1,0:T(8,128)(2,1)}, bf16[544,128]{1,0:T(8,128)(2,1)S(1)}, u32[]{:S(2)}, u32[]{:S(2)}) collective-permute-start(bf16[544,128]{1,0:T(8,128)(2,1)} %get-tuple-element.85), channel_id=1, source_target_pairs={{0,8},{4,12},{8,0},{12,4},{16,24},{20,28},{24,16},{28,20},{1,9},{5... | collective-permute-start | bytes 417800 | tf_op jit(solution)/shard_map/ppermute | solution.py:918
  128.4 14.9 %collective-permute-start.2 = (bf16[544,128]{1,0:T(8,128)(2,1)}, bf16[544,128]{1,0:T(8,128)(2,1)S(1)}, u32[]{:S(2)}, u32[]{:S(2)}) collective-permute-start(bf16[544,128]{1,0:T(8,128)(2,1)} %get-tuple-element.86), channel_id=1, source_target_pairs={{0,12},{4,8},{8,4},{12,0},{16,28},{20,24},{24,20},{28,16},{1,13},{... | collective-permute-start | bytes 417800 | tf_op jit(solution)/shard_map/ppermute | solution.py:918
  129.2 15.9 %collective-permute-start.4 = (bf16[544,128]{1,0:T(8,128)(2,1)}, bf16[544,128]{1,0:T(8,128)(2,1)S(1)}, u32[]{:S(2)}, u32[]{:S(2)}) collective-permute-start(bf16[544,128]{1,0:T(8,128)(2,1)} %get-tuple-element.92), channel_id=1, source_target_pairs={{0,20},{4,16},{8,28},{12,24},{16,4},{20,0},{24,12},{28,8},{1,21},{... | collective-permute-start | bytes 417800 | tf_op jit(solution)/shard_map/ppermute | solution.py:918
  132.9 16.2 %collective-permute-start.5 = (bf16[544,128]{1,0:T(8,128)(2,1)}, bf16[544,128]{1,0:T(8,128)(2,1)S(1)}, u32[]{:S(2)}, u32[]{:S(2)}) collective-permute-start(bf16[544,128]{1,0:T(8,128)(2,1)} %get-tuple-element.102), channel_id=1, source_target_pairs={{0,24},{4,28},{8,16},{12,20},{16,8},{20,12},{24,0},{28,4},{1,25},{... | collective-permute-start | bytes 417800 | tf_op jit(solution)/shard_map/ppermute | solution.py:918
  139.2 9.9 %collective-permute-start.6 = (bf16[544,128]{1,0:T(8,128)(2,1)S(1)}, bf16[544,128]{1,0:T(8,128)(2,1)S(1)}, u32[]{:S(2)}, u32[]{:S(2)}) collective-permute-start(bf16[544,128]{1,0:T(8,128)(2,1)S(1)} %copy-done.16), channel_id=1, source_target_pairs={{0,28},{4,24},{8,20},{12,16},{16,12},{20,8},{24,4},{28,0},{1,29},{... | collective-permute-start | bytes 417800 | tf_op jit(solution)/shard_map/ppermute | solution.py:918
  145.1 41.6 %all-to-all-start.3 = ((bf16[32,192,128]{2,1,0:T(8,128)(2,1)}), bf16[32,192,128]{2,1,0:T(8,128)(2,1)}, u32[]{:S(2)}, u32[]{:S(2)}) async-start(bf16[32,192,128]{2,1,0:T(8,128)(2,1)} %bitcast.44), calls=%async_computation.3 | async-start | bytes 3145728 | tf_op jit(solution)/shard_map/all_to_all | solution.py:914
  186.6 2.1 collective-permute-start.7
  187.2 2.3 %collective-permute-start.8 = (bf16[16,16384]{1,0:T(8,128)(2,1)S(1)}, bf16[16,16384]{1,0:T(8,128)(2,1)S(1)}, u32[]{:S(2)}, u32[]{:S(2)}) collective-permute-start(bf16[16,16384]{1,0:T(8,128)(2,1)S(1)} %get-tuple-element.112), channel_id=1, source_target_pairs={{0,1},{1,0},{2,3},{3,2},{4,5},{5,4},{6,7},{7,6},{8,9},{9,8},{10,11... | collective-permute-start | bytes 1572872 | tf_op jit(solution)/shard_map/ppermute | solution.py:918
  189.6 14.7 %collective-permute-start.9 = (bf16[16,16384]{1,0:T(8,128)(2,1)S(1)}, bf16[16,16384]{1,0:T(8,128)(2,1)S(1)}, u32[]{:S(2)}, u32[]{:S(2)}) collective-permute-start(bf16[16,16384]{1,0:T(8,128)(2,1)S(1)} %add_convert_fusion.3), channel_id=1, source_target_pairs={{0,2},{1,3},{2,0},{3,1},{4,6},{5,7},{6,4},{7,5},{8,10},{9,11},{10,... | collective-permute-start | bytes 1572872 | tf_op jit(solution)/shard_map/ppermute | solution.py:918
  193.6 21.7 %all-to-all-start.4 = ((bf16[8,224,128]{2,1,0:T(8,128)(2,1)}), bf16[8,224,128]{2,1,0:T(8,128)(2,1)S(1)}, u32[]{:S(2)}, u32[]{:S(2)}) async-start(bf16[8,224,128]{2,1,0:T(8,128)(2,1)} %broadcast_in_dim.8), calls=%async_computation.4 | async-start | bytes 917504 | tf_op jit(solution)/shard_map/all_to_all | solution.py:914
  201.2 13.9 %collective-permute-start.11 = (bf16[16,16384]{1,0:T(8,128)(2,1)S(1)}, bf16[16,16384]{1,0:T(8,128)(2,1)S(1)}, u32[]{:S(2)}, u32[]{:S(2)}) collective-permute-start(bf16[16,16384]{1,0:T(8,128)(2,1)S(1)} %add_convert_fusion.2), channel_id=1, source_target_pairs={{0,2},{1,3},{2,0},{3,1},{4,6},{5,7},{6,4},{7,5},{8,10},{9,11},{10,... | collective-permute-start | bytes 1572872 | tf_op jit(solution)/shard_map/ppermute | solution.py:918
  204.5 11.8 %collective-permute-start.10 = (bf16[16,16384]{1,0:T(8,128)(2,1)S(1)}, bf16[16,16384]{1,0:T(8,128)(2,1)S(1)}, u32[]{:S(2)}, u32[]{:S(2)}) collective-permute-start(bf16[16,16384]{1,0:T(8,128)(2,1)S(1)} %add_convert_fusion.1), channel_id=1, source_target_pairs={{0,1},{1,0},{2,3},{3,2},{4,5},{5,4},{6,7},{7,6},{8,9},{9,8},{10,11... | collective-permute-start | bytes 1572872 | tf_op jit(solution)/shard_map/ppermute | solution.py:918
  215.3 2.0 collective-permute-start.12
  (12 other events, 64.5 us)
Sparse Core Ops, SparseCore 0:
  29.1 19.6 all-gather.2
